TPU v7x, 32 devices: a whole 2x2x4 slice. The times are simulated.
32 devices in a mesh: dp: 4 (over z), row: 2 (over x), col: 4 (over y, core).
Axes of the slice: x: 2, y: 2, z: 4, core: 2. Of those that a mesh axis runs over, the one named last changes fastest.
Arguments:
- tokens: bfloat16 [768, 8192], P('col', ('dp', 'row')), may hold values from -6 to 6
- cotangent: bfloat16 [768, 8192], P('col', ('dp', 'row')), may hold values from -6 to 6
- segments: int32 [16, 512], P(('dp', 'col')), may hold values from 0 to 2, as said below
- first_gain: bfloat16 [2, 768], P(None, 'col'), may hold values from 0.099609375 to 1.8984375
- first_shift: bfloat16 [2, 768], P(None, 'col'), may hold values from -3 to 3
- qkv_weight: bfloat16 [2, 768, 3, 768], P(None, 'col', None, 'row'), may hold values from -0.3125 to 0.3125
- qv_bias: bfloat16 [2, 2, 768], P(None, None, 'row'), may hold values from -3 to 3
- out_weight: bfloat16 [2, 768, 768], P(None, 'col', 'row'), may hold values from -0.875 to 0.875
- out_bias: bfloat16 [2, 768], P(None, 'col'), may hold values from -3 to 3
- second_gain: bfloat16 [2, 768], P(None, 'col'), may hold values from 0.099609375 to 1.8984375
- second_shift: bfloat16 [2, 768], P(None, 'col'), may hold values from -3 to 3
- up_weight: bfloat16 [2, 768, 3072], P(None, 'col', 'row'), may hold values from -0.21875 to 0.21875
- up_bias: bfloat16 [2, 3072], P(None, 'row'), may hold values from -3 to 3
- down_weight: bfloat16 [2, 768, 3072], P(None, 'col', 'row'), may hold values from -0.15625 to 0.15625
- down_bias: bfloat16 [2, 768], P(None, 'col'), may hold values from -3 to 3
Outputs:
- activations: bfloat16 [768, 8192], P('col', ('dp', 'row'))
- input_grad: float32 [768, 8192], P('col', ('dp', 'row'))
- first_gain_grad: float32 [2, 768], P(None, 'col')
- first_shift_grad: float32 [2, 768], P(None, 'col')
- qkv_weight_grad: float32 [2, 768, 3, 768], P(None, 'col', None, 'row')
- qv_bias_grad: float32 [2, 2, 768], P(None, None, 'row')
- out_weight_grad: float32 [2, 768, 768], P(None, 'col', 'row')
- out_bias_grad: float32 [2, 768], P(None, 'col')
- second_gain_grad: float32 [2, 768], P(None, 'col')
- second_shift_grad: float32 [2, 768], P(None, 'col')
- up_weight_grad: float32 [2, 768, 3072], P(None, 'col', 'row')
- up_bias_grad: float32 [2, 3072], P(None, 'row')
- down_weight_grad: float32 [2, 768, 3072], P(None, 'col', 'row')
- down_bias_grad: float32 [2, 768], P(None, 'col')
Inputs may be any that keep to these rules, and one draw needn't show every extreme that they name: `segments`: within each row (one sequence) the numbers never fall; equal numbers mark one document; each sequence holds three documents, the first and the last cut at the sequence's ends.
All inputs are finite; a program needn't handle non-finite values.
Results may differ from a plain program's by a relative error of at most 0.02.
Values may be sent and summed in bfloat16 or wider, within the bound.
A program may use at most 192 MiB of HBM per device.

v0:
```python
from functools import partial

import jax
import jax.numpy as jnp
from jax import lax
from jax.sharding import PartitionSpec as P

D = 768
HEAD_DIM = 64
FF = 3072


EPSILON = 1e-05
NEGATIVE = -1e30


def shortened(value):

    def short(part):
        return part.astype(jnp.bfloat16) if part.dtype == jnp.float32 else part

    return jax.tree.map(short, value)


def contract_rows(left_side, right_side):
    return lax.dot_general(
        left_side, right_side, (((0,), (0,)), ((), ())), preferred_element_type=jnp.float32
    )


def contract_cols(left_side, right_side):
    return lax.dot_general(
        left_side, right_side, (((1,), (1,)), ((), ())), preferred_element_type=jnp.float32
    )


def norm_forward(residual, gain_vec, shift_vec):
    totals = lax.psum((jnp.sum(residual, axis=1), jnp.sum(residual * residual, axis=1)), "col")
    average = totals[0] / D
    variance = totals[1] / D - average * average
    inverse = lax.rsqrt(variance + EPSILON)
    unit_rows = (residual - average[:, None]) * inverse[:, None]
    return ((unit_rows * gain_vec + shift_vec).astype(jnp.bfloat16), unit_rows, inverse)


def norm_backward(upstream, unit_rows, inverse, gain_vec):
    scaled = upstream * gain_vec
    totals = lax.psum((jnp.sum(scaled, axis=1), jnp.sum(scaled * unit_rows, axis=1)), "col")
    result = inverse[:, None] * (
        scaled - totals[0][:, None] / D - unit_rows * (totals[1][:, None] / D)
    )
    return (result, jnp.sum(upstream * unit_rows, axis=0), jnp.sum(upstream, axis=0))


def widen_out(normed_low, weight_block, offsets):
    gathered = lax.all_gather(normed_low, "row", axis=0, tiled=True)
    partial_sum = jnp.dot(gathered, weight_block, preferred_element_type=jnp.float32)
    produced = lax.psum_scatter(partial_sum, "col", scatter_dimension=0, tiled=True)
    return (produced + offsets, gathered)


def widen_back(grad_low, kept_items, weight_block):
    all_grads = lax.all_gather(grad_low, "col", axis=0, tiled=True)
    weight_grad = contract_rows(kept_items, all_grads)
    row_grads = contract_cols(all_grads, weight_block)
    return (
        lax.psum_scatter(
            row_grads.astype(jnp.bfloat16), "row", scatter_dimension=0, tiled=True
        ).astype(jnp.float32),
        weight_grad,
    )


def narrow(inputs_low, weight_block, offsets):
    gathered_cols = lax.all_gather(inputs_low, "col", axis=0, tiled=True)
    partial_sum = contract_cols(gathered_cols, weight_block)
    return (
        lax.psum_scatter(partial_sum, "row", scatter_dimension=0, tiled=True) + offsets,
        gathered_cols,
    )


def narrow_back(grad_low, gathered_cols, weight_block):
    all_grads = lax.all_gather(grad_low, "row", axis=0, tiled=True)
    weight_grad = contract_rows(all_grads, gathered_cols)
    col_grads = jnp.dot(all_grads, weight_block, preferred_element_type=jnp.float32)
    owned = lax.psum_scatter(col_grads, "col", scatter_dimension=0, tiled=True)
    return (owned, weight_grad)


def masked_scores(queries, keys_block, document):
    length = document.shape[0]
    position = jnp.arange(length)
    allowed = (position[:, None] >= position[None, :]) & (document[:, None] == document[None, :])
    scores = jnp.einsum(
        "qhd,khd->hqk", queries, keys_block, preferred_element_type=jnp.float32
    ) * HEAD_DIM ** (-0.5)
    return jnp.where(allowed[None], scores, NEGATIVE)


def attend_forward(mixed_low, segments):
    sequences, length = segments.shape
    feature_width = mixed_low.shape[1] // 3
    head_count = feature_width // HEAD_DIM
    blocks = mixed_low.reshape(sequences, length, 3, head_count, HEAD_DIM)

    def one_sequence(pieces):
        heads_block, document = pieces
        scores = masked_scores(heads_block[:, 0], heads_block[:, 1], document)
        highest = jnp.max(scores, axis=-1, keepdims=True)
        exponent = jnp.exp(scores - highest)
        denominator = jnp.sum(exponent, axis=-1, keepdims=True)
        weights_low = (exponent / denominator).astype(jnp.bfloat16)
        attended = jnp.einsum(
            "hqk,khd->qhd", weights_low, heads_block[:, 2], preferred_element_type=jnp.float32
        )
        return (attended.reshape(length, feature_width), (highest + jnp.log(denominator))[..., 0])

    attended, logsum = lax.map(one_sequence, (blocks, segments))
    return (attended.reshape(sequences * length, feature_width), logsum)


def attend_backward(mixed_low, segments, logsum, grad_low):
    sequences, length = segments.shape
    feature_width = mixed_low.shape[1] // 3
    head_count = feature_width // HEAD_DIM
    blocks = mixed_low.reshape(sequences, length, 3, head_count, HEAD_DIM)
    out_grads = grad_low.reshape(sequences, length, head_count, HEAD_DIM)
    factor = HEAD_DIM ** (-0.5)

    def one_sequence(pieces):
        heads_block, document, log_total, out_grad = pieces
        queries = heads_block[:, 0]
        keys_block = heads_block[:, 1]
        values_block = heads_block[:, 2]
        scores = masked_scores(queries, keys_block, document)
        probs = jnp.exp(scores - log_total[:, :, None])
        value_grad = jnp.einsum(
            "hqk,qhd->khd", probs.astype(jnp.bfloat16), out_grad, preferred_element_type=jnp.float32
        )
        prob_grad = jnp.einsum(
            "qhd,khd->hqk", out_grad, values_block, preferred_element_type=jnp.float32
        )
        inner_sum = jnp.sum(probs * prob_grad, axis=-1, keepdims=True)
        score_grad = (probs * (prob_grad - inner_sum)).astype(jnp.bfloat16)
        query_grad = (
            jnp.einsum("hqk,khd->qhd", score_grad, keys_block, preferred_element_type=jnp.float32)
            * factor
        )
        key_grad = (
            jnp.einsum("hqk,qhd->khd", score_grad, queries, preferred_element_type=jnp.float32)
            * factor
        )
        return jnp.stack([query_grad, key_grad, value_grad], axis=1).reshape(
            length, 3 * feature_width
        )

    grads = lax.map(one_sequence, (blocks, segments, logsum, out_grads))
    return grads.reshape(sequences * length, 3 * feature_width)


def spread(partial_vec, start, total):
    return lax.dynamic_update_slice_in_dim(jnp.zeros((total,), jnp.float32), partial_vec, start, 0)


def shards(
    tokens,
    cotangent,
    segments,
    first_gain,
    first_shift,
    qkv_weight,
    qv_bias,
    out_weight,
    out_bias,
    second_gain,
    second_shift,
    up_weight,
    up_bias,
    down_weight,
    down_bias,
):
    layers = qkv_weight.shape[0]
    depth_in = qkv_weight.shape[1]
    head_width = qkv_weight.shape[3]
    hidden_width = up_weight.shape[2]
    residual = tokens.astype(jnp.float32).T
    stored = []
    for layer_at in range(layers):
        gain_one = first_gain[layer_at].astype(jnp.float32)
        shift_one = first_shift[layer_at].astype(jnp.float32)
        gain_two = second_gain[layer_at].astype(jnp.float32)
        shift_two = second_shift[layer_at].astype(jnp.float32)
        normed_one, unit_one, inverse_one = norm_forward(residual, gain_one, shift_one)
        query_bias = qv_bias[layer_at].astype(jnp.float32)
        offsets = jnp.concatenate([query_bias[0], jnp.zeros_like(query_bias[0]), query_bias[1]])
        mixing = qkv_weight[layer_at].reshape(depth_in, 3 * head_width)
        mixed, kept_one = widen_out(normed_one, mixing, offsets)
        mixed_low = mixed.astype(jnp.bfloat16)
        attended, logsum = attend_forward(mixed_low, segments)
        attended_low = attended.astype(jnp.bfloat16)
        branch, gathered_one = narrow(
            attended_low, out_weight[layer_at], out_bias[layer_at].astype(jnp.float32)
        )
        middle = residual + branch
        normed_two, unit_two, inverse_two = norm_forward(middle, gain_two, shift_two)
        upward, kept_two = widen_out(
            normed_two, up_weight[layer_at], up_bias[layer_at].astype(jnp.float32)
        )
        active_low = jax.nn.gelu(upward, approximate=True).astype(jnp.bfloat16)
        branch_two, gathered_two = narrow(
            active_low, down_weight[layer_at], down_bias[layer_at].astype(jnp.float32)
        )
        stored.append(
            (
                unit_one,
                inverse_one,
                mixing,
                kept_one,
                mixed_low,
                logsum,
                gathered_one,
                unit_two,
                inverse_two,
                kept_two,
                upward,
                gathered_two,
                gain_one,
                gain_two,
            )
        )
        residual = middle + branch_two
    activations = residual.astype(jnp.bfloat16).T
    col_start = lax.axis_index("col") * depth_in
    row_start = lax.axis_index("row") * head_width
    hidden_start = lax.axis_index("row") * hidden_width
    gradient = cotangent.astype(jnp.float32).T
    weight_parts = [None] * layers
    vector_parts = [None] * layers
    for layer_at in reversed(range(layers)):
        (
            unit_one,
            inverse_one,
            mixing,
            kept_one,
            mixed_low,
            logsum,
            gathered_one,
            unit_two,
            inverse_two,
            kept_two,
            upward,
            gathered_two,
            gain_one,
            gain_two,
        ) = stored[layer_at]
        down_in = gradient.astype(jnp.bfloat16)
        active_grad, down_grad = narrow_back(down_in, gathered_two, down_weight[layer_at])
        _, gelu_pull = jax.vjp(partial(jax.nn.gelu, approximate=True), upward)
        hidden_grad = gelu_pull(active_grad)[0].astype(jnp.bfloat16)
        normed_two_grad, up_grad = widen_back(hidden_grad, kept_two, up_weight[layer_at])
        back_two, gain_two_grad, shift_two_grad = norm_backward(
            normed_two_grad, unit_two, inverse_two, gain_two
        )
        middle_grad = gradient + back_two
        out_in = middle_grad.astype(jnp.bfloat16)
        attended_grad, out_grad = narrow_back(out_in, gathered_one, out_weight[layer_at])
        mixed_grad = attend_backward(
            mixed_low, segments, logsum, attended_grad.astype(jnp.bfloat16)
        ).astype(jnp.bfloat16)
        normed_one_grad, qkv_grad = widen_back(mixed_grad, kept_one, mixing)
        back_one, gain_one_grad, shift_one_grad = norm_backward(
            normed_one_grad, unit_one, inverse_one, gain_one
        )
        gradient = middle_grad + back_one
        local_grads = (qkv_grad.reshape(depth_in, 3, head_width), out_grad, up_grad, down_grad)
        weight_parts[layer_at] = local_grads
        mixed_sums = jnp.sum(mixed_grad.astype(jnp.float32), axis=0)
        query_part = spread(mixed_sums[:head_width], row_start, D)
        value_part = spread(mixed_sums[2 * head_width :], row_start, D)
        vector_parts[layer_at] = (
            spread(gain_one_grad, col_start, D),
            spread(shift_one_grad, col_start, D),
            spread(jnp.sum(out_in.astype(jnp.float32), axis=0), col_start, D),
            spread(gain_two_grad, col_start, D),
            spread(shift_two_grad, col_start, D),
            spread(jnp.sum(down_in.astype(jnp.float32), axis=0), col_start, D),
            jnp.stack([query_part, value_part]),
            spread(jnp.sum(hidden_grad.astype(jnp.float32), axis=0), hidden_start, FF),
        )
    stacked = tuple(
        (jnp.stack([weight_parts[level][member] for level in range(layers)]) for member in range(4))
    )
    stacked = jax.tree.map(
        lambda part: part.astype(jnp.float32), lax.psum(shortened(stacked), "dp")
    )
    vectors = tuple(
        (jnp.stack([vector_parts[level][member] for level in range(layers)]) for member in range(8))
    )
    vectors = lax.psum(vectors, ("dp", "row", "col"))
    first_gain_grad = lax.dynamic_slice_in_dim(vectors[0], col_start, depth_in, 1)
    first_shift_grad = lax.dynamic_slice_in_dim(vectors[1], col_start, depth_in, 1)
    out_bias_grad = lax.dynamic_slice_in_dim(vectors[2], col_start, depth_in, 1)
    second_gain_grad = lax.dynamic_slice_in_dim(vectors[3], col_start, depth_in, 1)
    second_shift_grad = lax.dynamic_slice_in_dim(vectors[4], col_start, depth_in, 1)
    down_bias_grad = lax.dynamic_slice_in_dim(vectors[5], col_start, depth_in, 1)
    qv_bias_grad = lax.dynamic_slice_in_dim(vectors[6], row_start, head_width, 2)
    up_bias_grad = lax.dynamic_slice_in_dim(vectors[7], hidden_start, hidden_width, 1)
    return (
        activations,
        gradient.T,
        first_gain_grad,
        first_shift_grad,
        stacked[0],
        qv_bias_grad,
        stacked[1],
        out_bias_grad,
        second_gain_grad,
        second_shift_grad,
        stacked[2],
        up_bias_grad,
        stacked[3],
        down_bias_grad,
    )


def solution(mesh):
    placed = (
        P("col", ("dp", "row")),
        P("col", ("dp", "row")),
        P(("dp", "col"), None),
        P(None, "col"),
        P(None, "col"),
        P(None, "col", None, "row"),
        P(None, None, "row"),
        P(None, "col", "row"),
        P(None, "col"),
        P(None, "col"),
        P(None, "col"),
        P(None, "col", "row"),
        P(None, "row"),
        P(None, "col", "row"),
        P(None, "col"),
    )
    return jax.shard_map(
        shards,
        mesh=mesh,
        in_specs=placed,
        out_specs=(
            P("col", ("dp", "row")),
            P("col", ("dp", "row")),
            P(None, "col"),
            P(None, "col"),
            P(None, "col", None, "row"),
            P(None, None, "row"),
            P(None, "col", "row"),
            P(None, "col"),
            P(None, "col"),
            P(None, "col"),
            P(None, "col", "row"),
            P(None, "row"),
            P(None, "col", "row"),
            P(None, "col"),
        ),
        check_vma=False,
    )
```

profile of v0, /device:TPU:0, one launch (start us, length us, event | category | flops | bytes accessed | tf_op | source)
XLA Modules:
  0.0 1685.6 jit_solution(3308384039028343239)
XLA Ops:
  11.0 8.5 all-reduce.8
  21.3 10.1 all_gather.48
  32.8 5.2 fusion.141
  39.0 79.1 %reduce-scatter.17.cloned.1.call-done = f32[512,1152]{1,0:T(8,128)} async-done(((f32[2048,1152]{1,0:T(8,128)}), f32[512,1152]{1,0:T(8,128)}) %reduce-scatter.17.cloned.1.call-update) | async-done | bytes 2359312 | tf_op jit(solution)/shard_map/reduce_scatter | solution.py:58
  126.6 19.8 %all-gather.9.cloned.1.call-done = bf16[2048,384]{0,1:T(8,128)(2,1)} async-done(((bf16[512,384]{0,1:T(8,128)(2,1)}), bf16[2048,384]{0,1:T(8,128)(2,1)}) %all-gather.9.cloned.1.call-update) | async-done | bytes 1572880 | tf_op jit(solution)/shard_map/all_gather | solution.py:75
  151.3 24.4 %reduce-scatter.19.cloned.1.call-done = f32[1024,192]{0,1:T(8,128)} async-done(((f32[2048,192]{0,1:T(8,128)}), f32[1024,192]{0,1:T(8,128)}) %reduce-scatter.19.cloned.1.call-update) | async-done | bytes 786448 | tf_op jit(solution)/shard_map/reduce_scatter | solution.py:78
  177.1 7.1 all-reduce.7
  184.4 10.3 all_gather.50
  195.6 6.4 fusion.98
  202.7 98.6 %reduce-scatter.21.cloned.1.call-done = f32[512,1536]{1,0:T(8,128)} async-done(((f32[2048,1536]{1,0:T(8,128)}), f32[512,1536]{1,0:T(8,128)}) %reduce-scatter.21.cloned.1.call-update) | async-done | bytes 3145744 | tf_op jit(solution)/shard_map/reduce_scatter | solution.py:58
  301.3 4.2 multiply_convert_fusion.3
  305.8 46.3 %all-gather.11.cloned.1.call-done = bf16[2048,1536]{1,0:T(8,128)(2,1)} async-done(((bf16[512,1536]{1,0:T(8,128)(2,1)}), bf16[2048,1536]{1,0:T(8,128)(2,1)}) %all-gather.11.cloned.1.call-update) | async-done | bytes 6291472 | tf_op jit(solution)/shard_map/all_gather | solution.py:75
  352.0 6.1 fusion.95
  359.4 24.9 %reduce-scatter.23.cloned.1.call-done = f32[1024,192]{0,1:T(8,128)} async-done(((f32[2048,192]{0,1:T(8,128)}), f32[1024,192]{0,1:T(8,128)}) %reduce-scatter.23.cloned.1.call-update) | async-done | bytes 786448 | tf_op jit(solution)/shard_map/reduce_scatter | solution.py:78
  385.7 7.0 all-reduce.6
  393.0 10.3 all_gather.52
  404.2 5.2 fusion.142
  409.5 78.6 %reduce-scatter.25.cloned.1.call-done = f32[512,1152]{1,0:T(8,128)} async-done(((f32[2048,1152]{1,0:T(8,128)}), f32[512,1152]{1,0:T(8,128)}) %reduce-scatter.25.cloned.1.call-update) | async-done | bytes 2359312 | tf_op jit(solution)/shard_map/reduce_scatter | solution.py:58
  500.1 19.8 %all-gather.13.cloned.1.call-done = bf16[2048,384]{0,1:T(8,128)(2,1)} async-done(((bf16[512,384]{0,1:T(8,128)(2,1)}), bf16[2048,384]{0,1:T(8,128)(2,1)}) %all-gather.13.cloned.1.call-update) | async-done | bytes 1572880 | tf_op jit(solution)/shard_map/all_gather | solution.py:75
  523.0 16.8 all_gather.56
  540.7 6.4 fusion.86
  547.2 6.0 reduce-scatter.27.cloned.1.call-done
  554.6 5.9 all-reduce.5
  560.7 11.9 all_gather.54
  572.6 7.8 fusion.91
  580.5 74.4 %reduce-scatter.33.cloned.1.call-done = f32[512,1536]{1,0:T(8,128)} async-done(((f32[2048,1536]{1,0:T(8,128)}), f32[512,1536]{1,0:T(8,128)}) %reduce-scatter.33.cloned.1.call-update) | async-done | bytes 3145744 | tf_op jit(solution)/shard_map/reduce_scatter | solution.py:87
  655.0 101.9 %reduce-scatter.29.cloned.1.call-done = f32[512,1536]{1,0:T(8,128)} async-done(((f32[2048,1536]{1,0:T(8,128)}), f32[512,1536]{1,0:T(8,128)}) %reduce-scatter.29.cloned.1.call-update) | async-done | bytes 3145744 | tf_op jit(solution)/shard_map/reduce_scatter | solution.py:58
  756.8 6.1 convert_reduce_fusion
  763.0 46.5 %all-gather.17.cloned.1.call-done = bf16[2048,1536]{1,0:T(8,128)(2,1)} async-done(((bf16[512,1536]{1,0:T(8,128)(2,1)}), bf16[2048,1536]{1,0:T(8,128)(2,1)}) %all-gather.17.cloned.1.call-update) | async-done | bytes 6291472 | tf_op jit(solution)/shard_map/all_gather | solution.py:63
  809.5 5.9 convolution_convert_fusion.9
  815.5 17.5 %reduce-scatter.35.cloned.1.call-done = bf16[1024,192]{0,1:T(8,128)(2,1)} async-done(((bf16[2048,192]{0,1:T(8,128)(2,1)}), bf16[1024,192]{0,1:T(8,128)(2,1)}) %reduce-scatter.35.cloned.1.call-update) | async-done | bytes 393232 | tf_op jit(solution)/shard_map/reduce_scatter | solution.py:67
  835.0 7.0 all-reduce.4
  844.2 10.3 all_gather.58
  858.7 37.4 %reduce-scatter.37.cloned.1.call-done = f32[512,384]{1,0:T(8,128)} async-done(((f32[2048,384]{1,0:T(8,128)}), f32[512,384]{1,0:T(8,128)}) %reduce-scatter.37.cloned.1.call-update) | async-done | bytes 786448 | tf_op jit(solution)/shard_map/reduce_scatter | solution.py:87
  899.9 4.6 multiply_reduce_fusion.1
  914.1 36.8 %all-gather.19.cloned.1.call-done = bf16[2048,1152]{0,1:T(8,128)(2,1)} async-done(((bf16[512,1152]{0,1:T(8,128)(2,1)}), bf16[2048,1152]{0,1:T(8,128)(2,1)}) %all-gather.19.cloned.1.call-update) | async-done | bytes 4718608 | tf_op jit(solution)/shard_map/all_gather | solution.py:63
  950.9 4.6 convolution_convert_fusion.1
  955.6 43.8 %all-gather.15.cloned.1.call-done = bf16[2048,1536]{1,0:T(8,128)(2,1)} async-done(((bf16[512,1536]{1,0:T(8,128)(2,1)}), bf16[2048,1536]{1,0:T(8,128)(2,1)}) %all-gather.15.cloned.1.call-update) | async-done | bytes 6291472 | tf_op jit(solution)/shard_map/all_gather | solution.py:75
  999.4 6.3 fusion.88
  1005.8 13.9 reduce-scatter.39.cloned.1.call-done
  1021.6 7.7 all-reduce.3
  1031.9 16.5 reduce-scatter.31.cloned.1.call-done
  1048.4 3.9 convert_reduce_fusion.10
  1052.3 11.5 all_gather.60
  1064.8 6.4 fusion.93
  1071.2 99.2 %reduce-scatter.41.cloned.1.call-done = f32[512,1536]{1,0:T(8,128)} async-done(((f32[2048,1536]{1,0:T(8,128)}), f32[512,1536]{1,0:T(8,128)}) %reduce-scatter.41.cloned.1.call-update) | async-done | bytes 3145744 | tf_op jit(solution)/shard_map/reduce_scatter | solution.py:87
  1170.4 5.7 convert_reduce_fusion.1
  1176.2 46.4 %all-gather.21.cloned.1.call-done = bf16[2048,1536]{1,0:T(8,128)(2,1)} async-done(((bf16[512,1536]{1,0:T(8,128)(2,1)}), bf16[2048,1536]{1,0:T(8,128)(2,1)}) %all-gather.21.cloned.1.call-update) | async-done | bytes 6291472 | tf_op jit(solution)/shard_map/all_gather | solution.py:63
  1222.6 5.9 convolution_convert_fusion.8
  1228.6 17.5 %reduce-scatter.43.cloned.1.call-done = bf16[1024,192]{0,1:T(8,128)(2,1)} async-done(((bf16[2048,192]{0,1:T(8,128)(2,1)}), bf16[1024,192]{0,1:T(8,128)(2,1)}) %reduce-scatter.43.cloned.1.call-update) | async-done | bytes 393232 | tf_op jit(solution)/shard_map/reduce_scatter | solution.py:67
  1248.1 7.0 all-reduce.2
  1257.2 10.2 all_gather.62
  1271.6 37.4 %reduce-scatter.45.cloned.1.call-done = f32[512,384]{1,0:T(8,128)} async-done(((f32[2048,384]{1,0:T(8,128)}), f32[512,384]{1,0:T(8,128)}) %reduce-scatter.45.cloned.1.call-update) | async-done | bytes 786448 | tf_op jit(solution)/shard_map/reduce_scatter | solution.py:87
  1312.8 4.6 multiply_reduce_fusion
  1327.2 5.3 fusion.29
  1332.5 5.7 fusion.27
  1349.0 4.3 convolution_convert_fusion.2
  1356.4 4.5 fusion.28
  1362.8 4.2 fusion.26
  1369.1 4.6 convolution_convert_fusion
  1382.7 4.9 convolution_convert_fusion.3
  1397.5 7.0 all-reduce.1
  1406.0 114.4 %all-reduce.13.cloned.1.call-done = (f32[2,768]{1,0:T(2,128)}, f32[2,768]{1,0:T(2,128)}, f32[2,2,768]{2,1,0:T(2,128)}, f32[2,768]{1,0:T(2,128)}, f32[2,768]{1,0:...) async-done(((f32[2,768]{1,0:T(2,128)}, f32[2,768]{1,0:T(2,128)}, f32[2,2,768]{2,1,0:T(2,128)}, f32[2,768]{1,0:T(2,128)}, f32[2,768]{1,0:T(2,128)}, ...) | async-done | bytes 73744 | tf_op jit(solution)/shard_map/psum | solution.py:300
  1530.9 140.7 %all-reduce.15.cloned.1.call-done = (bf16[2,192,3,384]{3,2,1,0:T(4,128)(2,1)}, bf16[2,192,384]{2,1,0:T(8,128)(2,1)}, bf16[2,192,1536]{2,1,0:T(8,128)(2,1)}, bf16[2,192,1536]{2,1,0:T(8,128)(2,1)}) async-done(((bf16[2,192,3,384]{3,2,1,0:T(4,128)(2,1)}, bf16[2,192,384]{2,1,0:T(8,128)(2,1)}, bf16[2,192,1536]{2,1,0:T(8,128)(2,1)}, bf16[2,192,1536]{2,1,0:T(8,128)(2,1)}), (bf16[2,192,3,384]{3,2,1,0:T(4,128)(2,1)}, ...) | async-done | bytes 3538960 | tf_op jit(solution)/shard_map/psum | solution.py:295
  (403 shorter events, 150.6 us)
Async XLA Ops:
  7.2 24.3 %copy-start.30 = (bf16[2,192,3,384]{3,1,2,0:T(8,128)(2,1)S(1)}, bf16[2,192,3,384]{3,1,2,0:T(8,128)(2,1)}, u32[]{:S(2)}) copy-start(bf16[2,192,3,384]{3,1,2,0:T(8,128)(2,1)} %param.20) | copy-start | bytes 2654212
  7.2 110.9 %reduce-scatter.17.cloned.1.call-start = ((), (), s32[]{:S(2)}) async-start(), calls=%async_computation.16 | async-start | bytes 11796480 | tf_op jit(solution)/shard_map/reduce_scatter | solution.py:58
  10.2 382.6 %copy-start.75 = (f32[1,192]{1,0:T(1,128)}, f32[1,192]{1,0:T(1,128)S(1)}, u32[]{:S(2)}) copy-start(f32[1,192]{1,0:T(1,128)S(1)} %get-tuple-element.197) | copy-start | bytes 2308
  38.0 108.3 %all-gather.9.cloned.1.call-start = ((), (), s32[]{:S(2)}) async-start(), calls=%async_computation.17 | async-start | bytes 1966080 | tf_op jit(solution)/shard_map/all_gather | solution.py:75
  39.0 82.8 %copy-start.34 = (pred[512,512]{0,1:T(8,128)(4,1)}, pred[512,512]{0,1:T(8,128)(4,1)S(1)}, u32[]{:S(2)}) copy-start(pred[512,512]{0,1:T(8,128)(4,1)S(1)} %fusion.56) | copy-start | bytes 786436
  124.5 21.8 %copy-start.23 = (bf16[2,192,384]{2,1,0:T(8,128)(2,1)S(1)}, bf16[2,192,384]{2,1,0:T(8,128)(2,1)}, u32[]{:S(2)}) copy-start(bf16[2,192,384]{2,1,0:T(8,128)(2,1)} %param.22) | copy-start | bytes 884740
  126.5 23.1 %copy-start.87 = (bf16[2,192]{1,0:T(2,128)(2,1)S(1)}, bf16[2,192]{1,0:T(2,128)(2,1)}, u32[]{:S(2)}) copy-start(bf16[2,192]{1,0:T(2,128)(2,1)} %param.23) | copy-start | bytes 2308
  126.5 23.6 %copy-start.88 = (bf16[2,192]{1,0:T(2,128)(2,1)S(1)}, bf16[2,192]{1,0:T(2,128)(2,1)}, u32[]{:S(2)}) copy-start(bf16[2,192]{1,0:T(2,128)(2,1)} %param.24) | copy-start | bytes 2308
  126.5 24.2 %copy-start.89 = (bf16[2,192]{1,0:T(2,128)(2,1)S(1)}, bf16[2,192]{1,0:T(2,128)(2,1)}, u32[]{:S(2)}) copy-start(bf16[2,192]{1,0:T(2,128)(2,1)} %param.25) | copy-start | bytes 2308
  126.5 49.2 %copy-start.2 = (bf16[192,1024]{1,0:T(8,128)(2,1)S(1)}, bf16[192,1024]{1,0:T(8,128)(2,1)}, u32[]{:S(2)}) copy-start(bf16[192,1024]{1,0:T(8,128)(2,1)} %param.15) | copy-start | bytes 1179652
  126.5 49.2 %reduce-scatter.19.cloned.1.call-start = ((), (), s32[]{:S(2)}) async-start(), calls=%async_computation.18 | async-start | bytes 2359296 | tf_op jit(solution)/shard_map/reduce_scatter | solution.py:78
  149.5 46.1 %copy-start.29 = (bf16[2,192,1536]{2,1,0:T(8,128)(2,1)S(1)}, bf16[2,192,1536]{2,1,0:T(8,128)(2,1)}, u32[]{:S(2)}) copy-start(bf16[2,192,1536]{2,1,0:T(8,128)(2,1)} %param.26) | copy-start | bytes 3538948
  149.5 151.8 %reduce-scatter.21.cloned.1.call-start = ((), (), s32[]{:S(2)}) async-start(), calls=%async_computation.19 | async-start | bytes 15728640 | tf_op jit(solution)/shard_map/reduce_scatter | solution.py:58
  150.7 51.2 %copy-start.67 = (f32[1,192]{1,0:T(1,128)}, f32[1,192]{1,0:T(1,128)S(1)}, u32[]{:S(2)}) copy-start(f32[1,192]{1,0:T(1,128)S(1)} %get-tuple-element.192) | copy-start | bytes 2308
  184.2 17.8 %copy-start.35 = (f32[1024]{0:T(1024)}, f32[1024]{0:T(1024)S(1)}, u32[]{:S(2)}) copy-start(f32[1024]{0:T(1024)S(1)} %get-tuple-element.181) | copy-start | bytes 12292
  184.2 17.8 %copy-start.38 = (f32[1024]{0:T(1024)}, f32[1024]{0:T(1024)S(1)}, u32[]{:S(2)}) copy-start(f32[1024]{0:T(1024)S(1)} %get-tuple-element.182) | copy-start | bytes 12292
  202.0 150.1 %all-gather.11.cloned.1.call-start = ((), (), s32[]{:S(2)}) async-start(), calls=%async_computation.20 | async-start | bytes 7864320 | tf_op jit(solution)/shard_map/all_gather | solution.py:75
  202.7 102.8 %copy-start.45 = (f32[1536]{0:T(1024)}, f32[1536]{0:T(1024)S(1)}, u32[]{:S(2)}) copy-start(f32[1536]{0:T(1024)S(1)} %get-tuple-element.117) | copy-start | bytes 18436
  301.3 50.8 %copy-start.26 = (bf16[2,192,1536]{2,1,0:T(8,128)(2,1)S(1)}, bf16[2,192,1536]{2,1,0:T(8,128)(2,1)}, u32[]{:S(2)}) copy-start(bf16[2,192,1536]{2,1,0:T(8,128)(2,1)} %param.28) | copy-start | bytes 3538948
  305.5 78.9 %reduce-scatter.23.cloned.1.call-start = ((), (), s32[]{:S(2)}) async-start(), calls=%async_computation.21 | async-start | bytes 2359296 | tf_op jit(solution)/shard_map/reduce_scatter | solution.py:78
  358.2 129.9 %reduce-scatter.25.cloned.1.call-start = ((), (), s32[]{:S(2)}) async-start(), calls=%async_computation.22 | async-start | bytes 11796480 | tf_op jit(solution)/shard_map/reduce_scatter | solution.py:58
  358.8 50.6 %copy-start.21 = (bf16[24,8,3,384]{3,1,2,0:T(8,128)(2,1)}, bf16[24,8,3,384]{3,1,2,0:T(8,128)(2,1)S(1)}, u32[]{:S(2)}) copy-start(bf16[24,8,3,384]{3,1,2,0:T(8,128)(2,1)S(1)} %copy.73) | copy-start | bytes 1327108
  392.8 16.6 copy-start.55
  392.8 16.6 copy-start.57
  409.5 110.4 %all-gather.13.cloned.1.call-start = ((), (), s32[]{:S(2)}) async-start(), calls=%async_computation.23 | async-start | bytes 1966080 | tf_op jit(solution)/shard_map/all_gather | solution.py:75
  500.0 23.1 %copy-start.16 = (bf16[192,1024]{1,0:T(8,128)(2,1)S(1)}, bf16[192,1024]{1,0:T(8,128)(2,1)}, u32[]{:S(2)}) copy-start(bf16[192,1024]{1,0:T(8,128)(2,1)} %param.16) | copy-start | bytes 1179652
  500.0 53.2 %reduce-scatter.27.cloned.1.call-start = ((), (), s32[]{:S(2)}) async-start(), calls=%async_computation.24 | async-start | bytes 2359296 | tf_op jit(solution)/shard_map/reduce_scatter | solution.py:78
  523.0 17.8 %copy-start.27 = (bf16[2,192,1536]{2,1,0:T(8,128)(2,1)S(1)}, bf16[2,192,1536]{2,1,0:T(8,128)(2,1)}, u32[]{:S(2)}) copy-start(bf16[2,192,1536]{2,1,0:T(8,128)(2,1)} %param.28) | copy-start | bytes 3538948
  523.0 132.0 %reduce-scatter.33.cloned.1.call-start = ((), (), s32[]{:S(2)}) async-start(), calls=%async_computation.28 | async-start | bytes 15728640 | tf_op jit(solution)/shard_map/reduce_scatter | solution.py:87
  547.1 13.4 copy-start.70
  547.1 13.4 copy-start.85
  547.1 209.7 %reduce-scatter.29.cloned.1.call-start = ((), (), s32[]{:S(2)}) async-start(), calls=%async_computation.25 | async-start | bytes 15728640 | tf_op jit(solution)/shard_map/reduce_scatter | solution.py:58
  560.5 281.6 %copy-start.41 = (f32[1024]{0:T(1024)}, f32[1024]{0:T(1024)S(1)}, u32[]{:S(2)}) copy-start(f32[1024]{0:T(1024)S(1)} %get-tuple-element.177) | copy-start | bytes 12292
  560.5 281.6 %copy-start.43 = (f32[1024]{0:T(1024)}, f32[1024]{0:T(1024)S(1)}, u32[]{:S(2)}) copy-start(f32[1024]{0:T(1024)S(1)} %get-tuple-element.178) | copy-start | bytes 12292
  580.5 229.0 %all-gather.17.cloned.1.call-start = ((), (), s32[]{:S(2)}) async-start(), calls=%async_computation.29 | async-start | bytes 7864320 | tf_op jit(solution)/shard_map/all_gather | solution.py:63
  763.0 70.1 %copy-start.71 = (f32[1,192]{1,0:T(1,128)S(1)}, f32[1,192]{1,0:T(1,128)}, u32[]{:S(2)}) copy-start(f32[1,192]{1,0:T(1,128)} %get-tuple-element.191) | copy-start | bytes 2308
  763.0 79.1 %copy-start.17 = (bf16[192,1024]{1,0:T(8,128)(2,1)S(1)}, bf16[192,1024]{1,0:T(8,128)(2,1)}, u32[]{:S(2)}) copy-start(bf16[192,1024]{1,0:T(8,128)(2,1)} %param.16) | copy-start | bytes 1179652
  763.0 70.1 %reduce-scatter.35.cloned.1.call-start = ((), (), s32[]{:S(2)}) async-start(), calls=%async_computation.30 | async-start | bytes 1179648 | tf_op jit(solution)/shard_map/reduce_scatter | solution.py:67
  815.5 80.6 %reduce-scatter.37.cloned.1.call-start = ((), (), s32[]{:S(2)}) async-start(), calls=%async_computation.31 | async-start | bytes 3932160 | tf_op jit(solution)/shard_map/reduce_scatter | solution.py:87
  857.9 93.0 %all-gather.19.cloned.1.call-start = ((), (), s32[]{:S(2)}) async-start(), calls=%async_computation.32 | async-start | bytes 5898240 | tf_op jit(solution)/shard_map/all_gather | solution.py:63
  913.3 86.1 %all-gather.15.cloned.1.call-start = ((), (), s32[]{:S(2)}) async-start(), calls=%async_computation.26 | async-start | bytes 7864320 | tf_op jit(solution)/shard_map/all_gather | solution.py:75
  913.9 105.7 %reduce-scatter.39.cloned.1.call-start = ((), (), s32[]{:S(2)}) async-start(), calls=%async_computation.33 | async-start | bytes 1179648 | tf_op jit(solution)/shard_map/reduce_scatter | solution.py:67
  955.5 64.1 %copy-start.56 = (f32[1024]{0:T(1024)S(1)}, f32[1024]{0:T(1024)}, u32[]{:S(2)}) copy-start(f32[1024]{0:T(1024)} %copy-done.55) | copy-start | bytes 12292
  955.5 64.1 %copy-start.58 = (f32[1024]{0:T(1024)S(1)}, f32[1024]{0:T(1024)}, u32[]{:S(2)}) copy-start(f32[1024]{0:T(1024)} %copy-done.57) | copy-start | bytes 12292
  955.5 92.9 %copy-start.42 = (f32[1024]{0:T(1024)S(1)}, f32[1024]{0:T(1024)}, u32[]{:S(2)}) copy-start(f32[1024]{0:T(1024)} %copy-done.41) | copy-start | bytes 12292
  955.5 92.9 %copy-start.44 = (f32[1024]{0:T(1024)S(1)}, f32[1024]{0:T(1024)}, u32[]{:S(2)}) copy-start(f32[1024]{0:T(1024)} %copy-done.43) | copy-start | bytes 12292
  955.6 92.9 %reduce-scatter.31.cloned.1.call-start = ((), (), s32[]{:S(2)}) async-start(), calls=%async_computation.27 | async-start | bytes 2359296 | tf_op jit(solution)/shard_map/reduce_scatter | solution.py:78
  1005.7 164.6 %reduce-scatter.41.cloned.1.call-start = ((), (), s32[]{:S(2)}) async-start(), calls=%async_computation.34 | async-start | bytes 15728640 | tf_op jit(solution)/shard_map/reduce_scatter | solution.py:87
  1048.4 16.3 copy-start.28
  1071.1 99.3 %copy-start.46 = (f32[1536]{0:T(1024)S(1)}, f32[1536]{0:T(1024)}, u32[]{:S(2)}) copy-start(f32[1536]{0:T(1024)} %copy-done.45) | copy-start | bytes 18436
  1071.1 151.5 %all-gather.21.cloned.1.call-start = ((), (), s32[]{:S(2)}) async-start(), calls=%async_computation.35 | async-start | bytes 7864320 | tf_op jit(solution)/shard_map/all_gather | solution.py:63
  1176.1 70.1 %copy-start.36 = (f32[1024]{0:T(1024)S(1)}, f32[1024]{0:T(1024)}, u32[]{:S(2)}) copy-start(f32[1024]{0:T(1024)} %copy-done.35) | copy-start | bytes 12292
  1176.1 70.1 %copy-start.39 = (f32[1024]{0:T(1024)S(1)}, f32[1024]{0:T(1024)}, u32[]{:S(2)}) copy-start(f32[1024]{0:T(1024)} %copy-done.38) | copy-start | bytes 12292
  1176.1 70.1 %copy-start.68 = (f32[1,192]{1,0:T(1,128)S(1)}, f32[1,192]{1,0:T(1,128)}, u32[]{:S(2)}) copy-start(f32[1,192]{1,0:T(1,128)} %copy-done.67) | copy-start | bytes 2308
  1176.1 79.1 %copy-start.3 = (f32[1024,192]{0,1:T(8,128)S(1)}, f32[1024,192]{0,1:T(8,128)}, u32[]{:S(2)}) copy-start(f32[1024,192]{0,1:T(8,128)} %get-tuple-element.152) | copy-start | bytes 2359300
  1176.1 70.0 %reduce-scatter.43.cloned.1.call-start = ((), (), s32[]{:S(2)}) async-start(), calls=%async_computation.36 | async-start | bytes 1179648 | tf_op jit(solution)/shard_map/reduce_scatter | solution.py:67
  1228.6 80.4 %reduce-scatter.45.cloned.1.call-start = ((), (), s32[]{:S(2)}) async-start(), calls=%async_computation.37 | async-start | bytes 3932160 | tf_op jit(solution)/shard_map/reduce_scatter | solution.py:87
  1255.1 12.3 copy-start.59
  1255.2 12.3 copy-start.61
  1270.8 98.3 %all-gather.23.cloned.1.call-start = ((), (), s32[]{:S(2)}) async-start(), calls=%async_computation.38 | async-start | bytes 5898240 | tf_op jit(solution)/shard_map/all_gather | solution.py:63
  1326.2 65.2 %reduce-scatter.47.cloned.1.call-start = ((), (), s32[]{:S(2)}) async-start(), calls=%async_computation.39 | async-start | bytes 1179648 | tf_op jit(solution)/shard_map/reduce_scatter | solution.py:67
  1373.7 146.7 %all-reduce.13.cloned.1.call-start = ((), (), s32[]{:S(2)}) async-start(), calls=%async_computation.40 | async-start | bytes 147456 | tf_op jit(solution)/shard_map/psum | solution.py:300
  1382.6 11.8 copy-start.19
  1394.4 277.2 %all-reduce.15.cloned.1.call-start = ((), (), s32[]{:S(2)}) async-start(), calls=%async_computation.41 | async-start | bytes 7667712 | tf_op jit(solution)/shard_map/psum | solution.py:295
  (62 other events, 296.9 us)
Sparse Core Ops, SparseCore 0:
  38.2 79.8 reduce-scatter.16
  126.7 19.6 all-gather.8
  149.6 26.0 reduce-scatter.18
  202.1 99.1 reduce-scatter.20
  305.6 46.3 all-gather.10
  358.3 26.0 reduce-scatter.22
  409.6 78.4 reduce-scatter.24
  500.1 19.6 all-gather.12
  523.1 30.0 reduce-scatter.26
  555.8 99.0 reduce-scatter.32
  657.7 99.0 reduce-scatter.28
  763.1 46.3 all-gather.16
  815.6 17.4 reduce-scatter.34
  858.0 38.0 reduce-scatter.36
  913.4 37.4 all-gather.18
  953.0 46.3 all-gather.14
  1002.2 17.4 reduce-scatter.38
  1022.3 26.0 reduce-scatter.30
  1071.3 99.0 reduce-scatter.40
  1176.2 46.3 all-gather.20
  1228.7 17.4 reduce-scatter.42
  1270.9 38.0 reduce-scatter.44
  1326.3 37.4 all-gather.22
  1373.8 17.5 reduce-scatter.46
  1399.0 121.3 all-reduce.12
  1524.2 147.3 all-reduce.14
where the time goes:
time: 1700 us; the launch traced here: 1690 us
  waiting for transfers between devices  1240 us (73%)
  blocking collectives  149 us (9%)
  matrix products  145 us (9%)
  other arithmetic  85.6 us (5%)
  local copies, waits for them, and re-layouts  44.3 us (3%)
    reduce_scatter x4, waiting for transfers between devices, widen_out(): lax.psum_scatter(partial_sum, 'col', scatter_dimension=0, tiled=True)  358 us
    reduce_scatter x4, waiting for transfers between devices, narrow_back(): owned = lax.psum_scatter(col_grads, 'col', scatter_dimension=0, tiled=True)  248 us
    psum x1, waiting for transfers between devices, shards(): lax.psum(shortened(stacked), 'dp')  141 us
    all_gather x4, waiting for transfers between devices, widen_back(): all_grads = lax.all_gather(grad_low, 'col', axis=0, tiled=True)  130 us
    all_gather x4, waiting for transfers between devices, narrow(): gathered_cols = lax.all_gather(inputs_low, 'col', axis=0, tiled=True)  130 us
    psum x1, waiting for transfers between devices, shards(): vectors = lax.psum(vectors, ('dp', 'row', 'col'))  114 us
    reduce_scatter x4, waiting for transfers between devices, narrow(): lax.psum_scatter(partial_sum, 'row', scatter_dimension=0, tiled=True)  72 us
    reduce_scatter x4, waiting for transfers between devices, widen_back(): lax.psum_scatter(row_grads.astype(jnp.bfloat16), 'row', scatter_dimension...  50.7 us
  transfers between devices with their start and end apart: 26, of which 25 were waited for; matrix products, arithmetic and copies ran while one was open for 6% of the time, Pallas kernels for 0%

commit v1 on v0

v1 whole, which is shorter than its diff:
```python
from functools import partial

import jax
import jax.numpy as jnp
from jax import lax
from jax.sharding import Mesh, PartitionSpec as P

HEAD_DIM = 64
EPSILON = 1e-05
NEGATIVE = -1e30
PLANE = ("row", "pair")


def contract_rows(left_side, right_side):
    return lax.dot_general(
        left_side, right_side, (((0,), (0,)), ((), ())), preferred_element_type=jnp.float32
    )


def contract_cols(left_side, right_side):
    return lax.dot_general(
        left_side, right_side, (((1,), (1,)), ((), ())), preferred_element_type=jnp.float32
    )


def plain(left_side, right_side):
    return jnp.dot(left_side, right_side, preferred_element_type=jnp.float32)


def pair_sum(value):
    return value + lax.ppermute(value, "core", [(0, 1), (1, 0)])


def norm_forward(residual, gain_vec, shift_vec):
    average = jnp.mean(residual, axis=1, keepdims=True)
    variance = jnp.mean(residual * residual, axis=1, keepdims=True) - average * average
    inverse = lax.rsqrt(variance + EPSILON)
    unit_rows = (residual - average) * inverse
    return ((unit_rows * gain_vec + shift_vec).astype(jnp.bfloat16), unit_rows, inverse)


def norm_backward(upstream, unit_rows, inverse, gain_vec):
    scaled = upstream * gain_vec
    first = jnp.mean(scaled, axis=1, keepdims=True)
    second = jnp.mean(scaled * unit_rows, axis=1, keepdims=True)
    result = inverse * (scaled - first - unit_rows * second)
    return (result, jnp.sum(upstream * unit_rows, axis=0), jnp.sum(upstream, axis=0))


def masked_scores(queries, keys_block, document):
    length = document.shape[0]
    position = jnp.arange(length)
    allowed = (position[:, None] >= position[None, :]) & (document[:, None] == document[None, :])
    scores = jnp.einsum(
        "hqd,hkd->hqk", queries, keys_block, preferred_element_type=jnp.float32
    ) * HEAD_DIM ** (-0.5)
    return jnp.where(allowed[None], scores, NEGATIVE)


def by_heads(value):
    return value.reshape(value.shape[0], -1, HEAD_DIM).transpose(1, 0, 2)


def from_heads(value):
    return value.transpose(1, 0, 2).reshape(value.shape[1], -1)


def attend_forward(queries, keys_block, values_block, document):
    scores = masked_scores(queries, keys_block, document)
    highest = jnp.max(scores, axis=-1, keepdims=True)
    exponent = jnp.exp(scores - highest)
    denominator = jnp.sum(exponent, axis=-1, keepdims=True)
    weights_low = (exponent / denominator).astype(jnp.bfloat16)
    attended = jnp.einsum(
        "hqk,hkd->hqd", weights_low, values_block, preferred_element_type=jnp.float32
    )
    return (attended, highest + jnp.log(denominator))


def attend_backward(queries, keys_block, values_block, document, logsum, out_grad):
    factor = HEAD_DIM ** (-0.5)
    probs = jnp.exp(masked_scores(queries, keys_block, document) - logsum)
    value_grad = jnp.einsum(
        "hqk,hqd->hkd", probs.astype(jnp.bfloat16), out_grad, preferred_element_type=jnp.float32
    )
    prob_grad = jnp.einsum(
        "hqd,hkd->hqk", out_grad, values_block, preferred_element_type=jnp.float32
    )
    inner_sum = jnp.sum(probs * prob_grad, axis=-1, keepdims=True)
    score_grad = (probs * (prob_grad - inner_sum)).astype(jnp.bfloat16)
    query_grad = (
        jnp.einsum("hqk,hkd->hqd", score_grad, keys_block, preferred_element_type=jnp.float32)
        * factor
    )
    key_grad = (
        jnp.einsum("hqk,hqd->hkd", score_grad, queries, preferred_element_type=jnp.float32)
        * factor
    )
    return query_grad, key_grad, value_grad


def share_weights(parts):
    joined = jnp.concatenate(parts, axis=-1)
    mine = lax.all_to_all(joined, "core", split_axis=2, concat_axis=1, tiled=True)
    return mine[:, :, 0]


def gather_plane(piece):
    everything = lax.all_gather(piece, PLANE, axis=0, tiled=False)
    rows = lax.axis_size("row")
    return everything.reshape(rows, -1, piece.shape[-1])


def scatter_plane(grads):
    pairs = lax.axis_size("pair")
    stacked = jnp.stack(grads).astype(jnp.bfloat16)
    stacked = stacked.reshape(len(grads) * pairs, -1, stacked.shape[-1])
    return lax.psum_scatter(stacked, PLANE, scatter_dimension=0, tiled=False)


def return_weights(piece):
    depth = piece.shape[0] // 2
    return lax.all_to_all(
        piece.reshape(2, depth, 1, piece.shape[-1]), "core", split_axis=0, concat_axis=2, tiled=True
    )[0].astype(jnp.float32)


def shards(
    tokens,
    cotangent,
    segments,
    first_gain,
    first_shift,
    qkv_weight,
    qv_bias,
    out_weight,
    out_bias,
    second_gain,
    second_shift,
    up_weight,
    up_bias,
    down_weight,
    down_bias,
):
    layers, depth_in, _, head_width = qkv_weight.shape
    hidden_width = up_weight.shape[2]
    half_head, half_hidden = head_width // 2, hidden_width // 2
    rows, pairs = lax.axis_size("row"), lax.axis_size("pair")
    at_row, at_pair, at_core = (lax.axis_index(name) for name in ("row", "pair", "core"))
    width = depth_in * pairs * 2
    length = segments.shape[1]

    attention_part = share_weights(
        [
            qkv_weight.reshape(layers, depth_in, 3, 2, half_head)
            .transpose(0, 1, 3, 2, 4)
            .reshape(layers, depth_in, 2, 3 * half_head),
            out_weight.reshape(layers, depth_in, 2, half_head),
        ]
    )
    forward_part = share_weights(
        [
            up_weight.reshape(layers, depth_in, 2, half_hidden),
            down_weight.reshape(layers, depth_in, 2, half_hidden),
        ]
    )
    attention_weights = []
    forward_weights = []
    for layer_at in range(layers):
        attention_weights.append(gather_plane(attention_part[layer_at]))
        forward_weights.append(gather_plane(forward_part[layer_at]))

    small = jnp.concatenate(
        [
            jnp.stack(
                [first_gain, first_shift, out_bias, second_gain, second_shift, down_bias]
            ).reshape(-1),
            qv_bias.reshape(-1),
            up_bias.reshape(-1),
            segments[0].astype(jnp.bfloat16),
        ]
    )
    small = lax.all_gather(small, ("row", "pair", "core"), axis=0, tiled=False).astype(jnp.float32)
    small = small.reshape(rows, pairs * 2, -1)
    cuts = [6 * layers * depth_in, 2 * layers * head_width, layers * hidden_width]
    cuts = [cuts[0], cuts[0] + cuts[1], cuts[0] + cuts[1] + cuts[2]]
    vectors = small[0, :, : cuts[0]].reshape(pairs * 2, 6, layers, depth_in)
    vectors = vectors.transpose(1, 2, 0, 3).reshape(6, layers, width)
    query_bias = small[:, 0, cuts[0] : cuts[1]].reshape(rows, layers, 2, 2, half_head)
    query_bias = lax.dynamic_index_in_dim(query_bias, at_core, 3, keepdims=False)
    hidden_bias = small[:, 0, cuts[1] : cuts[2]].reshape(rows, layers, 2, half_hidden)
    hidden_bias = lax.dynamic_index_in_dim(hidden_bias, at_core, 2, keepdims=False)
    document = lax.dynamic_index_in_dim(
        small[0, :, cuts[2] :], at_row * pairs + at_pair, 0, keepdims=False
    )

    both = jnp.stack([tokens, cotangent])
    both = lax.all_gather(both, "core", axis=1, tiled=True)
    both = lax.all_to_all(both, "pair", split_axis=2, concat_axis=1, tiled=True)
    residual = both[0].astype(jnp.float32).T
    gradient = both[1].astype(jnp.float32).T

    stored = []
    for layer_at in range(layers):
        gain_one, shift_one, bias_out, gain_two, shift_two, bias_down = vectors[:, layer_at]
        mixing = attention_weights[layer_at]
        normed_one, unit_one, inverse_one = norm_forward(residual, gain_one, shift_one)
        mixed = []
        for row in range(rows):
            offsets = jnp.concatenate(
                [
                    query_bias[row, layer_at, 0],
                    jnp.zeros((half_head,), jnp.float32),
                    query_bias[row, layer_at, 1],
                ]
            )
            produced = plain(normed_one, mixing[row][:, : 3 * half_head]) + offsets
            mixed.append(produced.astype(jnp.bfloat16).reshape(length, 3, half_head))
        mixed = jnp.concatenate(mixed, axis=2)
        heads = [by_heads(mixed[:, part]) for part in range(3)]
        attended, logsum = attend_forward(*heads, document)
        attended_low = from_heads(attended.astype(jnp.bfloat16))
        branch = sum(
            contract_cols(
                attended_low[:, row * half_head : (row + 1) * half_head],
                mixing[row][:, 3 * half_head :],
            )
            for row in range(rows)
        )
        middle = residual + (pair_sum(branch) + bias_out)
        normed_two, unit_two, inverse_two = norm_forward(middle, gain_two, shift_two)
        wide = forward_weights[layer_at]
        upward = [
            plain(normed_two, wide[row][:, :half_hidden]) + hidden_bias[row, layer_at]
            for row in range(rows)
        ]
        active = [jax.nn.gelu(part, approximate=True).astype(jnp.bfloat16) for part in upward]
        branch_two = sum(
            contract_cols(active[row], wide[row][:, half_hidden:]) for row in range(rows)
        )
        stored.append(
            (
                normed_one,
                unit_one,
                inverse_one,
                heads,
                logsum,
                attended_low,
                normed_two,
                unit_two,
                inverse_two,
                upward,
                active,
            )
        )
        residual = middle + (pair_sum(branch_two) + bias_down)

    def to_owner(value):
        blocks = value.T.reshape(pairs, 2, depth_in, length)
        blocks = lax.dynamic_index_in_dim(blocks, at_core, 1, keepdims=False)
        return lax.all_to_all(blocks, "pair", split_axis=0, concat_axis=2, tiled=True)[0]

    activations = to_owner(residual.astype(jnp.bfloat16))

    vector_parts = [None] * layers
    attention_grads = [None] * layers
    forward_grads = [None] * layers
    for layer_at in reversed(range(layers)):
        (
            normed_one,
            unit_one,
            inverse_one,
            heads,
            logsum,
            attended_low,
            normed_two,
            unit_two,
            inverse_two,
            upward,
            active,
        ) = stored[layer_at]
        gain_one, _, _, gain_two, _, _ = vectors[:, layer_at]
        mixing, wide = attention_weights[layer_at], forward_weights[layer_at]
        down_in = gradient.astype(jnp.bfloat16)
        hidden_grads = []
        parts = []
        normed_grad = 0.0
        for row in range(rows):
            down_grad = contract_rows(down_in, active[row])
            active_grad = plain(down_in, wide[row][:, half_hidden:])
            _, gelu_pull = jax.vjp(partial(jax.nn.gelu, approximate=True), upward[row])
            hidden_grad = gelu_pull(active_grad)[0].astype(jnp.bfloat16)
            up_grad = contract_rows(normed_two, hidden_grad)
            normed_grad = normed_grad + contract_cols(hidden_grad, wide[row][:, :half_hidden])
            hidden_grads.append(jnp.sum(hidden_grad.astype(jnp.float32), axis=0))
            parts.append(jnp.concatenate([up_grad, down_grad], axis=1))
        forward_grads[layer_at] = lax.psum(scatter_plane(parts), "dp")
        back_two, gain_two_grad, shift_two_grad = norm_backward(
            pair_sum(normed_grad), unit_two, inverse_two, gain_two
        )
        middle_grad = gradient + back_two
        out_in = middle_grad.astype(jnp.bfloat16)
        out_grads = []
        attended_grad = []
        for row in range(rows):
            span = slice(row * half_head, (row + 1) * half_head)
            out_grads.append(contract_rows(out_in, attended_low[:, span]))
            attended_grad.append(plain(out_in, mixing[row][:, 3 * half_head :]))
        attended_grad = jnp.concatenate(attended_grad, axis=1).astype(jnp.bfloat16)
        mixed_grad = [
            from_heads(part.astype(jnp.bfloat16))
            for part in attend_backward(*heads, document, logsum, by_heads(attended_grad))
        ]
        parts = []
        normed_grad = 0.0
        for row in range(rows):
            span = slice(row * half_head, (row + 1) * half_head)
            pieces = jnp.concatenate([part[:, span] for part in mixed_grad], axis=1)
            parts.append(
                jnp.concatenate([contract_rows(normed_one, pieces), out_grads[row]], axis=1)
            )
            normed_grad = normed_grad + contract_cols(pieces, mixing[row][:, : 3 * half_head])
        attention_grads[layer_at] = lax.psum(scatter_plane(parts), "dp")
        back_one, gain_one_grad, shift_one_grad = norm_backward(
            pair_sum(normed_grad), unit_one, inverse_one, gain_one
        )
        query_sums = jnp.stack(
            [jnp.sum(mixed_grad[part].astype(jnp.float32), axis=0) for part in (0, 2)]
        )
        vector_parts[layer_at] = (
            jnp.stack(
                [
                    gain_one_grad,
                    shift_one_grad,
                    jnp.sum(out_in.astype(jnp.float32), axis=0),
                    gain_two_grad,
                    shift_two_grad,
                    jnp.sum(down_in.astype(jnp.float32), axis=0),
                ]
            ),
            query_sums.reshape(2, rows, half_head),
            jnp.stack(hidden_grads),
        )
        gradient = middle_grad + back_one

    input_grad = to_owner(gradient)
    deep, asked, hidden = (
        jnp.stack([vector_parts[layer_at][part] for layer_at in range(layers)]) for part in range(3)
    )
    sums = lax.psum(
        jnp.concatenate([deep.reshape(-1), asked.reshape(-1), hidden.reshape(-1)]),
        ("dp", "row", "pair"),
    )
    hidden_sums = lax.all_gather(sums[deep.size :], "core", axis=0, tiled=False)
    deep_sums = lax.dynamic_slice_in_dim(
        sums[: deep.size].reshape(layers, 6, width), (at_pair * 2 + at_core) * depth_in, depth_in, 2
    )
    asked_sums = hidden_sums[:, : asked.size].reshape(2, layers, 2, rows, half_head)
    asked_sums = lax.dynamic_index_in_dim(asked_sums, at_row, 3, keepdims=False)
    asked_sums = asked_sums.transpose(1, 2, 0, 3).reshape(layers, 2, head_width)
    up_sums = hidden_sums[:, asked.size :].reshape(2, layers, rows, half_hidden)
    up_sums = lax.dynamic_index_in_dim(up_sums, at_row, 2, keepdims=False)
    up_sums = up_sums.transpose(1, 0, 2).reshape(layers, hidden_width)

    attention_out = jnp.stack([return_weights(part) for part in attention_grads])
    forward_out = jnp.stack([return_weights(part) for part in forward_grads])
    qkv_grad = attention_out[..., : 3 * half_head].reshape(layers, depth_in, 2, 3, half_head)
    qkv_grad = qkv_grad.transpose(0, 1, 3, 2, 4).reshape(layers, depth_in, 3, head_width)
    out_grad = attention_out[..., 3 * half_head :].reshape(layers, depth_in, head_width)
    up_grad = forward_out[..., :half_hidden].reshape(layers, depth_in, hidden_width)
    down_grad = forward_out[..., half_hidden:].reshape(layers, depth_in, hidden_width)
    return (
        activations,
        input_grad,
        deep_sums[:, 0],
        deep_sums[:, 1],
        qkv_grad,
        asked_sums,
        out_grad,
        deep_sums[:, 2],
        deep_sums[:, 3],
        deep_sums[:, 4],
        up_grad,
        up_sums,
        down_grad,
        deep_sums[:, 5],
    )


def solution(mesh):
    devices = mesh.devices
    depth, rows, cols = devices.shape
    chips = Mesh(devices.reshape(depth, rows, cols // 2, 2), ("dp", "row", "pair", "core"))
    col = ("pair", "core")
    placed = (
        P(col, ("dp", "row")),
        P(col, ("dp", "row")),
        P(("dp", "pair", "core"), None),
        P(None, col),
        P(None, col),
        P(None, col, None, "row"),
        P(None, None, "row"),
        P(None, col, "row"),
        P(None, col),
        P(None, col),
        P(None, col),
        P(None, col, "row"),
        P(None, "row"),
        P(None, col, "row"),
        P(None, col),
    )
    return jax.shard_map(
        shards,
        mesh=chips,
        in_specs=placed,
        out_specs=(
            P(col, ("dp", "row")),
            P(col, ("dp", "row")),
            P(None, col),
            P(None, col),
            P(None, col, None, "row"),
            P(None, None, "row"),
            P(None, col, "row"),
            P(None, col),
            P(None, col),
            P(None, col),
            P(None, col, "row"),
            P(None, "row"),
            P(None, col, "row"),
            P(None, col),
        ),
        check_vma=False,
    )
```

time: 1700 us -> 671 us (0.39)
  waiting for transfers between devices: 1240 us -> 277 us
  matrix products: 145 us -> 72.9 us
  local copies, waits for them, and re-layouts: 44.3 us -> 101 us
  blocking collectives: 149 us -> 115 us
  other arithmetic: 85.6 us -> 57.5 us
  starting transfers between devices: 1.93 us -> 22 us
    reduce_scatter x16 -> x0, waiting for transfers between devices: 729 us -> none  [the longest x4 358 us: widen_out(): lax.psum_scatter(partial_sum, 'col', scatter_dimension=0, tiled=True)]
    psum x2 -> x1, waiting for transfers between devices: 255 us -> 24 us  [shards(): attention_grads[layer_at] = lax.psum(scatter_plane(parts), 'dp')]
    all_gather x8 -> x5, waiting for transfers between devices: 259 us -> 98.8 us  [the longest x4 98.8 us: gather_plane(): everything = lax.all_gather(piece, PLANE, axis=0, tiled=False)]
    unnamed x26 -> x14, waiting for transfers between devices: 0.93 us -> 116 us
    all_gather x8 -> x2, blocking collectives: 91.4 us -> 13.4 us  [the longest x1 11.6 us: shards(): lax.all_gather(small, ('row', 'pair', 'core'), axis=0, tiled=False)]
    all_to_all x0 -> x5, waiting for transfers between devices: none -> 33.4 us  [the longest x1 25.5 us: shards(): both = lax.all_to_all(both, 'pair', split_axis=2, concat_axis=1, tiled=True)]
    dot_general x20 -> x28, matrix products: 71.5 us -> 38.5 us  [the longest x16 21.1 us: plain(): return jnp.dot(left_side, right_side, preferred_element_type=jnp.float32)]
    psum x8 -> x1, blocking collectives: 57.2 us -> 81 us  [shards(): lax.psum(jnp.concatenate([deep.reshape(-1), asked.reshape(-1), hidden.res...]
  transfers between devices with their start and end apart: 26 -> 23, of which waited for: 25 -> 13; matrix products, arithmetic and copies ran while one was open for 6% -> 25% of each run, Pallas kernels for 0% -> 0%
where the time goes in v1:
time: 671 us; the launch traced here: 663 us
  waiting for transfers between devices  277 us (41%)
  blocking collectives  115 us (17%)
  local copies, waits for them, and re-layouts  101 us (15%)
  matrix products  72.9 us (11%)
  other arithmetic  57.5 us (9%)
  starting transfers between devices  22 us (3%)
  between operations  17.2 us (3%)
    unnamed x14, waiting for transfers between devices  116 us
    all_gather x4, waiting for transfers between devices, gather_plane(): everything = lax.all_gather(piece, PLANE, axis=0, tiled=False)  98.8 us
    psum x1, blocking collectives, shards(): lax.psum(jnp.concatenate([deep.reshape(-1), asked.reshape(-1), hidden.res...  81 us
    unnamed x337, local copies, waits for them, and re-layouts  28.7 us
    all_to_all x1, waiting for transfers between devices, shards(): both = lax.all_to_all(both, 'pair', split_axis=2, concat_axis=1, tiled=True)  25.5 us
    psum x1, waiting for transfers between devices, shards(): attention_grads[layer_at] = lax.psum(scatter_plane(parts), 'dp')  24 us
    another operation x4, local copies, waits for them, and re-layouts, scatter_plane(): stacked = jnp.stack(grads).astype(jnp.bfloat16)  22 us
    dot_general x16, matrix products, plain(): return jnp.dot(left_side, right_side, preferred_element_type=jnp.float32)  21.1 us
  transfers between devices with their start and end apart: 23, of which 13 were waited for; matrix products, arithmetic and copies ran while one was open for 25% of the time, Pallas kernels for 0%

profile of v1, /device:TPU:0, one launch (start us, length us, event | category | flops | bytes accessed | tf_op | source)
XLA Modules:
  0.0 662.6 jit_solution(2073083201151259178)
XLA Ops:
  7.2 2.2 pad_maximum_fusion.6
  10.3 1.9 copy.158
  13.1 4.7 all_to_all.111
  20.7 2.0 pad_maximum_fusion.2
  23.0 5.6 all_to_all.112
  31.4 11.6 %all-gather.2 = bf16[8,1,7424]{2,1,0:T(2,128)(2,1)S(1)} all-gather(bf16[1,1,7424]{2,1,0:T(2,128)(2,1)S(1)} %reshape.555), channel_id=2, replica_groups=mesh['dp'=4,'row'=2,'pair'=2,'core'=2] {'row','pair','core'}, dimensions={0}, use_global_device_ids=true | all-gather | bytes 133632 | tf_op jit(solution)/shard_map/all_gather | solution.py:183
  44.2 4.9 copy.155
  49.2 3.7 all-to-all-start
  55.7 25.5 %all-to-all-done = bf16[2,384,1024]{1,0,2:T(2,128)(2,1)S(1)} async-done(((bf16[2,384,1024]{1,0,2:T(2,128)(2,1)}), bf16[2,384,1024]{1,0,2:T(2,128)(2,1)S(1)}, u32[]{:S(2)}, u32[]{:S(2)}) %all-to-all-start) | async-done | bytes 1572896 | tf_op jit(solution)/shard_map/all_to_all | solution.py:199
  84.4 2.0 fusion.153
  87.9 1.9 fusion.152
  94.2 1.8 copy-done
  103.2 2.4 fusion.146
  107.5 25.0 %all-gather.14.cloned.1.call-done = bf16[4,384,1536]{2,1,0:T(8,128)(2,1)} async-done(((bf16[1,384,1536]{2,1,0:T(8,128)(2,1)}), bf16[4,384,1536]{2,1,0:T(8,128)(2,1)}) %all-gather.14.cloned.1.call-update) | async-done | bytes 4718608 | tf_op jit(solution)/shard_map/all_gather | solution.py:109
  132.5 2.8 fusion.149
  138.5 2.2 convolution_add_fusion.7
  140.7 31.5 %all-gather.16.cloned.1.call-done = bf16[4,384,768]{2,1,0:T(8,128)(2,1)} async-done(((bf16[1,384,768]{2,1,0:T(8,128)(2,1)}), bf16[4,384,768]{2,1,0:T(8,128)(2,1)}) %all-gather.16.cloned.1.call-update) | async-done | bytes 2359312 | tf_op jit(solution)/shard_map/all_gather | solution.py:109
  172.2 1.8 fusion.151
  174.1 3.1 fusion.145
  188.8 42.3 %all-gather.18.cloned.1.call-done = bf16[4,384,1536]{2,1,0:T(8,128)(2,1)} async-done(((bf16[1,384,1536]{2,1,0:T(8,128)(2,1)}), bf16[4,384,1536]{2,1,0:T(8,128)(2,1)}) %all-gather.18.cloned.1.call-update) | async-done | bytes 4718608 | tf_op jit(solution)/shard_map/all_gather | solution.py:109
  231.0 2.8 fusion.148
  233.9 2.4 fusion.144
  238.3 2.2 convert_reduce_fusion.1
  241.3 2.2 convert_reduce_fusion.2
  251.1 2.8 convert_reduce_fusion.5
  259.2 2.4 convert_reduce_fusion.8
  261.7 2.0 multiply_reduce_fusion.1
  263.7 1.9 multiply_convert_fusion.1
  265.6 2.1 fusion.47
  274.3 4.3 copy.179
  278.7 2.3 convolution_convert_fusion.1
  282.4 2.0 convolution_add_fusion.2
  289.4 2.5 pad_maximum_fusion.1
  291.9 6.8 %copy.187 = bf16[2,768,1536]{2,1,0:T(8,128)(2,1)} copy(bf16[2,768,1536]{1,2,0:T(8,128)(2,1)} %pad_maximum_fusion.1) | data formatting | bytes 9437184 | tf_op jit(solution)/shard_map/stack | solution.py:116
  299.0 4.0 multiply_reduce_fusion.3
  305.2 2.2 convert_reduce_fusion.4
  309.3 2.2 convert_reduce_fusion.3
  312.8 3.0 collective-permute-done.6
  319.0 1.8 convolution_convert_fusion.16
  324.3 1.8 multiply_reduce_fusion
  326.2 1.9 multiply_convert_fusion
  334.6 4.3 copy.176
  340.0 2.1 convolution_convert_fusion.5
  347.4 2.6 pad_maximum_fusion
  350.0 6.8 %copy.185 = bf16[2,768,1536]{2,1,0:T(8,128)(2,1)} copy(bf16[2,768,1536]{1,2,0:T(8,128)(2,1)} %pad_maximum_fusion) | data formatting | bytes 9437184 | tf_op jit(solution)/shard_map/stack | solution.py:116
  357.1 2.3 fusion.99
  359.4 2.0 convolution_add_fusion
  361.7 14.5 %reduce-scatter.19.cloned.1.call-done = bf16[1,384,1536]{2,1,0:T(8,128)(2,1)} async-done(((bf16[4,384,1536]{2,1,0:T(8,128)(2,1)}), bf16[1,384,1536]{2,1,0:T(8,128)(2,1)}) %reduce-scatter.19.cloned.1.call-update) | async-done | bytes 1179664
  376.3 41.1 %reduce-scatter.13.cloned.1.call-done = bf16[1,384,768]{2,1,0:T(8,128)(2,1)} async-done(((bf16[4,384,768]{2,1,0:T(8,128)(2,1)}), bf16[1,384,768]{2,1,0:T(8,128)(2,1)}) %reduce-scatter.13.cloned.1.call-update) | async-done | bytes 589840
  417.3 60.1 %reduce-scatter.17.cloned.1.call-done = bf16[1,384,1536]{2,1,0:T(8,128)(2,1)} async-done(((bf16[4,384,1536]{2,1,0:T(8,128)(2,1)}), bf16[1,384,1536]{2,1,0:T(8,128)(2,1)}) %reduce-scatter.17.cloned.1.call-update) | async-done | bytes 1179664
  481.6 3.5 all-to-all-start.3
  485.6 6.4 all-to-all-done.3
  493.7 2.9 multiply_reduce_fusion.5
  498.7 3.5 all-to-all-start.4
  502.3 81.0 %psum.35 = f32[13824]{0:T(1024)S(1)} all-reduce(f32[13824]{0:T(1024)S(1)} %pad_maximum_fusion.21), channel_id=1, replica_groups=mesh['dp'=4,'row'=2,'pair'=2,'core'=2] {'dp','row','pair'}, use_global_device_ids=true, to_apply=%region_42.43 | all-reduce | flops 13824 | bytes 110592 | tf_op jit(solution)/shard_map/psum | solution.py:350
  583.3 1.8 all-gather.3
  591.9 24.0 %all-reduce.7.cloned.1.call-done = (bf16[2,192,1,768]{3,1,0,2:T(8,128)(2,1)}, bf16[2,192,1,768]{3,1,0,2:T(8,128)(2,1)}, bf16[2,192,1,1536]{3,1,0,2:T(8,128)(2,1)}, bf16[2,192,1,1536]{3,1,0,2:T(8,128)(2,1)}) async-done(((bf16[2,192,1,768]{3,1,0,2:T(8,128)(2,1)}, bf16[2,192,1,768]{3,1,0,2:T(8,128)(2,1)}, bf16[2,192,1,1536]{3,1,0,2:T(8,128)(2,1)}, bf16[2,192,1,1536]{3,1,0,2:T(8,128)(2,1)}), ...) | async-done | bytes 3538960 | tf_op jit(solution)/shard_map/psum | solution.py:323
  615.9 5.3 all_to_all.113
  621.2 3.5 all-to-all-start.5
  630.3 4.5 all-to-all-start.8
  634.8 2.2 copy.199
  638.6 3.4 copy.182
  642.0 3.1 reshape.533
  645.1 4.7 all_to_all.114
  (562 shorter events, 125.4 us)
Async XLA Ops:
  7.2 37.0 %all-gather.10.cloned.1.call-start = ((), (), s32[]{:S(2)}) async-start(), calls=%async_computation.13 | async-start | bytes 2359296 | tf_op jit(solution)/shard_map/all_gather | solution.py:198
  9.4 78.4 %all-gather.12.cloned.1.call-start = ((), (), s32[]{:S(2)}) async-start(), calls=%async_computation.14 | async-start | bytes 2949120 | tf_op jit(solution)/shard_map/all_gather | solution.py:109
  19.0 113.5 %all-gather.14.cloned.1.call-start = ((), (), s32[]{:S(2)}) async-start(), calls=%async_computation.15 | async-start | bytes 5898240 | tf_op jit(solution)/shard_map/all_gather | solution.py:109
  30.5 141.8 %all-gather.16.cloned.1.call-start = ((), (), s32[]{:S(2)}) async-start(), calls=%async_computation.16 | async-start | bytes 2949120 | tf_op jit(solution)/shard_map/all_gather | solution.py:109
  43.7 5.4 copy-start.69
  49.2 32.1 %all-to-all-start = ((bf16[2,384,1024]{1,0,2:T(2,128)(2,1)}), bf16[2,384,1024]{1,0,2:T(2,128)(2,1)S(1)}, u32[]{:S(2)}, u32[]{:S(2)}) async-start(bf16[2,384,1024]{1,0,2:T(2,128)(2,1)} %copy.155), calls=%async_computation | async-start | bytes 3145728 | tf_op jit(solution)/shard_map/all_to_all | solution.py:199
  52.8 178.2 %all-gather.18.cloned.1.call-start = ((), (), s32[]{:S(2)}) async-start(), calls=%async_computation.17 | async-start | bytes 5898240 | tf_op jit(solution)/shard_map/all_gather | solution.py:109
  54.8 31.9 %copy-start.91 = (f32[768]{0:T(1024)}, f32[768]{0:T(1024)S(1)}, u32[]{:S(2)}) copy-start(f32[768]{0:T(1024)S(1)} %get-tuple-element.47) | copy-start | bytes 9220
  89.7 7.5 %copy-start.26 = (bf16[2,384,768]{2,1,0:T(8,128)(2,1)}, bf16[2,384,768]{2,1,0:T(8,128)(2,1)S(1)}, u32[]{:S(2)}) copy-start(bf16[2,384,768]{2,1,0:T(8,128)(2,1)S(1)} %get-tuple-element.83) | copy-start | bytes 3538948
  89.7 8.1 %copy-start.7 = (bf16[2,384,768]{2,1,0:T(8,128)(2,1)}, bf16[2,384,768]{2,1,0:T(8,128)(2,1)S(1)}, u32[]{:S(2)}) copy-start(bf16[2,384,768]{2,1,0:T(8,128)(2,1)S(1)} %get-tuple-element.82) | copy-start | bytes 3538948
  98.4 4.8 copy-start.18
  98.4 4.8 collective-permute-start
  98.5 263.2 %reduce-scatter.15.cloned.1.call-start = ((), (), s32[]{:S(2)}) async-start(), calls=%async_computation.19 | async-start | bytes 2949120
  140.7 33.3 %collective-permute-start.1 = (f32[512,768]{1,0:T(8,128)}, f32[512,768]{1,0:T(8,128)}, u32[]{:S(2)}, u32[]{:S(2)}) collective-permute-start(f32[512,768]{1,0:T(8,128)} %convolution_add_fusion.7), channel_id=1, source_target_pairs={{0,1},{1,0},{2,3},{3,2},{4,5},{5,4},{6,7},{7,6},{8,9},{9,8},{10,11... | collective-permute-start | bytes 4718600 | tf_op jit(solution)/shard_map/ppermute | solution.py:31
  174.0 11.4 %copy-start.27 = (bf16[2,384,768]{2,1,0:T(8,128)(2,1)}, bf16[2,384,768]{2,1,0:T(8,128)(2,1)S(1)}, u32[]{:S(2)}) copy-start(bf16[2,384,768]{2,1,0:T(8,128)(2,1)S(1)} %get-tuple-element.81) | copy-start | bytes 3538948
  174.0 12.0 %copy-start.9 = (bf16[2,384,768]{2,1,0:T(8,128)(2,1)}, bf16[2,384,768]{2,1,0:T(8,128)(2,1)S(1)}, u32[]{:S(2)}) copy-start(bf16[2,384,768]{2,1,0:T(8,128)(2,1)S(1)} %get-tuple-element.80) | copy-start | bytes 3538948
  187.8 46.1 %collective-permute-start.2 = (f32[512,768]{1,0:T(8,128)}, f32[512,768]{1,0:T(8,128)}, u32[]{:S(2)}, u32[]{:S(2)}) collective-permute-start(f32[512,768]{1,0:T(8,128)} %convolution_add_fusion.10), channel_id=1, source_target_pairs={{0,1},{1,0},{2,3},{3,2},{4,5},{5,4},{6,7},{7,6},{8,9},{9,8},{10,11... | collective-permute-start | bytes 4718600 | tf_op jit(solution)/shard_map/ppermute | solution.py:31
  237.8 8.6 %copy-start.149 = (f32[512,768]{1,0:T(8,128)}, f32[512,768]{1,0:T(8,128)S(1)}, u32[]{:S(2)}) copy-start(f32[512,768]{1,0:T(8,128)S(1)} %convolution_add_fusion.5) | copy-start | bytes 4718596
  240.5 3.9 copy-start.58
  241.3 4.0 copy-start.151
  245.2 3.5 collective-permute-start.4
  247.5 3.6 collective-permute-start.3
  248.7 10.6 %slice-start.2 = ((s8[6291456]{0:T(1024)(128)(4,1)}), s8[4194304]{0:T(1024)(128)(4,1)S(1)}, s32[]{:S(2)}) async-start(s8[6291456]{0:T(1024)(128)(4,1)} %bitcast.345), calls=%async_computation.25 | async-start | bytes 8388608
  251.1 8.1 %slice-start.3 = ((s8[6291456]{0:T(1024)(128)(4,1)}), s8[2097152]{0:T(1024)(128)(4,1)S(1)}, s32[]{:S(2)}) async-start(s8[6291456]{0:T(1024)(128)(4,1)} %bitcast.345), calls=%async_computation.26 | async-start | bytes 4194304
  278.6 97.7 %reduce-scatter.19.cloned.1.call-start = ((), (), s32[]{:S(2)}) async-start(), calls=%async_computation.21 | async-start | bytes 5898240
  284.4 14.5 %collective-permute-start.5 = (f32[512,768]{1,0:T(8,128)}, f32[512,768]{1,0:T(8,128)}, u32[]{:S(2)}, u32[]{:S(2)}) collective-permute-start(f32[512,768]{1,0:T(8,128)} %convolution_add_fusion.2), channel_id=1, source_target_pairs={{0,1},{1,0},{2,3},{3,2},{4,5},{5,4},{6,7},{7,6},{8,9},{9,8},{10,11... | collective-permute-start | bytes 4718600 | tf_op jit(solution)/shard_map/ppermute | solution.py:31
  298.7 118.7 %reduce-scatter.13.cloned.1.call-start = ((), (), s32[]{:S(2)}) async-start(), calls=%async_computation.18 | async-start | bytes 2949120
  298.9 4.1 copy-start.4
  298.9 4.1 copy-start.16
  298.9 4.1 copy-start.85
  298.9 4.1 copy-start.102
  298.9 4.1 copy-start.104
  304.3 3.9 copy-start.56
  311.4 4.3 copy-start.83
  311.4 4.3 copy-start.98
  311.4 4.3 copy-start.100
  312.3 3.5 collective-permute-start.6
  315.8 6.6 slice-start
  317.2 5.2 slice-start.1
  319.0 4.6 copy-start.5
  338.9 138.6 %reduce-scatter.17.cloned.1.call-start = ((), (), s32[]{:S(2)}) async-start(), calls=%async_computation.20 | async-start | bytes 5898240
  356.8 259.1 %all-reduce.7.cloned.1.call-start = ((), (), s32[]{:S(2)}) async-start(), calls=%async_computation.22 | async-start | bytes 7077888 | tf_op jit(solution)/shard_map/psum | solution.py:323
  361.4 132.3 %collective-permute-start.7 = (f32[512,768]{1,0:T(8,128)}, f32[512,768]{1,0:T(8,128)}, u32[]{:S(2)}, u32[]{:S(2)}) collective-permute-start(f32[512,768]{1,0:T(8,128)} %convolution_add_fusion), channel_id=1, source_target_pairs={{0,1},{1,0},{2,3},{3,2},{4,5},{5,4},{6,7},{7,6},{8,9},{9,8},{10,11... | collective-permute-start | bytes 4718600 | tf_op jit(solution)/shard_map/ppermute | solution.py:31
  478.6 6.5 copy-start.13
  479.8 5.5 copy-start.127
  479.8 5.6 copy-start.128
  479.8 5.6 copy-start.116
  479.8 5.6 copy-start.115
  479.8 5.6 copy-start.106
  479.8 5.6 copy-start.107
  479.8 5.7 copy-start.108
  481.6 11.6 %copy-start.118 = (f32[768]{0:T(1024)S(1)}, f32[768]{0:T(1024)}, u32[]{:S(2)}) copy-start(f32[768]{0:T(1024)} %get-tuple-element.20) | copy-start | bytes 9220
  481.6 11.6 %copy-start.105 = (f32[768]{0:T(1024)S(1)}, f32[768]{0:T(1024)}, u32[]{:S(2)}) copy-start(f32[768]{0:T(1024)} %get-tuple-element.56) | copy-start | bytes 9220
  481.6 11.6 %copy-start.117 = (f32[768]{0:T(1024)S(1)}, f32[768]{0:T(1024)}, u32[]{:S(2)}) copy-start(f32[768]{0:T(1024)} %get-tuple-element.29) | copy-start | bytes 9220
  481.6 11.6 %copy-start.130 = (f32[768]{0:T(1024)S(1)}, f32[768]{0:T(1024)}, u32[]{:S(2)}) copy-start(f32[768]{0:T(1024)} %get-tuple-element.145) | copy-start | bytes 9220
  481.6 11.7 %copy-start.129 = (f32[768]{0:T(1024)S(1)}, f32[768]{0:T(1024)}, u32[]{:S(2)}) copy-start(f32[768]{0:T(1024)} %get-tuple-element.147) | copy-start | bytes 9220
  481.6 11.8 %copy-start.119 = (f32[768]{0:T(1024)S(1)}, f32[768]{0:T(1024)}, u32[]{:S(2)}) copy-start(f32[768]{0:T(1024)} %get-tuple-element.14) | copy-start | bytes 9220
  481.6 12.1 %copy-start.92 = (f32[768]{0:T(1024)S(1)}, f32[768]{0:T(1024)}, u32[]{:S(2)}) copy-start(f32[768]{0:T(1024)} %copy-done.91) | copy-start | bytes 9220
  481.6 12.0 %copy-start.94 = (f32[512]{0:T(512)S(1)}, f32[512]{0:T(512)}, u32[]{:S(2)}) copy-start(f32[512]{0:T(512)} %copy-done.93) | copy-start | bytes 6148
  481.6 12.0 %copy-start.96 = (f32[512]{0:T(512)S(1)}, f32[512]{0:T(512)}, u32[]{:S(2)}) copy-start(f32[512]{0:T(512)} %copy-done.95) | copy-start | bytes 6148
  481.6 10.3 %all-to-all-start.3 = ((bf16[2,192,512]{2,1,0:T(8,128)(2,1)}), bf16[2,192,512]{2,1,0:T(8,128)(2,1)S(1)}, u32[]{:S(2)}, u32[]{:S(2)}) async-start(bf16[2,192,512]{2,1,0:T(8,128)(2,1)} %dynamic-slice_bitcast_fusion.1), calls=%async_computation.3 | async-start | bytes 786432 | tf_op jit(solution)/shard_map/all_to_all | solution.py:261
  498.7 91.5 %all-to-all-start.4 = ((f32[2,192,512]{2,1,0:T(8,128)}), f32[2,192,512]{2,1,0:T(8,128)S(1)}, u32[]{:S(2)}, u32[]{:S(2)}) async-start(f32[2,192,512]{2,1,0:T(8,128)} %dynamic-slice_bitcast_fusion), calls=%async_computation.4 | async-start | bytes 1572864 | tf_op jit(solution)/shard_map/all_to_all | solution.py:261
  621.2 5.3 all-to-all-start.5
  630.3 14.8 %all-to-all-start.8 = ((bf16[2,192,1,1536]{3,1,2,0:T(8,128)(2,1)}), bf16[2,192,1,1536]{3,1,2,0:T(8,128)(2,1)}, u32[]{:S(2)}, u32[]{:S(2)}) async-start(bf16[2,192,1,1536]{3,1,2,0:T(8,128)(2,1)} %bitcast.459), calls=%async_computation.8 | async-start | bytes 2359296 | tf_op jit(solution)/shard_map/all_to_all | solution.py:123
  (116 other events, 215.5 us)
Sparse Core Ops, SparseCore 0:
  10.2 12.4 all-gather.9
  25.1 47.9 all-gather.11
  75.6 56.8 all-gather.13
  134.7 37.4 all-gather.15
  173.9 57.0 all-gather.17
  278.7 37.4 reduce-scatter.14
  319.1 57.0 reduce-scatter.18
  379.9 37.3 reduce-scatter.12
  420.3 57.0 reduce-scatter.16
  479.9 135.9 all-reduce.6

commit v2 on v1

--- a/solution.py
+++ b/solution.py
@@ -99,30 +99,57 @@
     return query_grad, key_grad, value_grad
 
 
+def swap(value, axis):
+    return lax.ppermute(value, axis, [(0, 1), (1, 0)])
+
+
+def by_core(mine, other, axis):
+    first = lax.axis_index("core") == 0
+    return jnp.concatenate([jnp.where(first, mine, other), jnp.where(first, other, mine)], axis)
+
+
 def share_weights(parts):
     joined = jnp.concatenate(parts, axis=-1)
-    mine = lax.all_to_all(joined, "core", split_axis=2, concat_axis=1, tiled=True)
-    return mine[:, :, 0]
+    first = lax.axis_index("core") == 0
+    kept = jnp.where(first, joined[:, 0], joined[:, 1])
+    given = jnp.where(first, joined[:, 1], joined[:, 0])
+    return by_core(kept, swap(given, "core"), 0)
 
 
 def gather_plane(piece):
-    everything = lax.all_gather(piece, PLANE, axis=0, tiled=False)
-    rows = lax.axis_size("row")
-    return everything.reshape(rows, -1, piece.shape[-1])
+    half = piece.shape[0] // 2
+    over_row, over_pair = swap(piece, "row"), swap(piece, "pair")
+    top, bottom = swap(over_row[:half], "pair"), swap(over_pair[half:], "row")
+    return (
+        jnp.concatenate([piece, over_pair], axis=0),
+        jnp.concatenate([over_row, top, bottom], axis=0),
+    )
+
+
+def added(left_side, right_side):
+    return left_side.astype(jnp.float32) + right_side.astype(jnp.float32)
 
 
 def scatter_plane(grads):
-    pairs = lax.axis_size("pair")
-    stacked = jnp.stack(grads).astype(jnp.bfloat16)
-    stacked = stacked.reshape(len(grads) * pairs, -1, stacked.shape[-1])
-    return lax.psum_scatter(stacked, PLANE, scatter_dimension=0, tiled=False)
+    own, other = (part.astype(jnp.bfloat16).reshape(2, 2, -1, part.shape[-1]) for part in grads)
+    sum_top = added(own[:, 0], swap(other[:, 0], "row")).astype(jnp.bfloat16)
+    theirs = swap(jnp.stack([own[1, 1], other[1, 1]]), "pair")
+    sum_own = added(own[0, 1], theirs[0])
+    sum_other = added(other[0, 1], theirs[1]).astype(jnp.bfloat16)
+    top = added(sum_top[0], swap(sum_top[1], "pair")).astype(jnp.bfloat16)
+    bottom = added(sum_own, swap(sum_other, "row")).astype(jnp.bfloat16)
+    return jnp.stack([top, bottom])
 
 
 def return_weights(piece):
-    depth = piece.shape[0] // 2
-    return lax.all_to_all(
-        piece.reshape(2, depth, 1, piece.shape[-1]), "core", split_axis=0, concat_axis=2, tiled=True
-    )[0].astype(jnp.float32)
+    first = lax.axis_index("core") == 0
+    kept = jnp.where(first, piece[0], piece[1])
+    given = jnp.where(first, piece[1], piece[0])
+    return by_core(kept[:, None], swap(given, "core")[:, None], 1).astype(jnp.float32)
+
+
+def chained(value, before):
+    return lax.optimization_barrier((value, before))[0]
 
 
 def shards(
@@ -150,25 +177,32 @@
     width = depth_in * pairs * 2
     length = segments.shape[1]
 
-    attention_part = share_weights(
-        [
-            qkv_weight.reshape(layers, depth_in, 3, 2, half_head)
-            .transpose(0, 1, 3, 2, 4)
-            .reshape(layers, depth_in, 2, 3 * half_head),
-            out_weight.reshape(layers, depth_in, 2, half_head),
-        ]
-    )
-    forward_part = share_weights(
-        [
-            up_weight.reshape(layers, depth_in, 2, half_hidden),
-            down_weight.reshape(layers, depth_in, 2, half_hidden),
-        ]
-    )
     attention_weights = []
     forward_weights = []
     for layer_at in range(layers):
-        attention_weights.append(gather_plane(attention_part[layer_at]))
-        forward_weights.append(gather_plane(forward_part[layer_at]))
+        attention_weights.append(
+            gather_plane(
+                share_weights(
+                    [
+                        qkv_weight[layer_at]
+                        .reshape(depth_in, 3, 2, half_head)
+                        .transpose(0, 2, 1, 3)
+                        .reshape(depth_in, 2, 3 * half_head),
+                        out_weight[layer_at].reshape(depth_in, 2, half_head),
+                    ]
+                )
+            )
+        )
+        forward_weights.append(
+            gather_plane(
+                share_weights(
+                    [
+                        up_weight[layer_at].reshape(depth_in, 2, half_hidden),
+                        down_weight[layer_at].reshape(depth_in, 2, half_hidden),
+                    ]
+                )
+            )
+        )
 
     small = jnp.concatenate(
         [
@@ -182,6 +216,12 @@
     )
     small = lax.all_gather(small, ("row", "pair", "core"), axis=0, tiled=False).astype(jnp.float32)
     small = small.reshape(rows, pairs * 2, -1)
+    document = lax.dynamic_index_in_dim(
+        small[0, :, small.shape[-1] - length :], at_row * pairs + at_pair, 0, keepdims=False
+    )
+    small = small.reshape(rows, pairs, 2, -1)
+    small = jnp.where(at_row == 0, small, small[::-1])
+    small = jnp.where(at_pair == 0, small, small[:, ::-1]).reshape(rows, pairs * 2, -1)
     cuts = [6 * layers * depth_in, 2 * layers * head_width, layers * hidden_width]
     cuts = [cuts[0], cuts[0] + cuts[1], cuts[0] + cuts[1] + cuts[2]]
     vectors = small[0, :, : cuts[0]].reshape(pairs * 2, 6, layers, depth_in)
@@ -190,15 +230,16 @@
     query_bias = lax.dynamic_index_in_dim(query_bias, at_core, 3, keepdims=False)
     hidden_bias = small[:, 0, cuts[1] : cuts[2]].reshape(rows, layers, 2, half_hidden)
     hidden_bias = lax.dynamic_index_in_dim(hidden_bias, at_core, 2, keepdims=False)
-    document = lax.dynamic_index_in_dim(
-        small[0, :, cuts[2] :], at_row * pairs + at_pair, 0, keepdims=False
-    )
-
-    both = jnp.stack([tokens, cotangent])
-    both = lax.all_gather(both, "core", axis=1, tiled=True)
-    both = lax.all_to_all(both, "pair", split_axis=2, concat_axis=1, tiled=True)
-    residual = both[0].astype(jnp.float32).T
-    gradient = both[1].astype(jnp.float32).T
+
+    def to_chip(value):
+        kept = lax.dynamic_slice_in_dim(value, at_pair * length, length, 1)
+        given = lax.dynamic_slice_in_dim(value, (1 - at_pair) * length, length, 1)
+        mine = jnp.stack([kept, swap(given, "pair")])
+        whole = by_core(mine[:, None], swap(mine, "core")[:, None], 1)
+        return whole.reshape(width, length).astype(jnp.float32).T
+
+    residual = to_chip(tokens)
+    gradient = to_chip(cotangent)
 
     stored = []
     for layer_at in range(layers):
@@ -257,8 +298,12 @@
 
     def to_owner(value):
         blocks = value.T.reshape(pairs, 2, depth_in, length)
-        blocks = lax.dynamic_index_in_dim(blocks, at_core, 1, keepdims=False)
-        return lax.all_to_all(blocks, "pair", split_axis=0, concat_axis=2, tiled=True)[0]
+        blocks = jnp.where(at_core == 0, blocks[:, 0], blocks[:, 1])
+        kept, came = blocks[0], swap(blocks[1], "pair")
+        first = at_pair == 0
+        return jnp.concatenate(
+            [jnp.where(first, kept, came), jnp.where(first, came, kept)], axis=1
+        )
 
     activations = to_owner(residual.astype(jnp.bfloat16))
 
@@ -294,7 +339,10 @@
             normed_grad = normed_grad + contract_cols(hidden_grad, wide[row][:, :half_hidden])
             hidden_grads.append(jnp.sum(hidden_grad.astype(jnp.float32), axis=0))
             parts.append(jnp.concatenate([up_grad, down_grad], axis=1))
-        forward_grads[layer_at] = lax.psum(scatter_plane(parts), "dp")
+        summed = scatter_plane(parts)
+        if layer_at + 1 < layers:
+            summed = chained(summed, attention_grads[layer_at + 1])
+        forward_grads[layer_at] = lax.psum(summed, "dp")
         back_two, gain_two_grad, shift_two_grad = norm_backward(
             pair_sum(normed_grad), unit_two, inverse_two, gain_two
         )
@@ -320,7 +368,8 @@
                 jnp.concatenate([contract_rows(normed_one, pieces), out_grads[row]], axis=1)
             )
             normed_grad = normed_grad + contract_cols(pieces, mixing[row][:, : 3 * half_head])
-        attention_grads[layer_at] = lax.psum(scatter_plane(parts), "dp")
+        summed = chained(scatter_plane(parts), forward_grads[layer_at])
+        attention_grads[layer_at] = lax.psum(summed, "dp")
         back_one, gain_one_grad, shift_one_grad = norm_backward(
             pair_sum(normed_grad), unit_one, inverse_one, gain_one
         )
@@ -347,11 +396,17 @@
     deep, asked, hidden = (
         jnp.stack([vector_parts[layer_at][part] for layer_at in range(layers)]) for part in range(3)
     )
+    deep = deep.reshape(layers, 6, pairs, 2 * depth_in)
+    deep = jnp.where(at_pair == 0, deep, deep[:, :, ::-1])
+    asked = jnp.where(at_row == 0, asked, asked[:, :, ::-1])
+    hidden = jnp.where(at_row == 0, hidden, hidden[:, ::-1])
     sums = lax.psum(
         jnp.concatenate([deep.reshape(-1), asked.reshape(-1), hidden.reshape(-1)]),
         ("dp", "row", "pair"),
     )
-    hidden_sums = lax.all_gather(sums[deep.size :], "core", axis=0, tiled=False)
+    hidden_sums = by_core(
+        sums[None, deep.size :], swap(sums[deep.size :], "core")[None], 0
+    )
     deep_sums = lax.dynamic_slice_in_dim(
         sums[: deep.size].reshape(layers, 6, width), (at_pair * 2 + at_core) * depth_in, depth_in, 2
     )

time: 671 us -> 685 us (1.021)
  waiting for transfers between devices: 277 us -> 192 us
  other arithmetic: 57.5 us -> 123 us
  local copies, waits for them, and re-layouts: 101 us -> 138 us
  blocking collectives: 115 us -> 86.1 us
  starting transfers between devices: 22 us -> 42 us
  matrix products: 72.9 us -> 80.5 us
    ppermute x0 -> x47, waiting for transfers between devices: none -> 128 us  [swap(): return lax.ppermute(value, axis, [(0, 1), (1, 0)])]
    unnamed x14 -> x4, waiting for transfers between devices: 116 us -> 0.07 us
    all_gather x5 -> x0, waiting for transfers between devices: 98.8 us -> none  [the longest x4 98.8 us: gather_plane(): everything = lax.all_gather(piece, PLANE, axis=0, tiled=False)]
    ppermute x0 -> x47, starting transfers between devices: none -> 41 us  [swap(): return lax.ppermute(value, axis, [(0, 1), (1, 0)])]
    psum x1 -> x4, waiting for transfers between devices: 24 us -> 63.4 us  [the longest x2 51.8 us: shards(): forward_grads[layer_at] = lax.psum(summed, 'dp')]
    all_to_all x5 -> x0, waiting for transfers between devices: 33.4 us -> none  [the longest x1 25.5 us: shards(): both = lax.all_to_all(both, 'pair', split_axis=2, concat_axis=1, tiled=True)]
    select_n x0 -> x24, other arithmetic: none -> 23.2 us  [the longest x7 7.74 us: by_core(): jnp.where(first, mine, other)]
    all_to_all x4 -> x0, blocking collectives: 20.3 us -> none  [the longest x2 10.3 us: share_weights(): lax.all_to_all(joined, 'core', split_axis=2, concat_axis=1, tiled=True)]
  transfers between devices with their start and end apart: 23 -> 59, of which waited for: 13 -> 18; matrix products, arithmetic and copies ran while one was open for 25% -> 44% of each run, Pallas kernels for 0% -> 0%
where the time goes in v2:
time: 685 us; the launch traced here: 678 us
  waiting for transfers between devices  192 us (28%)
  local copies, waits for them, and re-layouts  138 us (20%)
  other arithmetic  123 us (18%)
  blocking collectives  86.1 us (13%)
  matrix products  80.5 us (12%)
  starting transfers between devices  42 us (6%)
  between operations  17.8 us (3%)
    ppermute x47, waiting for transfers between devices, swap(): return lax.ppermute(value, axis, [(0, 1), (1, 0)])  128 us
    psum x1, blocking collectives, shards(): lax.psum(jnp.concatenate([deep.reshape(-1), asked.reshape(-1), hidden.res...  76.1 us
    psum x2, waiting for transfers between devices, shards(): forward_grads[layer_at] = lax.psum(summed, 'dp')  51.8 us
    ppermute x47, starting transfers between devices, swap(): return lax.ppermute(value, axis, [(0, 1), (1, 0)])  41 us
    unnamed x452, local copies, waits for them, and re-layouts  31.8 us
    dot_general x16, matrix products, contract_cols(): lax.dot_general(left_side, right_side, (((1,), (1,)), ((), ())), preferre...  27.4 us
    dot_general x16, matrix products, contract_rows(): lax.dot_general(left_side, right_side, (((0,), (0,)), ((), ())), preferre...  20.2 us
    dot_general x16, matrix products, plain(): return jnp.dot(left_side, right_side, preferred_element_type=jnp.float32)  14.7 us
  transfers between devices with their start and end apart: 59, of which 18 were waited for; matrix products, arithmetic and copies ran while one was open for 44% of the time, Pallas kernels for 0%

profile of v2, /device:TPU:0, one launch (start us, length us, event | category | flops | bytes accessed | tf_op | source)
XLA Modules:
  0.0 678.5 jit_solution(5006526704819928180)
XLA Ops:
  9.1 3.0 collective-permute-start
  23.8 10.0 %all-gather.1 = bf16[8,1,7424]{2,1,0:T(2,128)(2,1)S(1)} all-gather(bf16[1,1,7424]{2,1,0:T(2,128)(2,1)S(1)} %reshape.741), channel_id=2, replica_groups=mesh['dp'=4,'row'=2,'pair'=2,'core'=2] {'row','pair','core'}, dimensions={0}, use_global_device_ids=true | all-gather | bytes 133632 | tf_op jit(solution)/shard_map/all_gather | solution.py:217
  56.9 5.2 collective-permute-done.4
  69.8 3.0 collective-permute-done.5
  74.3 20.7 %collective-permute-done.6 = bf16[192,768]{0,1:T(8,128)(2,1)S(1)} collective-permute-done((bf16[192,768]{0,1:T(8,128)(2,1)S(1)}, bf16[192,768]{0,1:T(8,128)(2,1)S(1)}, u32[]{:S(2)}, u32[]{:S(2)}) %collective-permute-start.6) | collective-permute-done | bytes 294944 | tf_op jit(solution)/shard_map/ppermute | solution.py:103
  109.4 2.1 bitcast_select_fusion.13
  119.2 8.9 %collective-permute-done.11 = bf16[192,1536]{1,0:T(8,128)(2,1)S(1)} collective-permute-done((bf16[192,1536]{1,0:T(8,128)(2,1)S(1)}, bf16[192,1536]{1,0:T(8,128)(2,1)S(1)}, u32[]{:S(2)}, u32[]{:S(2)}) %collective-permute-start.11) | collective-permute-done | bytes 589856 | tf_op jit(solution)/shard_map/ppermute | solution.py:103
  129.7 2.0 collective-permute-done.12
  131.8 2.7 fusion.218
  138.0 2.2 convolution_add_fusion.8
  141.5 2.0 collective-permute-start.22
  145.4 2.0 collective-permute-start.17
  149.4 2.4 copy.214
  152.3 28.1 %collective-permute-done.17 = bf16[192,768]{0,1:T(8,128)(2,1)} collective-permute-done((bf16[192,768]{0,1:T(8,128)(2,1)}, bf16[192,768]{0,1:T(8,128)(2,1)}, u32[]{:S(2)}, u32[]{:S(2)}) %collective-permute-start.17) | collective-permute-done | bytes 294944 | tf_op jit(solution)/shard_map/ppermute | solution.py:103
  182.9 2.7 fusion.217
  204.8 8.9 %collective-permute-done.23 = bf16[192,1536]{1,0:T(8,128)(2,1)S(1)} collective-permute-done((bf16[192,1536]{1,0:T(8,128)(2,1)S(1)}, bf16[192,1536]{1,0:T(8,128)(2,1)S(1)}, u32[]{:S(2)}, u32[]{:S(2)}) %collective-permute-start.23) | collective-permute-done | bytes 589856 | tf_op jit(solution)/shard_map/ppermute | solution.py:103
  213.7 2.0 collective-permute-done.24
  215.8 2.3 fusion.216
  236.1 19.9 %collective-permute-done.46 = bf16[2,192,1536]{2,1,0:T(8,128)(2,1)S(1)} collective-permute-done((bf16[2,192,1536]{2,1,0:T(8,128)(2,1)S(1)}, bf16[2,192,1536]{2,1,0:T(8,128)(2,1)S(1)}, u32[]{:S(2)}, u32[]{:S(2)}) %collective-permute-start.46) | collective-permute-done | bytes 1179680 | tf_op jit(solution)/shard_map/ppermute | solution.py:103
  262.0 2.8 convert_reduce_fusion.5
  267.9 2.4 convert_reduce_fusion.8
  273.8 2.1 fusion.51
  279.3 2.0 fusion.129
  288.7 2.0 concatenate.308
  293.2 2.3 copy.212
  301.1 2.3 copy.241
  303.4 3.0 convolution_convert_fusion.9
  306.4 2.2 copy.238
  308.6 2.4 copy.239
  311.0 2.3 copy.242
  315.8 2.2 copy.246
  318.4 3.9 convolution_add_fusion.1
  323.3 2.2 copy.244
  333.4 5.1 collective-permute-done.42
  338.5 2.2 copy.245
  342.3 2.2 fusion.224
  356.5 2.4 collective-permute-done.45
  361.2 26.6 %all-reduce.5.cloned.1.call-done = bf16[2,192,1536]{2,1,0:T(8,128)(2,1)} async-done(((bf16[2,192,1536]{2,1,0:T(8,128)(2,1)}), bf16[2,192,1536]{2,1,0:T(8,128)(2,1)}) %all-reduce.5.cloned.1.call-update) | async-done | bytes 1179664 | tf_op jit(solution)/shard_map/psum | solution.py:345
  387.8 2.1 select_bitcast_fusion
  390.1 2.8 multiply_reduce_fusion.3
  399.5 2.4 convert_reduce_fusion.4
  403.9 2.0 fusion.102
  408.7 3.4 convolution_convert_fusion.7
  412.1 3.4 convolution_add_fusion.2
  421.9 11.6 %all-reduce.7.cloned.1.call-done = bf16[2,192,768]{1,2,0:T(8,128)(2,1)} async-done(((bf16[2,192,768]{1,2,0:T(8,128)(2,1)}), bf16[2,192,768]{1,2,0:T(8,128)(2,1)}) %all-reduce.7.cloned.1.call-update) | async-done | bytes 589840 | tf_op jit(solution)/shard_map/psum | solution.py:372
  435.0 2.3 fusion.155
  438.3 6.9 %collective-permute-done.38 = bf16[2,192,1536]{2,1,0:T(8,128)(2,1)} collective-permute-done((bf16[2,192,1536]{2,1,0:T(8,128)(2,1)}, bf16[2,192,1536]{2,1,0:T(8,128)(2,1)}, u32[]{:S(2)}, u32[]{:S(2)}) %collective-permute-start.38) | collective-permute-done | bytes 1179680 | tf_op jit(solution)/shard_map/ppermute | solution.py:103
  449.2 2.0 fusion.75
  452.7 3.5 multiply_reduce_fusion.4
  456.3 2.3 convert_reduce_fusion.7
  482.8 3.9 convolution_add_fusion
  487.7 2.3 copy.228
  494.7 10.1 %collective-permute-done.34 = bf16[2,192,768]{2,1,0:T(8,128)(2,1)} collective-permute-done((bf16[2,192,768]{2,1,0:T(8,128)(2,1)}, bf16[2,192,768]{2,1,0:T(8,128)(2,1)}, u32[]{:S(2)}, u32[]{:S(2)}) %collective-permute-start.34) | collective-permute-done | bytes 589856 | tf_op jit(solution)/shard_map/ppermute | solution.py:103
  504.8 2.2 copy.229
  508.4 2.2 fusion.223
  518.8 3.5 collective-permute-done.35
  524.7 25.2 %all-reduce.9.cloned.1.call-done = bf16[2,192,1536]{2,1,0:T(8,128)(2,1)} async-done(((bf16[2,192,1536]{2,1,0:T(8,128)(2,1)}), bf16[2,192,1536]{2,1,0:T(8,128)(2,1)}) %all-reduce.9.cloned.1.call-update) | async-done | bytes 1179664 | tf_op jit(solution)/shard_map/psum | solution.py:345
  549.8 2.1 select_bitcast_fusion.1
  552.1 3.8 multiply_reduce_fusion.5
  556.4 76.1 %psum.35 = f32[13824]{0:T(1024)S(1)} all-reduce(f32[13824]{0:T(1024)S(1)} %pad_maximum_fusion.51), channel_id=1, replica_groups=mesh['dp'=4,'row'=2,'pair'=2,'core'=2] {'dp','row','pair'}, use_global_device_ids=true, to_apply=%region_42.43 | all-reduce | flops 13824 | bytes 110592 | tf_op jit(solution)/shard_map/psum | solution.py:403
  633.7 3.0 add_bitcast_fusion
  661.3 2.2 copy.267
  665.0 3.4 copy.250
  668.4 3.1 reshape.704
  (849 shorter events, 270.0 us)
Async XLA Ops:
  7.2 380.6 %all-reduce.5.cloned.1.call-start = ((), (), s32[]{:S(2)}) async-start(), calls=%async_computation | async-start | bytes 2359296 | tf_op jit(solution)/shard_map/psum | solution.py:345
  9.1 32.2 %collective-permute-start = (bf16[192,512]{1,0:T(8,128)(2,1)}, bf16[192,512]{1,0:T(8,128)(2,1)}, u32[]{:S(2)}, u32[]{:S(2)}) collective-permute-start(bf16[192,512]{1,0:T(8,128)(2,1)} %get-tuple-element.132), channel_id=1, source_target_pairs={{0,2},{2,0},{1,3},{3,1},{4,6},{6,4},{5,7},{7,5},{8,10},{10,8},{9,1... | collective-permute-start | bytes 589832 | tf_op jit(solution)/shard_map/ppermute | solution.py:103
  13.9 93.9 %collective-permute-start.27 = (bf16[192,512]{1,0:T(8,128)(2,1)}, bf16[192,512]{1,0:T(8,128)(2,1)}, u32[]{:S(2)}, u32[]{:S(2)}) collective-permute-start(bf16[192,512]{1,0:T(8,128)(2,1)} %get-tuple-element.130), channel_id=1, source_target_pairs={{0,2},{2,0},{1,3},{3,1},{4,6},{6,4},{5,7},{7,5},{8,10},{10,8},{9,1... | collective-permute-start | bytes 589832 | tf_op jit(solution)/shard_map/ppermute | solution.py:103
  16.5 92.4 %collective-permute-start.14 = (bf16[192,768]{0,1:T(8,128)(2,1)}, bf16[192,768]{0,1:T(8,128)(2,1)}, u32[]{:S(2)}, u32[]{:S(2)}) collective-permute-start(bf16[192,768]{0,1:T(8,128)(2,1)} %select_bitcast_fusion.8), channel_id=1, source_target_pairs={{0,1},{1,0},{2,3},{3,2},{4,5},{5,4},{6,7},{7,6},{8,9},{9,8},{10,11... | collective-permute-start | bytes 884744 | tf_op jit(solution)/shard_map/ppermute | solution.py:103
  18.9 24.5 %collective-permute-start.2 = (bf16[192,768]{0,1:T(8,128)(2,1)}, bf16[192,768]{0,1:T(8,128)(2,1)}, u32[]{:S(2)}, u32[]{:S(2)}) collective-permute-start(bf16[192,768]{0,1:T(8,128)(2,1)} %select_bitcast_fusion.9), channel_id=1, source_target_pairs={{0,1},{1,0},{2,3},{3,2},{4,5},{5,4},{6,7},{7,6},{8,9},{9,8},{10,11... | collective-permute-start | bytes 884744 | tf_op jit(solution)/shard_map/ppermute | solution.py:103
  23.5 28.4 %collective-permute-start.8 = (bf16[192,1536]{1,0:T(8,128)(2,1)}, bf16[192,1536]{1,0:T(8,128)(2,1)}, u32[]{:S(2)}, u32[]{:S(2)}) collective-permute-start(bf16[192,1536]{1,0:T(8,128)(2,1)} %select_bitcast_fusion.3), channel_id=1, source_target_pairs={{0,1},{1,0},{2,3},{3,2},{4,5},{5,4},{6,7},{7,6},{8,9},{9,8},{10,11... | collective-permute-start | bytes 1769480 | tf_op jit(solution)/shard_map/ppermute | solution.py:103
  40.6 94.0 %copy-start.131 = (f32[768]{0:T(1024)}, f32[768]{0:T(1024)S(1)}, u32[]{:S(2)}) copy-start(f32[768]{0:T(1024)S(1)} %get-tuple-element.50) | copy-start | bytes 9220
  40.6 145.1 %copy-start.133 = (f32[768]{0:T(1024)}, f32[768]{0:T(1024)S(1)}, u32[]{:S(2)}) copy-start(f32[768]{0:T(1024)S(1)} %get-tuple-element.47) | copy-start | bytes 9220
  42.3 4.8 collective-permute-start.1
  45.7 16.5 %collective-permute-start.4 = (bf16[384,768]{0,1:T(8,128)(2,1)}, bf16[384,768]{0,1:T(8,128)(2,1)}, u32[]{:S(2)}, u32[]{:S(2)}) collective-permute-start(bf16[384,768]{0,1:T(8,128)(2,1)} %pad_maximum_fusion.22), channel_id=1, source_target_pairs={{0,4},{4,0},{1,5},{5,1},{2,6},{6,2},{3,7},{7,3},{8,12},{12,8},{9,1... | collective-permute-start | bytes 1769480 | tf_op jit(solution)/shard_map/ppermute | solution.py:103
  47.1 17.6 %collective-permute-start.3 = (bf16[384,768]{0,1:T(8,128)(2,1)}, bf16[384,768]{0,1:T(8,128)(2,1)}, u32[]{:S(2)}, u32[]{:S(2)}) collective-permute-start(bf16[384,768]{0,1:T(8,128)(2,1)} %pad_maximum_fusion.22), channel_id=1, source_target_pairs={{0,2},{2,0},{1,3},{3,1},{4,6},{6,4},{5,7},{7,5},{8,10},{10,8},{9,1... | collective-permute-start | bytes 1769480 | tf_op jit(solution)/shard_map/ppermute | solution.py:103
  51.8 79.9 %copy-start.2 = (f32[768,512]{0,1:T(8,128)}, f32[768,512]{0,1:T(8,128)S(1)}, u32[]{:S(2)}) copy-start(f32[768,512]{0,1:T(8,128)S(1)} %copy.200) | copy-start | bytes 4718596
  54.9 56.6 %collective-permute-start.10 = (bf16[384,1536]{1,0:T(8,128)(2,1)}, bf16[384,1536]{1,0:T(8,128)(2,1)}, u32[]{:S(2)}, u32[]{:S(2)}) collective-permute-start(bf16[384,1536]{1,0:T(8,128)(2,1)} %pad_maximum_fusion.4), channel_id=1, source_target_pairs={{0,4},{4,0},{1,5},{5,1},{2,6},{6,2},{3,7},{7,3},{8,12},{12,8},{9,1... | collective-permute-start | bytes 3538952 | tf_op jit(solution)/shard_map/ppermute | solution.py:103
  63.2 9.6 %collective-permute-start.5 = (bf16[192,768]{0,1:T(8,128)(2,1)S(1)}, bf16[192,768]{0,1:T(8,128)(2,1)S(1)}, u32[]{:S(2)}, u32[]{:S(2)}) collective-permute-start(bf16[192,768]{0,1:T(8,128)(2,1)S(1)} %slice.679), channel_id=1, source_target_pairs={{0,2},{2,0},{1,3},{3,1},{4,6},{6,4},{5,7},{7,5},{8,10},{10,8},{9,1... | collective-permute-start | bytes 884744 | tf_op jit(solution)/shard_map/ppermute | solution.py:103
  65.9 29.0 %collective-permute-start.6 = (bf16[192,768]{0,1:T(8,128)(2,1)S(1)}, bf16[192,768]{0,1:T(8,128)(2,1)S(1)}, u32[]{:S(2)}, u32[]{:S(2)}) collective-permute-start(bf16[192,768]{0,1:T(8,128)(2,1)S(1)} %slice.680), channel_id=1, source_target_pairs={{0,4},{4,0},{1,5},{5,1},{2,6},{6,2},{3,7},{7,3},{8,12},{12,8},{9,1... | collective-permute-start | bytes 884744 | tf_op jit(solution)/shard_map/ppermute | solution.py:103
  72.8 41.7 %collective-permute-start.9 = (bf16[384,1536]{1,0:T(8,128)(2,1)}, bf16[384,1536]{1,0:T(8,128)(2,1)}, u32[]{:S(2)}, u32[]{:S(2)}) collective-permute-start(bf16[384,1536]{1,0:T(8,128)(2,1)} %pad_maximum_fusion.4), channel_id=1, source_target_pairs={{0,2},{2,0},{1,3},{3,1},{4,6},{6,4},{5,7},{7,5},{8,10},{10,8},{9,1... | collective-permute-start | bytes 3538952 | tf_op jit(solution)/shard_map/ppermute | solution.py:103
  106.7 25.0 %collective-permute-start.7 = (f32[512,768]{1,0:T(8,128)S(1)}, f32[512,768]{1,0:T(8,128)}, u32[]{:S(2)}, u32[]{:S(2)}) collective-permute-start(f32[512,768]{1,0:T(8,128)S(1)} %convolution_add_fusion.11), channel_id=1, source_target_pairs={{0,1},{1,0},{2,3},{3,2},{4,5},{5,4},{6,7},{7,6},{8,9},{9,8},{10,11... | collective-permute-start | bytes 4718600 | tf_op jit(solution)/shard_map/ppermute | solution.py:31
  107.8 32.4 %collective-permute-start.20 = (bf16[192,1536]{1,0:T(8,128)(2,1)}, bf16[192,1536]{1,0:T(8,128)(2,1)S(1)}, u32[]{:S(2)}, u32[]{:S(2)}) collective-permute-start(bf16[192,1536]{1,0:T(8,128)(2,1)} %select_bitcast_fusion.2), channel_id=1, source_target_pairs={{0,1},{1,0},{2,3},{3,2},{4,5},{5,4},{6,7},{7,6},{8,9},{9,8},{10,11... | collective-permute-start | bytes 1769480 | tf_op jit(solution)/shard_map/ppermute | solution.py:103
  108.9 34.7 %collective-permute-start.28 = (bf16[2,192,512]{2,1,0:T(8,128)(2,1)S(1)}, bf16[2,192,512]{2,1,0:T(8,128)(2,1)S(1)}, u32[]{:S(2)}, u32[]{:S(2)}) collective-permute-start(bf16[2,192,512]{2,1,0:T(8,128)(2,1)S(1)} %pad_maximum_fusion.38), channel_id=1, source_target_pairs={{0,1},{1,0},{2,3},{3,2},{4,5},{5,4},{6,7},{7,6},{8,9},{9,8},{10,11... | collective-permute-start | bytes 1179656 | tf_op jit(solution)/shard_map/ppermute | solution.py:103
  112.7 15.4 %collective-permute-start.11 = (bf16[192,1536]{1,0:T(8,128)(2,1)S(1)}, bf16[192,1536]{1,0:T(8,128)(2,1)S(1)}, u32[]{:S(2)}, u32[]{:S(2)}) collective-permute-start(bf16[192,1536]{1,0:T(8,128)(2,1)S(1)} %slice.697), channel_id=1, source_target_pairs={{0,2},{2,0},{1,3},{3,1},{4,6},{6,4},{5,7},{7,5},{8,10},{10,8},{9,1... | collective-permute-start | bytes 1769480 | tf_op jit(solution)/shard_map/ppermute | solution.py:103
  115.7 15.9 %collective-permute-start.12 = (bf16[192,1536]{1,0:T(8,128)(2,1)S(1)}, bf16[192,1536]{1,0:T(8,128)(2,1)S(1)}, u32[]{:S(2)}, u32[]{:S(2)}) collective-permute-start(bf16[192,1536]{1,0:T(8,128)(2,1)S(1)} %slice.698), channel_id=1, source_target_pairs={{0,4},{4,0},{1,5},{5,1},{2,6},{6,2},{3,7},{7,3},{8,12},{12,8},{9,1... | collective-permute-start | bytes 1769480 | tf_op jit(solution)/shard_map/ppermute | solution.py:103
  128.1 16.5 %collective-permute-start.16 = (bf16[384,768]{0,1:T(8,128)(2,1)S(1)}, bf16[384,768]{0,1:T(8,128)(2,1)S(1)}, u32[]{:S(2)}, u32[]{:S(2)}) collective-permute-start(bf16[384,768]{0,1:T(8,128)(2,1)S(1)} %pad_maximum_fusion.23), channel_id=1, source_target_pairs={{0,4},{4,0},{1,5},{5,1},{2,6},{6,2},{3,7},{7,3},{8,12},{12,8},{9,1... | collective-permute-start | bytes 1769480 | tf_op jit(solution)/shard_map/ppermute | solution.py:103
  131.7 15.8 %collective-permute-start.15 = (bf16[384,768]{0,1:T(8,128)(2,1)S(1)}, bf16[384,768]{0,1:T(8,128)(2,1)S(1)}, u32[]{:S(2)}, u32[]{:S(2)}) collective-permute-start(bf16[384,768]{0,1:T(8,128)(2,1)S(1)} %pad_maximum_fusion.23), channel_id=1, source_target_pairs={{0,2},{2,0},{1,3},{3,1},{4,6},{6,4},{5,7},{7,5},{8,10},{10,8},{9,1... | collective-permute-start | bytes 1769480 | tf_op jit(solution)/shard_map/ppermute | solution.py:103
  140.2 42.7 %collective-permute-start.13 = (f32[512,768]{1,0:T(8,128)}, f32[512,768]{1,0:T(8,128)}, u32[]{:S(2)}, u32[]{:S(2)}) collective-permute-start(f32[512,768]{1,0:T(8,128)} %convolution_add_fusion.8), channel_id=1, source_target_pairs={{0,1},{1,0},{2,3},{3,2},{4,5},{5,4},{6,7},{7,6},{8,9},{9,8},{10,11... | collective-permute-start | bytes 4718600 | tf_op jit(solution)/shard_map/ppermute | solution.py:31
  141.5 55.2 %collective-permute-start.22 = (bf16[384,1536]{1,0:T(8,128)(2,1)}, bf16[384,1536]{1,0:T(8,128)(2,1)}, u32[]{:S(2)}, u32[]{:S(2)}) collective-permute-start(bf16[384,1536]{1,0:T(8,128)(2,1)} %pad_maximum_fusion.7), channel_id=1, source_target_pairs={{0,4},{4,0},{1,5},{5,1},{2,6},{6,2},{3,7},{7,3},{8,12},{12,8},{9,1... | collective-permute-start | bytes 3538952 | tf_op jit(solution)/shard_map/ppermute | solution.py:103
  143.6 55.4 %collective-permute-start.21 = (bf16[384,1536]{1,0:T(8,128)(2,1)}, bf16[384,1536]{1,0:T(8,128)(2,1)}, u32[]{:S(2)}, u32[]{:S(2)}) collective-permute-start(bf16[384,1536]{1,0:T(8,128)(2,1)} %pad_maximum_fusion.7), channel_id=1, source_target_pairs={{0,2},{2,0},{1,3},{3,1},{4,6},{6,4},{5,7},{7,5},{8,10},{10,8},{9,1... | collective-permute-start | bytes 3538952 | tf_op jit(solution)/shard_map/ppermute | solution.py:103
  145.4 34.9 %collective-permute-start.17 = (bf16[192,768]{0,1:T(8,128)(2,1)}, bf16[192,768]{0,1:T(8,128)(2,1)}, u32[]{:S(2)}, u32[]{:S(2)}) collective-permute-start(bf16[192,768]{0,1:T(8,128)(2,1)} %slice.707), channel_id=1, source_target_pairs={{0,2},{2,0},{1,3},{3,1},{4,6},{6,4},{5,7},{7,5},{8,10},{10,8},{9,1... | collective-permute-start | bytes 884744 | tf_op jit(solution)/shard_map/ppermute | solution.py:103
  148.4 32.0 %collective-permute-start.18 = (bf16[192,768]{0,1:T(8,128)(2,1)}, bf16[192,768]{0,1:T(8,128)(2,1)}, u32[]{:S(2)}, u32[]{:S(2)}) collective-permute-start(bf16[192,768]{0,1:T(8,128)(2,1)} %slice.708), channel_id=1, source_target_pairs={{0,4},{4,0},{1,5},{5,1},{2,6},{6,2},{3,7},{7,3},{8,12},{12,8},{9,1... | collective-permute-start | bytes 884744 | tf_op jit(solution)/shard_map/ppermute | solution.py:103
  151.9 42.5 %copy-start.75 = (bf16[768,192]{0,1:T(8,128)(2,1)}, bf16[768,192]{0,1:T(8,128)(2,1)S(1)}, u32[]{:S(2)}) copy-start(bf16[768,192]{0,1:T(8,128)(2,1)S(1)} %pad_maximum_fusion.40) | copy-start | bytes 884740
  196.0 19.8 %collective-permute-start.19 = (f32[512,768]{1,0:T(8,128)}, f32[512,768]{1,0:T(8,128)}, u32[]{:S(2)}, u32[]{:S(2)}) collective-permute-start(f32[512,768]{1,0:T(8,128)} %convolution_add_fusion.10), channel_id=1, source_target_pairs={{0,1},{1,0},{2,3},{3,2},{4,5},{5,4},{6,7},{7,6},{8,9},{9,8},{10,11... | collective-permute-start | bytes 4718600 | tf_op jit(solution)/shard_map/ppermute | solution.py:31
  197.9 15.8 %collective-permute-start.23 = (bf16[192,1536]{1,0:T(8,128)(2,1)S(1)}, bf16[192,1536]{1,0:T(8,128)(2,1)S(1)}, u32[]{:S(2)}, u32[]{:S(2)}) collective-permute-start(bf16[192,1536]{1,0:T(8,128)(2,1)S(1)} %slice.723), channel_id=1, source_target_pairs={{0,2},{2,0},{1,3},{3,1},{4,6},{6,4},{5,7},{7,5},{8,10},{10,8},{9,1... | collective-permute-start | bytes 1769480 | tf_op jit(solution)/shard_map/ppermute | solution.py:103
  200.2 15.5 %collective-permute-start.24 = (bf16[192,1536]{1,0:T(8,128)(2,1)S(1)}, bf16[192,1536]{1,0:T(8,128)(2,1)S(1)}, u32[]{:S(2)}, u32[]{:S(2)}) collective-permute-start(bf16[192,1536]{1,0:T(8,128)(2,1)S(1)} %slice.724), channel_id=1, source_target_pairs={{0,4},{4,0},{1,5},{5,1},{2,6},{6,2},{3,7},{7,3},{8,12},{12,8},{9,1... | collective-permute-start | bytes 1769480 | tf_op jit(solution)/shard_map/ppermute | solution.py:103
  228.6 27.3 %collective-permute-start.46 = (bf16[2,192,1536]{2,1,0:T(8,128)(2,1)S(1)}, bf16[2,192,1536]{2,1,0:T(8,128)(2,1)S(1)}, u32[]{:S(2)}, u32[]{:S(2)}) collective-permute-start(bf16[2,192,1536]{2,1,0:T(8,128)(2,1)S(1)} %fusion.64), channel_id=1, source_target_pairs={{0,4},{4,0},{1,5},{5,1},{2,6},{6,2},{3,7},{7,3},{8,12},{12,8},{9,1... | collective-permute-start | bytes 3538952 | tf_op jit(solution)/shard_map/ppermute | solution.py:103
  231.4 27.6 %collective-permute-start.48 = (bf16[2,192,1536]{2,1,0:T(8,128)(2,1)S(1)}, bf16[2,192,1536]{2,1,0:T(8,128)(2,1)S(1)}, u32[]{:S(2)}, u32[]{:S(2)}) collective-permute-start(bf16[2,192,1536]{2,1,0:T(8,128)(2,1)S(1)} %pad_maximum_fusion.10), channel_id=1, source_target_pairs={{0,2},{2,0},{1,3},{3,1},{4,6},{6,4},{5,7},{7,5},{8,10},{10,8},{9,1... | collective-permute-start | bytes 3538952 | tf_op jit(solution)/shard_map/ppermute | solution.py:103
  234.9 25.6 %collective-permute-start.29 = (f32[512,768]{1,0:T(8,128)S(1)}, f32[512,768]{1,0:T(8,128)S(1)}, u32[]{:S(2)}, u32[]{:S(2)}) collective-permute-start(f32[512,768]{1,0:T(8,128)S(1)} %convolution_add_fusion.3), channel_id=1, source_target_pairs={{0,1},{1,0},{2,3},{3,2},{4,5},{5,4},{6,7},{7,6},{8,9},{9,8},{10,11... | collective-permute-start | bytes 4718600 | tf_op jit(solution)/shard_map/ppermute | solution.py:31
  235.0 26.9 %collective-permute-start.25 = (f32[512,768]{1,0:T(8,128)S(1)}, f32[512,768]{1,0:T(8,128)S(1)}, u32[]{:S(2)}, u32[]{:S(2)}) collective-permute-start(f32[512,768]{1,0:T(8,128)S(1)} %convolution_add_fusion.5), channel_id=1, source_target_pairs={{0,1},{1,0},{2,3},{3,2},{4,5},{5,4},{6,7},{7,6},{8,9},{9,8},{10,11... | collective-permute-start | bytes 4718600 | tf_op jit(solution)/shard_map/ppermute | solution.py:31
  257.2 70.0 %collective-permute-start.47 = (bf16[192,1536]{1,0:T(8,128)(2,1)}, bf16[192,1536]{1,0:T(8,128)(2,1)}, u32[]{:S(2)}, u32[]{:S(2)}) collective-permute-start(bf16[192,1536]{1,0:T(8,128)(2,1)} %slice_bitcast_fusion.4), channel_id=1, source_target_pairs={{0,2},{2,0},{1,3},{3,1},{4,6},{6,4},{5,7},{7,5},{8,10},{10,8},{9,1... | collective-permute-start | bytes 1769480 | tf_op jit(solution)/shard_map/ppermute | solution.py:103
  260.2 68.5 %collective-permute-start.49 = (bf16[192,1536]{1,0:T(8,128)(2,1)}, bf16[192,1536]{1,0:T(8,128)(2,1)}, u32[]{:S(2)}, u32[]{:S(2)}) collective-permute-start(bf16[192,1536]{1,0:T(8,128)(2,1)} %fusion.71), channel_id=1, source_target_pairs={{0,4},{4,0},{1,5},{5,1},{2,6},{6,2},{3,7},{7,3},{8,12},{12,8},{9,1... | collective-permute-start | bytes 1769480 | tf_op jit(solution)/shard_map/ppermute | solution.py:103
  298.1 33.5 %collective-permute-start.26 = (bf16[192,512]{1,0:T(8,128)(2,1)}, bf16[192,512]{1,0:T(8,128)(2,1)}, u32[]{:S(2)}, u32[]{:S(2)}) collective-permute-start(bf16[192,512]{1,0:T(8,128)(2,1)} %slice_bitcast_fusion.16), channel_id=1, source_target_pairs={{0,2},{2,0},{1,3},{3,1},{4,6},{6,4},{5,7},{7,5},{8,10},{10,8},{9,1... | collective-permute-start | bytes 589832 | tf_op jit(solution)/shard_map/ppermute | solution.py:103
  318.0 24.3 %collective-permute-start.44 = (bf16[2,192,768]{2,1,0:T(8,128)(2,1)}, bf16[2,192,768]{2,1,0:T(8,128)(2,1)}, u32[]{:S(2)}, u32[]{:S(2)}) collective-permute-start(bf16[2,192,768]{2,1,0:T(8,128)(2,1)} %copy.246), channel_id=1, source_target_pairs={{0,2},{2,0},{1,3},{3,1},{4,6},{6,4},{5,7},{7,5},{8,10},{10,8},{9,1... | collective-permute-start | bytes 1769480 | tf_op jit(solution)/shard_map/ppermute | solution.py:103
  325.5 13.0 %collective-permute-start.42 = (bf16[2,192,768]{2,1,0:T(8,128)(2,1)}, bf16[2,192,768]{2,1,0:T(8,128)(2,1)}, u32[]{:S(2)}, u32[]{:S(2)}) collective-permute-start(bf16[2,192,768]{2,1,0:T(8,128)(2,1)} %copy.244), channel_id=1, source_target_pairs={{0,4},{4,0},{1,5},{5,1},{2,6},{6,2},{3,7},{7,3},{8,12},{12,8},{9,1... | collective-permute-start | bytes 1769480 | tf_op jit(solution)/shard_map/ppermute | solution.py:103
  327.3 62.8 %collective-permute-start.30 = (f32[512,768]{1,0:T(8,128)}, f32[512,768]{1,0:T(8,128)}, u32[]{:S(2)}, u32[]{:S(2)}) collective-permute-start(f32[512,768]{1,0:T(8,128)} %convolution_add_fusion.1), channel_id=1, source_target_pairs={{0,1},{1,0},{2,3},{3,2},{4,5},{5,4},{6,7},{7,6},{8,9},{9,8},{10,11... | collective-permute-start | bytes 4718600 | tf_op jit(solution)/shard_map/ppermute | solution.py:31
  331.4 102.1 %all-reduce.7.cloned.1.call-start = ((), (), s32[]{:S(2)}) async-start(), calls=%async_computation.1 | async-start | bytes 1572864 | tf_op jit(solution)/shard_map/psum | solution.py:372
  347.2 8.1 %collective-permute-start.43 = (bf16[192,768]{0,1:T(8,128)(2,1)}, bf16[192,768]{0,1:T(8,128)(2,1)}, u32[]{:S(2)}, u32[]{:S(2)}) collective-permute-start(bf16[192,768]{0,1:T(8,128)(2,1)} %slice_bitcast_fusion.10), channel_id=1, source_target_pairs={{0,2},{2,0},{1,3},{3,1},{4,6},{6,4},{5,7},{7,5},{8,10},{10,8},{9,1... | collective-permute-start | bytes 884744 | tf_op jit(solution)/shard_map/ppermute | solution.py:103
  350.8 8.1 %collective-permute-start.45 = (bf16[192,768]{0,1:T(8,128)(2,1)}, bf16[192,768]{0,1:T(8,128)(2,1)}, u32[]{:S(2)}, u32[]{:S(2)}) collective-permute-start(bf16[192,768]{0,1:T(8,128)(2,1)} %fusion.121), channel_id=1, source_target_pairs={{0,4},{4,0},{1,5},{5,1},{2,6},{6,2},{3,7},{7,3},{8,12},{12,8},{9,1... | collective-permute-start | bytes 884744 | tf_op jit(solution)/shard_map/ppermute | solution.py:103
  389.9 44.9 %collective-permute-start.54 = (bf16[192,1536]{1,0:T(8,128)(2,1)}, bf16[192,1536]{1,0:T(8,128)(2,1)}, u32[]{:S(2)}, u32[]{:S(2)}) collective-permute-start(bf16[192,1536]{1,0:T(8,128)(2,1)} %select_bitcast_fusion), channel_id=1, source_target_pairs={{0,1},{1,0},{2,3},{3,2},{4,5},{5,4},{6,7},{7,6},{8,9},{9,8},{10,11... | collective-permute-start | bytes 1769480 | tf_op jit(solution)/shard_map/ppermute | solution.py:103
  390.0 159.8 %all-reduce.9.cloned.1.call-start = ((), (), s32[]{:S(2)}) async-start(), calls=%async_computation.2 | async-start | bytes 2359296 | tf_op jit(solution)/shard_map/psum | solution.py:345
  416.6 28.6 %collective-permute-start.38 = (bf16[2,192,1536]{2,1,0:T(8,128)(2,1)}, bf16[2,192,1536]{2,1,0:T(8,128)(2,1)}, u32[]{:S(2)}, u32[]{:S(2)}) collective-permute-start(bf16[2,192,1536]{2,1,0:T(8,128)(2,1)} %fusion.68), channel_id=1, source_target_pairs={{0,4},{4,0},{1,5},{5,1},{2,6},{6,2},{3,7},{7,3},{8,12},{12,8},{9,1... | collective-permute-start | bytes 3538952 | tf_op jit(solution)/shard_map/ppermute | solution.py:103
  420.3 29.0 %collective-permute-start.40 = (bf16[2,192,1536]{2,1,0:T(8,128)(2,1)}, bf16[2,192,1536]{2,1,0:T(8,128)(2,1)}, u32[]{:S(2)}, u32[]{:S(2)}) collective-permute-start(bf16[2,192,1536]{2,1,0:T(8,128)(2,1)} %pad_maximum_fusion.8), channel_id=1, source_target_pairs={{0,2},{2,0},{1,3},{3,1},{4,6},{6,4},{5,7},{7,5},{8,10},{10,8},{9,1... | collective-permute-start | bytes 3538952 | tf_op jit(solution)/shard_map/ppermute | solution.py:103
  421.8 31.0 %collective-permute-start.31 = (f32[512,768]{1,0:T(8,128)}, f32[512,768]{1,0:T(8,128)}, u32[]{:S(2)}, u32[]{:S(2)}) collective-permute-start(f32[512,768]{1,0:T(8,128)} %convolution_add_fusion.2), channel_id=1, source_target_pairs={{0,1},{1,0},{2,3},{3,2},{4,5},{5,4},{6,7},{7,6},{8,9},{9,8},{10,11... | collective-permute-start | bytes 4718600 | tf_op jit(solution)/shard_map/ppermute | solution.py:31
  434.8 2.6 collective-permute-start.51
  447.7 42.9 %collective-permute-start.39 = (bf16[192,1536]{1,0:T(8,128)(2,1)}, bf16[192,1536]{1,0:T(8,128)(2,1)}, u32[]{:S(2)}, u32[]{:S(2)}) collective-permute-start(bf16[192,1536]{1,0:T(8,128)(2,1)} %slice_bitcast_fusion.8), channel_id=1, source_target_pairs={{0,2},{2,0},{1,3},{3,1},{4,6},{6,4},{5,7},{7,5},{8,10},{10,8},{9,1... | collective-permute-start | bytes 1769480 | tf_op jit(solution)/shard_map/ppermute | solution.py:103
  451.3 40.8 %collective-permute-start.41 = (bf16[192,1536]{1,0:T(8,128)(2,1)}, bf16[192,1536]{1,0:T(8,128)(2,1)}, u32[]{:S(2)}, u32[]{:S(2)}) collective-permute-start(bf16[192,1536]{1,0:T(8,128)(2,1)} %fusion.75), channel_id=1, source_target_pairs={{0,4},{4,0},{1,5},{5,1},{2,6},{6,2},{3,7},{7,3},{8,12},{12,8},{9,1... | collective-permute-start | bytes 1769480 | tf_op jit(solution)/shard_map/ppermute | solution.py:103
  481.8 26.6 %collective-permute-start.36 = (bf16[2,192,768]{2,1,0:T(8,128)(2,1)}, bf16[2,192,768]{2,1,0:T(8,128)(2,1)}, u32[]{:S(2)}, u32[]{:S(2)}) collective-permute-start(bf16[2,192,768]{2,1,0:T(8,128)(2,1)} %copy.232), channel_id=1, source_target_pairs={{0,2},{2,0},{1,3},{3,1},{4,6},{6,4},{5,7},{7,5},{8,10},{10,8},{9,1... | collective-permute-start | bytes 1769480 | tf_op jit(solution)/shard_map/ppermute | solution.py:103
  490.1 14.7 %collective-permute-start.34 = (bf16[2,192,768]{2,1,0:T(8,128)(2,1)}, bf16[2,192,768]{2,1,0:T(8,128)(2,1)}, u32[]{:S(2)}, u32[]{:S(2)}) collective-permute-start(bf16[2,192,768]{2,1,0:T(8,128)(2,1)} %copy.228), channel_id=1, source_target_pairs={{0,4},{4,0},{1,5},{5,1},{2,6},{6,2},{3,7},{7,3},{8,12},{12,8},{9,1... | collective-permute-start | bytes 1769480 | tf_op jit(solution)/shard_map/ppermute | solution.py:103
  490.6 61.4 %collective-permute-start.32 = (f32[512,768]{1,0:T(8,128)}, f32[512,768]{1,0:T(8,128)}, u32[]{:S(2)}, u32[]{:S(2)}) collective-permute-start(f32[512,768]{1,0:T(8,128)} %convolution_add_fusion), channel_id=1, source_target_pairs={{0,1},{1,0},{2,3},{3,2},{4,5},{5,4},{6,7},{7,6},{8,9},{9,8},{10,11... | collective-permute-start | bytes 4718600 | tf_op jit(solution)/shard_map/ppermute | solution.py:31
  494.7 161.1 %all-reduce.11.cloned.1.call-start = ((), (), s32[]{:S(2)}) async-start(), calls=%async_computation.3 | async-start | bytes 1572864 | tf_op jit(solution)/shard_map/psum | solution.py:372
  512.5 9.7 %collective-permute-start.35 = (bf16[192,768]{0,1:T(8,128)(2,1)}, bf16[192,768]{0,1:T(8,128)(2,1)}, u32[]{:S(2)}, u32[]{:S(2)}) collective-permute-start(bf16[192,768]{0,1:T(8,128)(2,1)} %slice_bitcast_fusion.12), channel_id=1, source_target_pairs={{0,2},{2,0},{1,3},{3,1},{4,6},{6,4},{5,7},{7,5},{8,10},{10,8},{9,1... | collective-permute-start | bytes 884744 | tf_op jit(solution)/shard_map/ppermute | solution.py:103
  514.2 9.2 %collective-permute-start.37 = (bf16[192,768]{0,1:T(8,128)(2,1)}, bf16[192,768]{0,1:T(8,128)(2,1)S(1)}, u32[]{:S(2)}, u32[]{:S(2)}) collective-permute-start(bf16[192,768]{0,1:T(8,128)(2,1)} %fusion.125), channel_id=1, source_target_pairs={{0,4},{4,0},{1,5},{5,1},{2,6},{6,2},{3,7},{7,3},{8,12},{12,8},{9,1... | collective-permute-start | bytes 884744 | tf_op jit(solution)/shard_map/ppermute | solution.py:103
  552.0 98.3 %collective-permute-start.53 = (bf16[192,1536]{1,0:T(8,128)(2,1)}, bf16[192,1536]{1,0:T(8,128)(2,1)}, u32[]{:S(2)}, u32[]{:S(2)}) collective-permute-start(bf16[192,1536]{1,0:T(8,128)(2,1)} %select_bitcast_fusion.1), channel_id=1, source_target_pairs={{0,1},{1,0},{2,3},{3,2},{4,5},{5,4},{6,7},{7,6},{8,9},{9,8},{10,11... | collective-permute-start | bytes 1769480 | tf_op jit(solution)/shard_map/ppermute | solution.py:103
  552.1 81.6 %copy-start.22 = (f32[512,768]{1,0:T(8,128)S(1)}, f32[512,768]{1,0:T(8,128)}, u32[]{:S(2)}) copy-start(f32[512,768]{1,0:T(8,128)} %get-tuple-element.63) | copy-start | bytes 4718596
  638.8 4.6 collective-permute-start.52
  643.4 14.0 %collective-permute-start.33 = (f32[192,512]{1,0:T(8,128)S(1)}, f32[192,512]{1,0:T(8,128)}, u32[]{:S(2)}, u32[]{:S(2)}) collective-permute-start(f32[192,512]{1,0:T(8,128)S(1)} %slice_bitcast_fusion.14), channel_id=1, source_target_pairs={{0,2},{2,0},{1,3},{3,1},{4,6},{6,4},{5,7},{7,5},{8,10},{10,8},{9,1... | collective-permute-start | bytes 1179656 | tf_op jit(solution)/shard_map/ppermute | solution.py:103
  656.9 2.5 collective-permute-start.50
  (203 other events, 1078.5 us)
Sparse Core Ops, SparseCore 0:
  331.5 56.2 all-reduce.4
  390.2 43.2 all-reduce.6
  494.8 55.0 all-reduce.8
  552.6 44.0 all-reduce.10

commit v3 on v1

--- a/solution.py
+++ b/solution.py
@@ -99,10 +99,21 @@
     return query_grad, key_grad, value_grad
 
 
+def swap(value, axis):
+    return lax.ppermute(value, axis, [(0, 1), (1, 0)])
+
+
+def in_order(name, mine, other, axis):
+    first = lax.axis_index(name) == 0
+    return jnp.concatenate([jnp.where(first, mine, other), jnp.where(first, other, mine)], axis)
+
+
 def share_weights(parts):
     joined = jnp.concatenate(parts, axis=-1)
-    mine = lax.all_to_all(joined, "core", split_axis=2, concat_axis=1, tiled=True)
-    return mine[:, :, 0]
+    first = lax.axis_index("core") == 0
+    kept = jnp.where(first, joined[:, 0], joined[:, 1])
+    given = jnp.where(first, joined[:, 1], joined[:, 0])
+    return in_order("core", kept, swap(given, "core"), 0)
 
 
 def gather_plane(piece):
@@ -115,14 +126,56 @@
     pairs = lax.axis_size("pair")
     stacked = jnp.stack(grads).astype(jnp.bfloat16)
     stacked = stacked.reshape(len(grads) * pairs, -1, stacked.shape[-1])
-    return lax.psum_scatter(stacked, PLANE, scatter_dimension=0, tiled=False)
+    return lax.optimization_barrier(
+        lax.psum_scatter(stacked, PLANE, scatter_dimension=0, tiled=False)
+    )
+
+
+def partners(step):
+    size = lax.axis_size("dp")
+    return [(place, place ^ step) for place in range(size)]
+
+
+def group_sum(value):
+    size, place = lax.axis_size("dp"), lax.axis_index("dp")
+    if size & (size - 1):
+        return lax.psum(value, "dp")
+    step = 1
+    while step < size:
+        half = value.shape[0] // 2
+        upper = (place // step) % 2 == 1
+        kept = jnp.where(upper, value[half:], value[:half])
+        given = jnp.where(upper, value[:half], value[half:])
+        came = lax.ppermute(given, "dp", partners(step))
+        value = (kept.astype(jnp.float32) + came.astype(jnp.float32)).astype(jnp.bfloat16)
+        step *= 2
+    while step > 1:
+        step //= 2
+        upper = (place // step) % 2 == 1
+        came = lax.ppermute(value, "dp", partners(step))
+        value = jnp.concatenate([jnp.where(upper, came, value), jnp.where(upper, value, came)])
+    return value
+
+
+def vector_sum(value):
+    value = value + swap(value, "row")
+    value = value + swap(value, "pair")
+    size = lax.axis_size("dp")
+    if size & (size - 1):
+        return lax.psum(value, "dp")
+    step = 1
+    while step < size:
+        value = value + lax.ppermute(value, "dp", partners(step))
+        step *= 2
+    return value
 
 
 def return_weights(piece):
-    depth = piece.shape[0] // 2
-    return lax.all_to_all(
-        piece.reshape(2, depth, 1, piece.shape[-1]), "core", split_axis=0, concat_axis=2, tiled=True
-    )[0].astype(jnp.float32)
+    piece = piece.reshape(2, -1, piece.shape[-1])
+    first = lax.axis_index("core") == 0
+    kept = jnp.where(first, piece[0], piece[1])
+    given = jnp.where(first, piece[1], piece[0])
+    return in_order("core", kept[:, None], swap(given, "core")[:, None], 1).astype(jnp.float32)
 
 
 def shards(
@@ -150,25 +203,24 @@
     width = depth_in * pairs * 2
     length = segments.shape[1]
 
-    attention_part = share_weights(
-        [
-            qkv_weight.reshape(layers, depth_in, 3, 2, half_head)
-            .transpose(0, 1, 3, 2, 4)
-            .reshape(layers, depth_in, 2, 3 * half_head),
-            out_weight.reshape(layers, depth_in, 2, half_head),
-        ]
-    )
-    forward_part = share_weights(
-        [
-            up_weight.reshape(layers, depth_in, 2, half_hidden),
-            down_weight.reshape(layers, depth_in, 2, half_hidden),
-        ]
-    )
     attention_weights = []
     forward_weights = []
     for layer_at in range(layers):
-        attention_weights.append(gather_plane(attention_part[layer_at]))
-        forward_weights.append(gather_plane(forward_part[layer_at]))
+        gathered = gather_plane(
+            share_weights(
+                [
+                    up_weight[layer_at].reshape(depth_in, 2, half_hidden),
+                    down_weight[layer_at].reshape(depth_in, 2, half_hidden),
+                    qkv_weight[layer_at]
+                    .reshape(depth_in, 3, 2, half_head)
+                    .transpose(0, 2, 1, 3)
+                    .reshape(depth_in, 2, 3 * half_head),
+                    out_weight[layer_at].reshape(depth_in, 2, half_head),
+                ]
+            )
+        )
+        forward_weights.append(gathered[..., : 2 * half_hidden])
+        attention_weights.append(gathered[..., 2 * half_hidden :])
 
     small = jnp.concatenate(
         [
@@ -194,11 +246,15 @@
         small[0, :, cuts[2] :], at_row * pairs + at_pair, 0, keepdims=False
     )
 
-    both = jnp.stack([tokens, cotangent])
-    both = lax.all_gather(both, "core", axis=1, tiled=True)
-    both = lax.all_to_all(both, "pair", split_axis=2, concat_axis=1, tiled=True)
-    residual = both[0].astype(jnp.float32).T
-    gradient = both[1].astype(jnp.float32).T
+    def to_chip(value):
+        kept = lax.dynamic_slice_in_dim(value, at_pair * length, length, 1)
+        given = lax.dynamic_slice_in_dim(value, (1 - at_pair) * length, length, 1)
+        mine = in_order("pair", kept[None], swap(given, "pair")[None], 0)
+        whole = in_order("core", mine[:, None], swap(mine, "core")[:, None], 1)
+        return whole.reshape(width, length).astype(jnp.float32).T
+
+    residual = to_chip(tokens)
+    gradient = to_chip(cotangent)
 
     stored = []
     for layer_at in range(layers):
@@ -257,8 +313,11 @@
 
     def to_owner(value):
         blocks = value.T.reshape(pairs, 2, depth_in, length)
-        blocks = lax.dynamic_index_in_dim(blocks, at_core, 1, keepdims=False)
-        return lax.all_to_all(blocks, "pair", split_axis=0, concat_axis=2, tiled=True)[0]
+        blocks = jnp.where(at_core == 0, blocks[:, 0], blocks[:, 1])
+        first = at_pair == 0
+        kept = jnp.where(first, blocks[0], blocks[1])
+        given = jnp.where(first, blocks[1], blocks[0])
+        return in_order("pair", kept, swap(given, "pair"), 1)
 
     activations = to_owner(residual.astype(jnp.bfloat16))
 
@@ -294,7 +353,7 @@
             normed_grad = normed_grad + contract_cols(hidden_grad, wide[row][:, :half_hidden])
             hidden_grads.append(jnp.sum(hidden_grad.astype(jnp.float32), axis=0))
             parts.append(jnp.concatenate([up_grad, down_grad], axis=1))
-        forward_grads[layer_at] = lax.psum(scatter_plane(parts), "dp")
+        forward_grads[layer_at] = scatter_plane(parts)
         back_two, gain_two_grad, shift_two_grad = norm_backward(
             pair_sum(normed_grad), unit_two, inverse_two, gain_two
         )
@@ -320,7 +379,7 @@
                 jnp.concatenate([contract_rows(normed_one, pieces), out_grads[row]], axis=1)
             )
             normed_grad = normed_grad + contract_cols(pieces, mixing[row][:, : 3 * half_head])
-        attention_grads[layer_at] = lax.psum(scatter_plane(parts), "dp")
+        attention_grads[layer_at] = scatter_plane(parts)
         back_one, gain_one_grad, shift_one_grad = norm_backward(
             pair_sum(normed_grad), unit_one, inverse_one, gain_one
         )
@@ -343,15 +402,22 @@
         )
         gradient = middle_grad + back_one
 
+    first_parts = [(attention_grads[layer], forward_grads[layer]) for layer in range(1, layers)]
+    gradient, first_parts = lax.optimization_barrier((gradient, first_parts))
+    for layer_at in range(1, layers):
+        attention_grads[layer_at], forward_grads[layer_at] = first_parts[layer_at - 1]
+    for layer_at in reversed(range(layers)):
+        forward_grads[layer_at] = group_sum(forward_grads[layer_at])
+        attention_grads[layer_at] = group_sum(attention_grads[layer_at])
     input_grad = to_owner(gradient)
     deep, asked, hidden = (
         jnp.stack([vector_parts[layer_at][part] for layer_at in range(layers)]) for part in range(3)
     )
-    sums = lax.psum(
-        jnp.concatenate([deep.reshape(-1), asked.reshape(-1), hidden.reshape(-1)]),
-        ("dp", "row", "pair"),
-    )
-    hidden_sums = lax.all_gather(sums[deep.size :], "core", axis=0, tiled=False)
+    sums = vector_sum(
+        jnp.concatenate([deep.reshape(-1), asked.reshape(-1), hidden.reshape(-1)])
+    )
+    ours = sums[deep.size :]
+    hidden_sums = in_order("core", ours[None], swap(ours, "core")[None], 0)
     deep_sums = lax.dynamic_slice_in_dim(
         sums[: deep.size].reshape(layers, 6, width), (at_pair * 2 + at_core) * depth_in, depth_in, 2
     )

time: 671 us -> 618 us (0.921)
  blocking collectives: 115 us -> 12.8 us
  waiting for transfers between devices: 277 us -> 238 us
  local copies, waits for them, and re-layouts: 101 us -> 137 us
  other arithmetic: 57.5 us -> 92.5 us
  starting transfers between devices: 22 us -> 33.8 us
    ppermute x0 -> x33, waiting for transfers between devices: none -> 138 us  [the longest x8 57.6 us: group_sum(): came = lax.ppermute(given, 'dp', partners(step))]
    unnamed x14 -> x10, waiting for transfers between devices: 116 us -> 0.47 us
    psum x1 -> x0, blocking collectives: 81 us -> none  [shards(): lax.psum(jnp.concatenate([deep.reshape(-1), asked.reshape(-1), hidden.res...]
    all_to_all x5 -> x0, waiting for transfers between devices: 33.4 us -> none  [the longest x1 25.5 us: shards(): both = lax.all_to_all(both, 'pair', split_axis=2, concat_axis=1, tiled=True)]
    ppermute x0 -> x33, starting transfers between devices: none -> 30.6 us  [the longest x8 12.4 us: group_sum(): came = lax.ppermute(given, 'dp', partners(step))]
    psum x1 -> x0, waiting for transfers between devices: 24 us -> none  [shards(): attention_grads[layer_at] = lax.psum(scatter_plane(parts), 'dp')]
    select_n x0 -> x29, other arithmetic: none -> 23.8 us  [the longest x1 10.6 us: share_weights(): kept = jnp.where(first, joined[:, 0], joined[:, 1])]
    all_to_all x4 -> x0, blocking collectives: 20.3 us -> none  [the longest x2 10.3 us: share_weights(): lax.all_to_all(joined, 'core', split_axis=2, concat_axis=1, tiled=True)]
  transfers between devices with their start and end apart: 23 -> 47, of which waited for: 13 -> 23; matrix products, arithmetic and copies ran while one was open for 25% -> 31% of each run, Pallas kernels for 0% -> 0%
where the time goes in v3:
time: 618 us; the launch traced here: 607 us
  waiting for transfers between devices  238 us (39%)
  local copies, waits for them, and re-layouts  137 us (22%)
  other arithmetic  92.5 us (15%)
  matrix products  74.8 us (12%)
  starting transfers between devices  33.8 us (5%)
  between operations  17.6 us (3%)
  blocking collectives  12.8 us (2%)
    all_gather x2, waiting for transfers between devices, gather_plane(): everything = lax.all_gather(piece, PLANE, axis=0, tiled=False)  96.5 us
    ppermute x8, waiting for transfers between devices, group_sum(): came = lax.ppermute(given, 'dp', partners(step))  57.6 us
    ppermute x8, waiting for transfers between devices, group_sum(): came = lax.ppermute(value, 'dp', partners(step))  57.4 us
    unnamed x362, local copies, waits for them, and re-layouts  32.7 us
    another operation x4, local copies, waits for them, and re-layouts, scatter_plane(): stacked = jnp.stack(grads).astype(jnp.bfloat16)  22.3 us
    dot_general x16, matrix products, plain(): return jnp.dot(left_side, right_side, preferred_element_type=jnp.float32)  21.4 us
    ppermute x15, waiting for transfers between devices, swap(): return lax.ppermute(value, axis, [(0, 1), (1, 0)])  20.7 us
    dot_general x16, matrix products, contract_cols(): lax.dot_general(left_side, right_side, (((1,), (1,)), ((), ())), preferre...  19.4 us
  transfers between devices with their start and end apart: 47, of which 23 were waited for; matrix products, arithmetic and copies ran while one was open for 31% of the time, Pallas kernels for 0%

profile of v3, /device:TPU:0, one launch (start us, length us, event | category | flops | bytes accessed | tf_op | source)
XLA Modules:
  0.0 606.5 jit_solution(678733149835364082)
XLA Ops:
  17.6 9.0 %concatenate.201 = bf16[192,2,2304]{2,1,0:T(2,128)(2,1)S(1)} concatenate(bf16[192,2,768]{2,1,0:T(2,128)(2,1)S(1)} %reshape_squeeze.61, bf16[192,2,768]{2,1,0:T(2,128)(2,1)} %reshape_squeeze.62, bf16[192,2,576]{2,1,0:T(2,128)(2,1)} %copy.214, bf16[192,2,192]{2,1,0:T(2,128)(2,1)S(1)} %reshape_squeeze.64), dimensions={2} | concatenate | bytes 3538944 | tf_op jit(solution)/shard_map/concatenate | solution.py:112
  26.7 9.6 %concatenate.196 = bf16[192,2,2304]{2,1,0:T(2,128)(2,1)} concatenate(bf16[192,2,768]{2,1,0:T(2,128)(2,1)S(1)} %reshape_squeeze.52, bf16[192,2,768]{2,1,0:T(2,128)(2,1)} %reshape_squeeze.53, bf16[192,2,576]{2,1,0:T(2,128)(2,1)} %copy.211, bf16[192,2,192]{2,1,0:T(2,128)(2,1)S(1)} %reshape_squeeze.55), dimensions={2} | concatenate | bytes 3538944 | tf_op jit(solution)/shard_map/concatenate | solution.py:112
  36.3 10.6 %broadcast_select_fusion.1 = (bf16[192,1,2304]{2,1,0:T(2,128)(2,1)}, bf16[192,1,2304]{2,1,0:T(2,128)(2,1)}, bf16[192,1,2304]{2,1,0:T(2,128)(2,1)S(1)}, bf16[192,1,2304]{2,1,0:T(2,128)(2,1)S(1)}) fusion(pred[]{:T(512)S(6)} %eq.37, bf16[192,2,2304]{2,1,0:T(2,128)(2,1)S(1)} %concatenate.201, bf16[192,2,2304]{2,1,0:T(2,128)(2,1)} %concatenate.196), kind=kLoop, calls=%fused_computation.19 | loop fusion | flops 1769472 | bytes 7077889 | tf_op jit(solution)/shard_map/jit(_where)/select_n | solution.py:114
  47.5 2.1 collective-permute-done.2
  52.2 3.0 collective-permute-start.9
  55.3 2.6 copy.277
  58.2 12.8 %all-gather.3 = bf16[8,1,7424]{2,1,0:T(2,128)(2,1)S(1)} all-gather(bf16[1,1,7424]{2,1,0:T(2,128)(2,1)S(1)} %reshape.642), channel_id=2, replica_groups=mesh['dp'=4,'row'=2,'pair'=2,'core'=2] {'row','pair','core'}, dimensions={0}, use_global_device_ids=true | all-gather | bytes 133632 | tf_op jit(solution)/shard_map/all_gather | solution.py:235
  85.9 45.9 %all-gather.7.cloned.1.call-done = bf16[1536,2304]{1,0:T(8,128)(2,1)} async-done(((bf16[384,2304]{1,0:T(8,128)(2,1)}), bf16[1536,2304]{1,0:T(8,128)(2,1)}) %all-gather.7.cloned.1.call-update) | async-done | bytes 7077904 | tf_op jit(solution)/shard_map/all_gather | solution.py:120
  146.8 2.7 slice_bitcast_fusion.4
  149.6 4.0 fusion.146
  156.8 2.6 convolution_add_fusion.7
  159.8 50.6 %all-gather.9.cloned.1.call-done = bf16[1536,2304]{1,0:T(8,128)(2,1)} async-done(((bf16[384,2304]{1,0:T(8,128)(2,1)}), bf16[1536,2304]{1,0:T(8,128)(2,1)}) %all-gather.9.cloned.1.call-update) | async-done | bytes 7077904 | tf_op jit(solution)/shard_map/all_gather | solution.py:120
  212.2 3.1 fusion.145
  220.5 2.3 copy-done.1
  225.9 3.3 collective-permute-done.10
  232.1 2.3 convert_reduce_fusion.1
  235.2 2.4 convert_reduce_fusion.2
  238.5 2.0 convolution_add_fusion.3
  241.8 2.3 convolution_add_fusion.4
  244.5 2.3 copy.218
  247.6 4.0 multiply_reduce_fusion.2
  251.6 4.9 convert_reduce_fusion.5
  261.8 2.4 convert_reduce_fusion.8
  268.0 2.1 fusion.47
  276.7 4.3 copy.225
  281.1 2.3 convolution_convert_fusion.5
  286.2 2.0 convolution_add_fusion.2
  291.8 2.6 pad_maximum_fusion
  294.4 6.7 %copy.226 = bf16[2,768,1536]{2,1,0:T(8,128)(2,1)} copy(bf16[2,768,1536]{1,2,0:T(8,128)(2,1)} %pad_maximum_fusion) | data formatting | bytes 9437184 | tf_op jit(solution)/shard_map/stack | solution.py:127
  301.8 4.0 multiply_reduce_fusion.3
  307.9 2.2 convert_reduce_fusion.4
  312.0 2.2 convert_reduce_fusion.3
  315.6 3.0 collective-permute-done.13
  320.1 2.3 convert_reduce_fusion.7
  338.3 4.3 copy.228
  342.7 2.3 convolution_convert_fusion.1
  352.7 2.0 convolution_add_fusion
  355.4 2.6 pad_maximum_fusion.1
  358.0 7.0 %copy.233 = bf16[2,768,1536]{2,1,0:T(8,128)(2,1)} copy(bf16[2,768,1536]{1,2,0:T(8,128)(2,1)} %pad_maximum_fusion.1) | data formatting | bytes 9437184 | tf_op jit(solution)/shard_map/stack | solution.py:127
  370.7 9.6 %collective-permute-done.8 = bf16[192,512]{1,0:T(8,128)(2,1)S(1)} collective-permute-done((bf16[192,512]{1,0:T(8,128)(2,1)S(1)}, bf16[192,512]{1,0:T(8,128)(2,1)S(1)}, u32[]{:S(2)}, u32[]{:S(2)}) %collective-permute-start.8) | collective-permute-done | bytes 196640 | tf_op jit(solution)/shard_map/ppermute | solution.py:103
  389.0 4.3 multiply_reduce_fusion.5
  405.1 3.4 collective-permute-done.16
  411.3 2.3 collective-permute-done.17
  415.8 2.6 collective-permute-done.18
  418.4 1.9 collective-permute-start.19
  420.4 3.0 multiply_add_fusion
  438.0 2.9 collective-permute-done.25
  442.0 2.1 collective-permute-start.26
  444.0 18.4 %collective-permute-done.20 = bf16[192,768]{1,0:T(8,128)(2,1)S(1)} collective-permute-done((bf16[192,768]{1,0:T(8,128)(2,1)S(1)}, bf16[192,768]{1,0:T(8,128)(2,1)S(1)}, u32[]{:S(2)}, u32[]{:S(2)}) %collective-permute-start.20) | collective-permute-done | bytes 294944 | tf_op jit(solution)/shard_map/ppermute | solution.py:149
  467.8 8.5 %collective-permute-done.21 = bf16[96,768]{1,0:T(8,128)(2,1)S(1)} collective-permute-done((bf16[96,768]{1,0:T(8,128)(2,1)S(1)}, bf16[96,768]{1,0:T(8,128)(2,1)S(1)}, u32[]{:S(2)}, u32[]{:S(2)}) %collective-permute-start.21) | collective-permute-done | bytes 147488 | tf_op jit(solution)/shard_map/ppermute | solution.py:149
  476.7 3.0 collective-permute-start.37
  479.7 8.6 %collective-permute-done.27 = bf16[96,768]{1,0:T(8,128)(2,1)S(1)} collective-permute-done((bf16[96,768]{1,0:T(8,128)(2,1)S(1)}, bf16[96,768]{1,0:T(8,128)(2,1)S(1)}, u32[]{:S(2)}, u32[]{:S(2)}) %collective-permute-start.27) | collective-permute-done | bytes 147488 | tf_op jit(solution)/shard_map/ppermute | solution.py:155
  488.5 3.1 collective-permute-done.22
  495.1 2.6 collective-permute-done.37
  497.9 12.4 %collective-permute-done.28 = bf16[192,768]{1,0:T(8,128)(2,1)S(1)} collective-permute-done((bf16[192,768]{1,0:T(8,128)(2,1)S(1)}, bf16[192,768]{1,0:T(8,128)(2,1)S(1)}, u32[]{:S(2)}, u32[]{:S(2)}) %collective-permute-start.28) | collective-permute-done | bytes 294944 | tf_op jit(solution)/shard_map/ppermute | solution.py:155
  510.5 6.1 %collective-permute-done.23 = bf16[192,768]{1,0:T(8,128)(2,1)S(1)} collective-permute-done((bf16[192,768]{1,0:T(8,128)(2,1)S(1)}, bf16[192,768]{1,0:T(8,128)(2,1)S(1)}, u32[]{:S(2)}, u32[]{:S(2)}) %collective-permute-start.23) | collective-permute-done | bytes 294944 | tf_op jit(solution)/shard_map/ppermute | solution.py:155
  516.9 12.3 %collective-permute-done.31 = bf16[192,1536]{1,0:T(8,128)(2,1)S(1)} collective-permute-done((bf16[192,1536]{1,0:T(8,128)(2,1)S(1)}, bf16[192,1536]{1,0:T(8,128)(2,1)S(1)}, u32[]{:S(2)}, u32[]{:S(2)}) %collective-permute-start.31) | collective-permute-done | bytes 589856 | tf_op jit(solution)/shard_map/ppermute | solution.py:149
  529.9 2.5 collective-permute-start.39
  532.5 12.9 %collective-permute-done.32 = bf16[96,1536]{1,0:T(8,128)(2,1)S(1)} collective-permute-done((bf16[96,1536]{1,0:T(8,128)(2,1)S(1)}, bf16[96,1536]{1,0:T(8,128)(2,1)S(1)}, u32[]{:S(2)}, u32[]{:S(2)}) %collective-permute-start.32) | collective-permute-done | bytes 294944 | tf_op jit(solution)/shard_map/ppermute | solution.py:149
  545.7 16.0 %collective-permute-done.33 = bf16[96,1536]{1,0:T(8,128)(2,1)S(1)} collective-permute-done((bf16[96,1536]{1,0:T(8,128)(2,1)S(1)}, bf16[96,1536]{1,0:T(8,128)(2,1)S(1)}, u32[]{:S(2)}, u32[]{:S(2)}) %collective-permute-start.33) | collective-permute-done | bytes 294944 | tf_op jit(solution)/shard_map/ppermute | solution.py:155
  565.1 11.1 %collective-permute-done.34 = bf16[192,1536]{1,0:T(8,128)(2,1)S(1)} collective-permute-done((bf16[192,1536]{1,0:T(8,128)(2,1)S(1)}, bf16[192,1536]{1,0:T(8,128)(2,1)S(1)}, u32[]{:S(2)}, u32[]{:S(2)}) %collective-permute-start.34) | collective-permute-done | bytes 589856 | tf_op jit(solution)/shard_map/ppermute | solution.py:155
  581.7 1.9 copy.229
  583.6 4.4 copy.230
  588.0 4.4 reshape.623
  (691 shorter events, 189.9 us)
Async XLA Ops:
  7.2 124.6 %all-gather.7.cloned.1.call-start = ((), (), s32[]{:S(2)}) async-start(), calls=%async_computation.4 | async-start | bytes 8847360 | tf_op jit(solution)/shard_map/all_gather | solution.py:120
  47.0 2.6 collective-permute-start.2
  51.1 159.3 %all-gather.9.cloned.1.call-start = ((), (), s32[]{:S(2)}) async-start(), calls=%async_computation.5 | async-start | bytes 8847360 | tf_op jit(solution)/shard_map/all_gather | solution.py:120
  52.2 25.7 %collective-permute-start.9 = (bf16[192,512]{1,0:T(8,128)(2,1)S(1)}, bf16[192,512]{1,0:T(8,128)(2,1)}, u32[]{:S(2)}, u32[]{:S(2)}) collective-permute-start(bf16[192,512]{1,0:T(8,128)(2,1)S(1)} %constant_dynamic-slice_fusion.8), channel_id=1, source_target_pairs={{0,2},{2,0},{1,3},{3,1},{4,6},{6,4},{5,7},{7,5},{8,10},{10,8},{9,1... | collective-permute-start | bytes 589832 | tf_op jit(solution)/shard_map/ppermute | solution.py:103
  55.1 22.7 %collective-permute-start = (bf16[192,512]{1,0:T(8,128)(2,1)S(1)}, bf16[192,512]{1,0:T(8,128)(2,1)}, u32[]{:S(2)}, u32[]{:S(2)}) collective-permute-start(bf16[192,512]{1,0:T(8,128)(2,1)S(1)} %constant_dynamic-slice_fusion.12), channel_id=1, source_target_pairs={{0,2},{2,0},{1,3},{3,1},{4,6},{6,4},{5,7},{7,5},{8,10},{10,8},{9,1... | collective-permute-start | bytes 589832 | tf_op jit(solution)/shard_map/ppermute | solution.py:103
  55.3 18.2 %copy-start.14 = (bf16[192,1,2304]{2,1,0:T(2,128)(2,1)S(1)}, bf16[192,1,2304]{2,1,0:T(2,128)(2,1)}, u32[]{:S(2)}) copy-start(bf16[192,1,2304]{2,1,0:T(2,128)(2,1)} %get-tuple-element.104) | copy-start | bytes 2654212
  57.9 14.1 %collective-permute-start.5 = (bf16[192,2304]{1,0:T(8,128)(2,1)}, bf16[192,2304]{1,0:T(8,128)(2,1)S(1)}, u32[]{:S(2)}, u32[]{:S(2)}) collective-permute-start(bf16[192,2304]{1,0:T(8,128)(2,1)} %bitcast.331), channel_id=1, source_target_pairs={{0,1},{1,0},{2,3},{3,2},{4,5},{5,4},{6,7},{7,6},{8,9},{9,8},{10,11... | collective-permute-start | bytes 2654216 | tf_op jit(solution)/shard_map/ppermute | solution.py:103
  76.1 328.9 %reduce-scatter.13.cloned.1.call-start = ((), (), s32[]{:S(2)}) async-start(), calls=%async_computation.6 | async-start | bytes 2949120
  79.8 3.0 collective-permute-start.1
  81.9 71.6 %copy-start.94 = (f32[768]{0:T(1024)}, f32[768]{0:T(1024)S(1)}, u32[]{:S(2)}) copy-start(f32[768]{0:T(1024)S(1)} %get-tuple-element.50) | copy-start | bytes 9220
  81.9 133.4 %copy-start.96 = (f32[768]{0:T(1024)}, f32[768]{0:T(1024)S(1)}, u32[]{:S(2)}) copy-start(f32[768]{0:T(1024)S(1)} %get-tuple-element.47) | copy-start | bytes 9220
  85.5 48.1 %copy-start.105 = (f32[512]{0:T(512)}, f32[512]{0:T(512)S(1)}, u32[]{:S(2)}) copy-start(f32[512]{0:T(512)S(1)} %get-tuple-element.181) | copy-start | bytes 6148
  85.5 48.1 %copy-start.106 = (f32[512]{0:T(512)}, f32[512]{0:T(512)S(1)}, u32[]{:S(2)}) copy-start(f32[512]{0:T(512)S(1)} %get-tuple-element.182) | copy-start | bytes 6148
  85.9 48.5 %copy-start.73 = (bf16[512,768]{1,0:T(8,128)(2,1)}, bf16[512,768]{1,0:T(8,128)(2,1)S(1)}, u32[]{:S(2)}) copy-start(bf16[512,768]{1,0:T(8,128)(2,1)S(1)} %add_convert_fusion.4) | copy-start | bytes 2359300
  142.2 7.3 %collective-permute-start.3 = (f32[512,768]{1,0:T(8,128)S(1)}, f32[512,768]{1,0:T(8,128)}, u32[]{:S(2)}, u32[]{:S(2)}) collective-permute-start(f32[512,768]{1,0:T(8,128)S(1)} %convolution_add_fusion.11), channel_id=1, source_target_pairs={{0,1},{1,0},{2,3},{3,2},{4,5},{5,4},{6,7},{7,6},{8,9},{9,8},{10,11... | collective-permute-start | bytes 4718600 | tf_op jit(solution)/shard_map/ppermute | solution.py:31
  159.4 52.8 %collective-permute-start.4 = (f32[512,768]{1,0:T(8,128)}, f32[512,768]{1,0:T(8,128)}, u32[]{:S(2)}, u32[]{:S(2)}) collective-permute-start(f32[512,768]{1,0:T(8,128)} %convolution_add_fusion.7), channel_id=1, source_target_pairs={{0,1},{1,0},{2,3},{3,2},{4,5},{5,4},{6,7},{7,6},{8,9},{9,8},{10,11... | collective-permute-start | bytes 4718600 | tf_op jit(solution)/shard_map/ppermute | solution.py:31
  212.2 11.9 %copy-start.31 = (bf16[768,768]{1,0:T(8,128)(2,1)}, bf16[768,768]{1,0:T(8,128)(2,1)S(1)}, u32[]{:S(2)}) copy-start(bf16[768,768]{1,0:T(8,128)(2,1)S(1)} %get-tuple-element.89) | copy-start | bytes 3538948
  212.2 12.5 %copy-start.10 = (bf16[768,768]{1,0:T(8,128)(2,1)}, bf16[768,768]{1,0:T(8,128)(2,1)S(1)}, u32[]{:S(2)}) copy-start(bf16[768,768]{1,0:T(8,128)(2,1)S(1)} %get-tuple-element.88) | copy-start | bytes 3538948
  215.3 14.6 %copy-start.2 = (f32[512,768]{1,0:T(8,128)}, f32[512,768]{1,0:T(8,128)S(1)}, u32[]{:S(2)}) copy-start(f32[512,768]{1,0:T(8,128)S(1)} %get-tuple-element.84) | copy-start | bytes 4718596
  225.2 4.7 collective-permute-start.6
  225.7 3.6 collective-permute-start.10
  240.6 7.0 %collective-permute-start.11 = (f32[512,768]{1,0:T(8,128)}, f32[512,768]{1,0:T(8,128)}, u32[]{:S(2)}, u32[]{:S(2)}) collective-permute-start(f32[512,768]{1,0:T(8,128)} %convolution_add_fusion.3), channel_id=1, source_target_pairs={{0,1},{1,0},{2,3},{3,2},{4,5},{5,4},{6,7},{7,6},{8,9},{9,8},{10,11... | collective-permute-start | bytes 4718600 | tf_op jit(solution)/shard_map/ppermute | solution.py:31
  244.1 7.5 %collective-permute-start.7 = (f32[512,768]{1,0:T(8,128)}, f32[512,768]{1,0:T(8,128)}, u32[]{:S(2)}, u32[]{:S(2)}) collective-permute-start(f32[512,768]{1,0:T(8,128)} %convolution_add_fusion.4), channel_id=1, source_target_pairs={{0,1},{1,0},{2,3},{3,2},{4,5},{5,4},{6,7},{7,6},{8,9},{9,8},{10,11... | collective-permute-start | bytes 4718600 | tf_op jit(solution)/shard_map/ppermute | solution.py:31
  247.6 14.2 %slice-start.2 = ((s8[6291456]{0:T(1024)(128)(4,1)}), s8[4194304]{0:T(1024)(128)(4,1)S(1)}, s32[]{:S(2)}) async-start(s8[6291456]{0:T(1024)(128)(4,1)} %bitcast.344), calls=%async_computation.12 | async-start | bytes 8388608
  281.0 147.9 %reduce-scatter.15.cloned.1.call-start = ((), (), s32[]{:S(2)}) async-start(), calls=%async_computation.7 | async-start | bytes 5898240
  288.2 13.3 %collective-permute-start.12 = (f32[512,768]{1,0:T(8,128)}, f32[512,768]{1,0:T(8,128)}, u32[]{:S(2)}, u32[]{:S(2)}) collective-permute-start(f32[512,768]{1,0:T(8,128)} %convolution_add_fusion.2), channel_id=1, source_target_pairs={{0,1},{1,0},{2,3},{3,2},{4,5},{5,4},{6,7},{7,6},{8,9},{9,8},{10,11... | collective-permute-start | bytes 4718600 | tf_op jit(solution)/shard_map/ppermute | solution.py:31
  301.1 134.3 %reduce-scatter.17.cloned.1.call-start = ((), (), s32[]{:S(2)}) async-start(), calls=%async_computation.8 | async-start | bytes 2949120
  315.1 3.5 collective-permute-start.13
  342.7 149.4 %reduce-scatter.19.cloned.1.call-start = ((), (), s32[]{:S(2)}) async-start(), calls=%async_computation.9 | async-start | bytes 5898240
  354.7 34.4 %collective-permute-start.14 = (f32[512,768]{1,0:T(8,128)}, f32[512,768]{1,0:T(8,128)}, u32[]{:S(2)}, u32[]{:S(2)}) collective-permute-start(f32[512,768]{1,0:T(8,128)} %convolution_add_fusion), channel_id=1, source_target_pairs={{0,1},{1,0},{2,3},{3,2},{4,5},{5,4},{6,7},{7,6},{8,9},{9,8},{10,11... | collective-permute-start | bytes 4718600 | tf_op jit(solution)/shard_map/ppermute | solution.py:31
  367.3 13.0 %copy-start.133 = (f32[768]{0:T(1024)S(1)}, f32[768]{0:T(1024)}, u32[]{:S(2)}) copy-start(f32[768]{0:T(1024)} %get-tuple-element.26) | copy-start | bytes 9220
  367.3 13.0 %copy-start.119 = (f32[768]{0:T(1024)S(1)}, f32[768]{0:T(1024)}, u32[]{:S(2)}) copy-start(f32[768]{0:T(1024)} %get-tuple-element.70) | copy-start | bytes 9220
  367.3 13.6 %copy-start.132 = (f32[768]{0:T(1024)S(1)}, f32[768]{0:T(1024)}, u32[]{:S(2)}) copy-start(f32[768]{0:T(1024)} %get-tuple-element.35) | copy-start | bytes 9220
  368.5 20.5 %copy-start.104 = (f32[768]{0:T(1024)S(1)}, f32[768]{0:T(1024)}, u32[]{:S(2)}) copy-start(f32[768]{0:T(1024)} %copy-done.103) | copy-start | bytes 9220
  368.6 11.8 %collective-permute-start.8 = (bf16[192,512]{1,0:T(8,128)(2,1)S(1)}, bf16[192,512]{1,0:T(8,128)(2,1)S(1)}, u32[]{:S(2)}, u32[]{:S(2)}) collective-permute-start(bf16[192,512]{1,0:T(8,128)(2,1)S(1)} %select_bitcast_fusion.15), channel_id=1, source_target_pairs={{0,2},{2,0},{1,3},{3,1},{4,6},{6,4},{5,7},{7,5},{8,10},{10,8},{9,1... | collective-permute-start | bytes 589832 | tf_op jit(solution)/shard_map/ppermute | solution.py:103
  393.3 27.0 %copy-start.16 = (f32[512,768]{1,0:T(8,128)S(1)}, f32[512,768]{1,0:T(8,128)}, u32[]{:S(2)}) copy-start(f32[512,768]{1,0:T(8,128)} %get-tuple-element.75) | copy-start | bytes 4718596
  402.7 5.8 collective-permute-start.16
  409.3 4.2 collective-permute-start.17
  413.6 4.9 collective-permute-start.18
  418.4 5.1 collective-permute-start.19
  423.6 3.7 collective-permute-start.30
  430.9 10.0 %collective-permute-start.25 = (bf16[192,768]{1,0:T(8,128)(2,1)S(1)}, bf16[192,768]{1,0:T(8,128)(2,1)}, u32[]{:S(2)}, u32[]{:S(2)}) collective-permute-start(bf16[192,768]{1,0:T(8,128)(2,1)S(1)} %broadcast_select_fusion.22), channel_id=1, source_target_pairs={{0,8},{8,0},{16,24},{24,16},{1,9},{9,1},{17,25},{25,17},{2,10},{10... | collective-permute-start | bytes 884744 | tf_op jit(solution)/shard_map/ppermute | solution.py:149
  433.4 30.7 %collective-permute-start.15 = (f32[192,512]{1,0:T(8,128)}, f32[192,512]{1,0:T(8,128)}, u32[]{:S(2)}, u32[]{:S(2)}) collective-permute-start(f32[192,512]{1,0:T(8,128)} %select_bitcast_fusion.4), channel_id=1, source_target_pairs={{0,2},{2,0},{1,3},{3,1},{4,6},{6,4},{5,7},{7,5},{8,10},{10,8},{9,1... | collective-permute-start | bytes 1179656 | tf_op jit(solution)/shard_map/ppermute | solution.py:103
  434.6 41.8 %collective-permute-start.36 = (bf16[192,1536]{1,0:T(8,128)(2,1)S(1)}, bf16[192,1536]{1,0:T(8,128)(2,1)S(1)}, u32[]{:S(2)}, u32[]{:S(2)}) collective-permute-start(bf16[192,1536]{1,0:T(8,128)(2,1)S(1)} %broadcast_select_fusion.6), channel_id=1, source_target_pairs={{0,8},{8,0},{16,24},{24,16},{1,9},{9,1},{17,25},{25,17},{2,10},{10... | collective-permute-start | bytes 1769480 | tf_op jit(solution)/shard_map/ppermute | solution.py:149
  435.4 27.0 %copy-start.40 = (bf16[1,384,768]{2,1,0:T(8,128)(2,1)S(1)}, bf16[1,384,768]{2,1,0:T(8,128)(2,1)}, u32[]{:S(2)}) copy-start(bf16[1,384,768]{2,1,0:T(8,128)(2,1)} %reduce-scatter.17.cloned.1.call-done) | copy-start | bytes 1769476
  436.6 25.9 %collective-permute-start.20 = (bf16[192,768]{1,0:T(8,128)(2,1)S(1)}, bf16[192,768]{1,0:T(8,128)(2,1)S(1)}, u32[]{:S(2)}, u32[]{:S(2)}) collective-permute-start(bf16[192,768]{1,0:T(8,128)(2,1)S(1)} %broadcast_select_fusion.25), channel_id=1, source_target_pairs={{0,8},{8,0},{16,24},{24,16},{1,9},{9,1},{17,25},{25,17},{2,10},{10... | collective-permute-start | bytes 884744 | tf_op jit(solution)/shard_map/ppermute | solution.py:149
  442.0 24.3 %collective-permute-start.26 = (bf16[96,768]{1,0:T(8,128)(2,1)S(1)}, bf16[96,768]{1,0:T(8,128)(2,1)S(1)}, u32[]{:S(2)}, u32[]{:S(2)}) collective-permute-start(bf16[96,768]{1,0:T(8,128)(2,1)S(1)} %broadcast_select_fusion.33), channel_id=1, source_target_pairs={{0,16},{8,24},{16,0},{24,8},{1,17},{9,25},{17,1},{25,9},{2,18},{10... | collective-permute-start | bytes 442376 | tf_op jit(solution)/shard_map/ppermute | solution.py:149
  462.6 13.7 %collective-permute-start.21 = (bf16[96,768]{1,0:T(8,128)(2,1)S(1)}, bf16[96,768]{1,0:T(8,128)(2,1)S(1)}, u32[]{:S(2)}, u32[]{:S(2)}) collective-permute-start(bf16[96,768]{1,0:T(8,128)(2,1)S(1)} %broadcast_select_fusion.36), channel_id=1, source_target_pairs={{0,16},{8,24},{16,0},{24,8},{1,17},{9,25},{17,1},{25,9},{2,18},{10... | collective-permute-start | bytes 442376 | tf_op jit(solution)/shard_map/ppermute | solution.py:149
  466.3 22.0 %collective-permute-start.27 = (bf16[96,768]{1,0:T(8,128)(2,1)S(1)}, bf16[96,768]{1,0:T(8,128)(2,1)S(1)}, u32[]{:S(2)}, u32[]{:S(2)}) collective-permute-start(bf16[96,768]{1,0:T(8,128)(2,1)S(1)} %add_convert_fusion.11), channel_id=1, source_target_pairs={{0,16},{8,24},{16,0},{24,8},{1,17},{9,25},{17,1},{25,9},{2,18},{10... | collective-permute-start | bytes 442376 | tf_op jit(solution)/shard_map/ppermute | solution.py:155
  476.4 15.2 %collective-permute-start.22 = (bf16[96,768]{1,0:T(8,128)(2,1)S(1)}, bf16[96,768]{1,0:T(8,128)(2,1)S(1)}, u32[]{:S(2)}, u32[]{:S(2)}) collective-permute-start(bf16[96,768]{1,0:T(8,128)(2,1)S(1)} %add_convert_fusion.12), channel_id=1, source_target_pairs={{0,16},{8,24},{16,0},{24,8},{1,17},{9,25},{17,1},{25,9},{2,18},{10... | collective-permute-start | bytes 442376 | tf_op jit(solution)/shard_map/ppermute | solution.py:155
  476.7 20.9 %collective-permute-start.37 = (bf16[96,1536]{1,0:T(8,128)(2,1)S(1)}, bf16[96,1536]{1,0:T(8,128)(2,1)S(1)}, u32[]{:S(2)}, u32[]{:S(2)}) collective-permute-start(bf16[96,1536]{1,0:T(8,128)(2,1)S(1)} %broadcast_select_fusion.16), channel_id=1, source_target_pairs={{0,16},{8,24},{16,0},{24,8},{1,17},{9,25},{17,1},{25,9},{2,18},{10... | collective-permute-start | bytes 884744 | tf_op jit(solution)/shard_map/ppermute | solution.py:149
  488.4 21.9 %collective-permute-start.28 = (bf16[192,768]{1,0:T(8,128)(2,1)S(1)}, bf16[192,768]{1,0:T(8,128)(2,1)S(1)}, u32[]{:S(2)}, u32[]{:S(2)}) collective-permute-start(bf16[192,768]{1,0:T(8,128)(2,1)S(1)} %pad_maximum_fusion.20), channel_id=1, source_target_pairs={{0,8},{8,0},{16,24},{24,16},{1,9},{9,1},{17,25},{25,17},{2,10},{10... | collective-permute-start | bytes 884744 | tf_op jit(solution)/shard_map/ppermute | solution.py:155
  491.6 25.0 %collective-permute-start.23 = (bf16[192,768]{1,0:T(8,128)(2,1)S(1)}, bf16[192,768]{1,0:T(8,128)(2,1)S(1)}, u32[]{:S(2)}, u32[]{:S(2)}) collective-permute-start(bf16[192,768]{1,0:T(8,128)(2,1)S(1)} %pad_maximum_fusion.19), channel_id=1, source_target_pairs={{0,8},{8,0},{16,24},{24,16},{1,9},{9,1},{17,25},{25,17},{2,10},{10... | collective-permute-start | bytes 884744 | tf_op jit(solution)/shard_map/ppermute | solution.py:155
  493.4 35.8 %collective-permute-start.31 = (bf16[192,1536]{1,0:T(8,128)(2,1)S(1)}, bf16[192,1536]{1,0:T(8,128)(2,1)S(1)}, u32[]{:S(2)}, u32[]{:S(2)}) collective-permute-start(bf16[192,1536]{1,0:T(8,128)(2,1)S(1)} %broadcast_select_fusion.9), channel_id=1, source_target_pairs={{0,8},{8,0},{16,24},{24,16},{1,9},{9,1},{17,25},{25,17},{2,10},{10... | collective-permute-start | bytes 1769480 | tf_op jit(solution)/shard_map/ppermute | solution.py:149
  497.8 31.4 %copy-start.22 = (bf16[1,384,1536]{2,1,0:T(8,128)(2,1)S(1)}, bf16[1,384,1536]{2,1,0:T(8,128)(2,1)}, u32[]{:S(2)}) copy-start(bf16[1,384,1536]{2,1,0:T(8,128)(2,1)} %reduce-scatter.19.cloned.1.call-done) | copy-start | bytes 3538948
  497.8 32.0 %collective-permute-start.38 = (bf16[96,1536]{1,0:T(8,128)(2,1)S(1)}, bf16[96,1536]{1,0:T(8,128)(2,1)S(1)}, u32[]{:S(2)}, u32[]{:S(2)}) collective-permute-start(bf16[96,1536]{1,0:T(8,128)(2,1)S(1)} %add_convert_fusion.7), channel_id=1, source_target_pairs={{0,16},{8,24},{16,0},{24,8},{1,17},{9,25},{17,1},{25,9},{2,18},{10... | collective-permute-start | bytes 884744 | tf_op jit(solution)/shard_map/ppermute | solution.py:155
  510.5 35.1 %collective-permute-start.29 = (bf16[192,768]{1,0:T(8,128)(2,1)S(1)}, bf16[192,768]{1,0:T(8,128)(2,1)S(1)}, u32[]{:S(2)}, u32[]{:S(2)}) collective-permute-start(bf16[192,768]{1,0:T(8,128)(2,1)S(1)} %get-tuple-element.67), channel_id=1, source_target_pairs={{0,1},{1,0},{2,3},{3,2},{4,5},{5,4},{6,7},{7,6},{8,9},{9,8},{10,11... | collective-permute-start | bytes 884744 | tf_op jit(solution)/shard_map/ppermute | solution.py:103
  516.8 28.9 %collective-permute-start.24 = (bf16[192,768]{1,0:T(8,128)(2,1)S(1)}, bf16[192,768]{1,0:T(8,128)(2,1)S(1)}, u32[]{:S(2)}, u32[]{:S(2)}) collective-permute-start(bf16[192,768]{1,0:T(8,128)(2,1)S(1)} %get-tuple-element.64), channel_id=1, source_target_pairs={{0,1},{1,0},{2,3},{3,2},{4,5},{5,4},{6,7},{7,6},{8,9},{9,8},{10,11... | collective-permute-start | bytes 884744 | tf_op jit(solution)/shard_map/ppermute | solution.py:103
  529.4 15.9 %collective-permute-start.32 = (bf16[96,1536]{1,0:T(8,128)(2,1)S(1)}, bf16[96,1536]{1,0:T(8,128)(2,1)S(1)}, u32[]{:S(2)}, u32[]{:S(2)}) collective-permute-start(bf16[96,1536]{1,0:T(8,128)(2,1)S(1)} %broadcast_select_fusion.19), channel_id=1, source_target_pairs={{0,16},{8,24},{16,0},{24,8},{1,17},{9,25},{17,1},{25,9},{2,18},{10... | collective-permute-start | bytes 884744 | tf_op jit(solution)/shard_map/ppermute | solution.py:149
  529.9 33.5 %collective-permute-start.39 = (bf16[192,1536]{1,0:T(8,128)(2,1)S(1)}, bf16[192,1536]{1,0:T(8,128)(2,1)S(1)}, u32[]{:S(2)}, u32[]{:S(2)}) collective-permute-start(bf16[192,1536]{1,0:T(8,128)(2,1)S(1)} %pad_maximum_fusion.13), channel_id=1, source_target_pairs={{0,8},{8,0},{16,24},{24,16},{1,9},{9,1},{17,25},{25,17},{2,10},{10... | collective-permute-start | bytes 1769480 | tf_op jit(solution)/shard_map/ppermute | solution.py:155
  545.5 16.2 %collective-permute-start.33 = (bf16[96,1536]{1,0:T(8,128)(2,1)S(1)}, bf16[96,1536]{1,0:T(8,128)(2,1)S(1)}, u32[]{:S(2)}, u32[]{:S(2)}) collective-permute-start(bf16[96,1536]{1,0:T(8,128)(2,1)S(1)} %add_convert_fusion.8), channel_id=1, source_target_pairs={{0,16},{8,24},{16,0},{24,8},{1,17},{9,25},{17,1},{25,9},{2,18},{10... | collective-permute-start | bytes 884744 | tf_op jit(solution)/shard_map/ppermute | solution.py:155
  561.8 14.4 %collective-permute-start.34 = (bf16[192,1536]{1,0:T(8,128)(2,1)S(1)}, bf16[192,1536]{1,0:T(8,128)(2,1)S(1)}, u32[]{:S(2)}, u32[]{:S(2)}) collective-permute-start(bf16[192,1536]{1,0:T(8,128)(2,1)S(1)} %pad_maximum_fusion.12), channel_id=1, source_target_pairs={{0,8},{8,0},{16,24},{24,16},{1,9},{9,1},{17,25},{25,17},{2,10},{10... | collective-permute-start | bytes 1769480 | tf_op jit(solution)/shard_map/ppermute | solution.py:155
  565.1 27.3 %collective-permute-start.40 = (bf16[192,1536]{1,0:T(8,128)(2,1)}, bf16[192,1536]{1,0:T(8,128)(2,1)}, u32[]{:S(2)}, u32[]{:S(2)}) collective-permute-start(bf16[192,1536]{1,0:T(8,128)(2,1)} %get-tuple-element.61), channel_id=1, source_target_pairs={{0,1},{1,0},{2,3},{3,2},{4,5},{5,4},{6,7},{7,6},{8,9},{9,8},{10,11... | collective-permute-start | bytes 1769480 | tf_op jit(solution)/shard_map/ppermute | solution.py:103
  577.9 15.8 %collective-permute-start.35 = (bf16[192,1536]{1,0:T(8,128)(2,1)}, bf16[192,1536]{1,0:T(8,128)(2,1)}, u32[]{:S(2)}, u32[]{:S(2)}) collective-permute-start(bf16[192,1536]{1,0:T(8,128)(2,1)} %get-tuple-element.58), channel_id=1, source_target_pairs={{0,1},{1,0},{2,3},{3,2},{4,5},{5,4},{6,7},{7,6},{8,9},{9,8},{10,11... | collective-permute-start | bytes 1769480 | tf_op jit(solution)/shard_map/ppermute | solution.py:103
  (155 other events, 442.4 us)
Sparse Core Ops, SparseCore 0:
  51.2 80.5 all-gather.6
  133.6 76.6 all-gather.8
  281.1 37.3 reduce-scatter.12
  321.4 61.2 reduce-scatter.14
  386.1 38.5 reduce-scatter.16
  427.6 64.4 reduce-scatter.18

commit v4 on v3

--- a/solution.py
+++ b/solution.py
@@ -109,10 +109,14 @@
 
 
 def share_weights(parts):
-    joined = jnp.concatenate(parts, axis=-1)
     first = lax.axis_index("core") == 0
-    kept = jnp.where(first, joined[:, 0], joined[:, 1])
-    given = jnp.where(first, joined[:, 1], joined[:, 0])
+    kept, given = [], []
+    for part in parts:
+        half = part.shape[-1] // 2
+        lower, upper = part[..., :half], part[..., half:]
+        kept.append(jnp.where(first, lower, upper).reshape(part.shape[0], -1))
+        given.append(jnp.where(first, upper, lower).reshape(part.shape[0], -1))
+    kept, given = jnp.concatenate(kept, axis=1), jnp.concatenate(given, axis=1)
     return in_order("core", kept, swap(given, "core"), 0)
 
 
@@ -174,8 +178,13 @@
     piece = piece.reshape(2, -1, piece.shape[-1])
     first = lax.axis_index("core") == 0
     kept = jnp.where(first, piece[0], piece[1])
-    given = jnp.where(first, piece[1], piece[0])
-    return in_order("core", kept[:, None], swap(given, "core")[:, None], 1).astype(jnp.float32)
+    came = swap(jnp.where(first, piece[1], piece[0]), "core")
+    return jnp.where(first, kept, came), jnp.where(first, came, kept)
+
+
+def join_halves(pieces, start, stop, inner):
+    shaped = [part[:, start:stop].reshape((-1,) + inner) for part in pieces]
+    return jnp.concatenate(shaped, axis=-1).astype(jnp.float32)
 
 
 def shards(
@@ -209,13 +218,10 @@
         gathered = gather_plane(
             share_weights(
                 [
-                    up_weight[layer_at].reshape(depth_in, 2, half_hidden),
-                    down_weight[layer_at].reshape(depth_in, 2, half_hidden),
-                    qkv_weight[layer_at]
-                    .reshape(depth_in, 3, 2, half_head)
-                    .transpose(0, 2, 1, 3)
-                    .reshape(depth_in, 2, 3 * half_head),
-                    out_weight[layer_at].reshape(depth_in, 2, half_head),
+                    up_weight[layer_at],
+                    down_weight[layer_at],
+                    qkv_weight[layer_at],
+                    out_weight[layer_at],
                 ]
             )
         )
@@ -428,13 +434,17 @@
     up_sums = lax.dynamic_index_in_dim(up_sums, at_row, 2, keepdims=False)
     up_sums = up_sums.transpose(1, 0, 2).reshape(layers, hidden_width)
 
-    attention_out = jnp.stack([return_weights(part) for part in attention_grads])
-    forward_out = jnp.stack([return_weights(part) for part in forward_grads])
-    qkv_grad = attention_out[..., : 3 * half_head].reshape(layers, depth_in, 2, 3, half_head)
-    qkv_grad = qkv_grad.transpose(0, 1, 3, 2, 4).reshape(layers, depth_in, 3, head_width)
-    out_grad = attention_out[..., 3 * half_head :].reshape(layers, depth_in, head_width)
-    up_grad = forward_out[..., :half_hidden].reshape(layers, depth_in, hidden_width)
-    down_grad = forward_out[..., half_hidden:].reshape(layers, depth_in, hidden_width)
+    attention_out = [return_weights(part) for part in attention_grads]
+    forward_out = [return_weights(part) for part in forward_grads]
+    split = 3 * half_head
+    qkv_grad = jnp.stack([join_halves(part, 0, split, (3, half_head)) for part in attention_out])
+    out_grad = jnp.stack(
+        [join_halves(part, split, split + half_head, (half_head,)) for part in attention_out]
+    )
+    up_grad = jnp.stack([join_halves(part, 0, half_hidden, (half_hidden,)) for part in forward_out])
+    down_grad = jnp.stack(
+        [join_halves(part, half_hidden, 2 * half_hidden, (half_hidden,)) for part in forward_out]
+    )
     return (
         activations,
         input_grad,

time: 618 us -> 614 us (level)
  local copies, waits for them, and re-layouts: 137 us -> 122 us
  waiting for transfers between devices: 238 us -> 253 us
    all_gather x0 -> x2, local copies, waits for them, and re-layouts: none -> 20.7 us  [gather_plane(): everything = lax.all_gather(piece, PLANE, axis=0, tiled=False)]
    ppermute x8, waiting for transfers between devices: 57.6 us -> 76.7 us  [group_sum(): came = lax.ppermute(given, 'dp', partners(step))]
    concatenate x2 -> x10, local copies, waits for them, and re-layouts: 18.6 us -> 2.16 us  [the longest x2 1.97 us: share_weights(): jnp.concatenate(given, axis=1)]
    reshape x6 -> x0, local copies, waits for them, and re-layouts: 12 us -> none  [the longest x1 4.37 us: shards(): qkv_grad.transpose(0, 1, 3, 2, 4).reshape(layers, depth_in, 3, head_width)]
    unnamed x362 -> x391, local copies, waits for them, and re-layouts: 32.7 us -> 36.1 us
    select_n x5 -> x16, other arithmetic: 14.2 us -> 13.9 us  [the longest x8 5.7 us: share_weights(): kept.append(jnp.where(first, lower, upper).reshape(part.shape[0], -1))]
  transfers between devices with their start and end apart: 47 -> 47, of which waited for: 23 -> 22; matrix products, arithmetic and copies ran while one was open for 31% -> 33% of each run, Pallas kernels for 0% -> 0%
where the time goes in v4:
time: 614 us; the launch traced here: 604 us
  waiting for transfers between devices  253 us (41%)
  local copies, waits for them, and re-layouts  122 us (20%)
  other arithmetic  96.3 us (16%)
  matrix products  71.5 us (12%)
  starting transfers between devices  32.6 us (5%)
  between operations  17.5 us (3%)
  blocking collectives  10.7 us (2%)
    all_gather x2, waiting for transfers between devices, gather_plane(): everything = lax.all_gather(piece, PLANE, axis=0, tiled=False)  92.9 us
    ppermute x8, waiting for transfers between devices, group_sum(): came = lax.ppermute(given, 'dp', partners(step))  76.7 us
    ppermute x8, waiting for transfers between devices, group_sum(): came = lax.ppermute(value, 'dp', partners(step))  61.7 us
    unnamed x391, local copies, waits for them, and re-layouts  36.1 us
    all_gather x2, local copies, waits for them, and re-layouts, gather_plane(): everything = lax.all_gather(piece, PLANE, axis=0, tiled=False)  20.7 us
    another operation x4, local copies, waits for them, and re-layouts, scatter_plane(): stacked = jnp.stack(grads).astype(jnp.bfloat16)  20.3 us
    dot_general x16, matrix products, plain(): return jnp.dot(left_side, right_side, preferred_element_type=jnp.float32)  20.1 us
    dot_general x16, matrix products, contract_cols(): lax.dot_general(left_side, right_side, (((1,), (1,)), ((), ())), preferre...  17.7 us
  transfers between devices with their start and end apart: 47, of which 22 were waited for; matrix products, arithmetic and copies ran while one was open for 33% of the time, Pallas kernels for 0%

profile of v4, /device:TPU:0, one launch (start us, length us, event | category | flops | bytes accessed | tf_op | source)
XLA Modules:
  0.0 603.8 jit_solution(985133991405260574)
XLA Ops:
  28.7 3.3 broadcast_select_fusion.1
  34.8 3.0 collective-permute-start.9
  42.3 10.7 %all-gather.3 = bf16[8,1,7424]{2,1,0:T(2,128)(2,1)S(1)} all-gather(bf16[1,1,7424]{2,1,0:T(2,128)(2,1)S(1)} %reshape.730), channel_id=2, replica_groups=mesh['dp'=4,'row'=2,'pair'=2,'core'=2] {'row','pair','core'}, dimensions={0}, use_global_device_ids=true | all-gather | bytes 133632 | tf_op jit(solution)/shard_map/all_gather | solution.py:241
  54.0 1.9 pad_maximum_fusion.5
  57.0 2.0 select_bitcast_fusion.6
  64.6 49.6 %all-gather.7.cloned.1.call-done = bf16[1536,2304]{0,1:T(8,128)(2,1)} async-done(((bf16[384,2304]{0,1:T(8,128)(2,1)}), bf16[1536,2304]{0,1:T(8,128)(2,1)}) %all-gather.7.cloned.1.call-update) | async-done | bytes 7077904 | tf_op jit(solution)/shard_map/all_gather | solution.py:124
  114.3 10.1 %copy.228 = bf16[1536,2304]{1,0:T(8,128)(2,1)} copy(bf16[1536,2304]{0,1:T(8,128)(2,1)} %all-gather.7.cloned.1.call-done) | data formatting | bytes 14155776 | tf_op jit(solution)/shard_map/all_gather | solution.py:124
  124.3 2.0 slice_bitcast_fusion.6
  136.9 2.7 slice_bitcast_fusion.2
  139.6 3.9 fusion.146
  149.5 43.2 %all-gather.9.cloned.1.call-done = bf16[1536,2304]{0,1:T(8,128)(2,1)} async-done(((bf16[384,2304]{0,1:T(8,128)(2,1)}), bf16[1536,2304]{0,1:T(8,128)(2,1)}) %all-gather.9.cloned.1.call-update) | async-done | bytes 7077904 | tf_op jit(solution)/shard_map/all_gather | solution.py:124
  192.7 10.7 %copy.238 = bf16[1536,2304]{1,0:T(8,128)(2,1)} copy(bf16[1536,2304]{0,1:T(8,128)(2,1)} %all-gather.9.cloned.1.call-done) | data formatting | bytes 14155776 | tf_op jit(solution)/shard_map/all_gather | solution.py:124
  203.4 1.9 slice_bitcast_fusion.4
  205.5 2.6 fusion.145
  213.3 2.3 copy-done.1
  218.6 3.3 collective-permute-done.10
  225.0 2.3 convert_reduce_fusion.1
  228.0 2.4 convert_reduce_fusion.2
  231.4 2.0 convolution_add_fusion.3
  234.6 2.3 convolution_add_fusion.4
  237.3 2.3 copy.242
  240.4 4.0 multiply_reduce_fusion.2
  244.5 4.9 convert_reduce_fusion.5
  254.6 2.4 convert_reduce_fusion.8
  260.8 2.1 fusion.47
  269.2 4.3 copy.249
  273.6 2.3 convolution_convert_fusion.5
  278.7 2.0 convolution_add_fusion.2
  284.2 2.7 pad_maximum_fusion
  286.9 6.7 %copy.251 = bf16[2,768,1536]{2,1,0:T(8,128)(2,1)} copy(bf16[2,768,1536]{1,2,0:T(8,128)(2,1)} %pad_maximum_fusion) | data formatting | bytes 9437184 | tf_op jit(solution)/shard_map/stack | solution.py:131
  294.3 3.5 multiply_reduce_fusion.3
  299.9 2.2 convert_reduce_fusion.4
  304.0 2.2 convert_reduce_fusion.3
  308.4 3.0 collective-permute-done.13
  312.9 2.3 convert_reduce_fusion.7
  329.3 2.4 copy.253
  338.8 6.4 %collective-permute-done.8 = bf16[192,512]{1,0:T(8,128)(2,1)S(1)} collective-permute-done((bf16[192,512]{1,0:T(8,128)(2,1)S(1)}, bf16[192,512]{1,0:T(8,128)(2,1)S(1)}, u32[]{:S(2)}, u32[]{:S(2)}) %collective-permute-start.8) | collective-permute-done | bytes 196640 | tf_op jit(solution)/shard_map/ppermute | solution.py:103
  349.9 2.1 convolution_convert_fusion.1
  354.6 2.0 convolution_add_fusion
  360.0 2.6 pad_maximum_fusion.1
  362.6 6.9 %copy.256 = bf16[2,768,1536]{2,1,0:T(8,128)(2,1)} copy(bf16[2,768,1536]{1,2,0:T(8,128)(2,1)} %pad_maximum_fusion.1) | data formatting | bytes 9437184 | tf_op jit(solution)/shard_map/stack | solution.py:131
  373.4 3.9 multiply_reduce_fusion.5
  385.6 3.7 collective-permute-done.17
  390.9 2.7 collective-permute-done.18
  393.6 2.5 collective-permute-start.19
  396.1 3.6 multiply_add_fusion
  405.0 3.0 copy.252
  418.2 1.9 collective-permute-start.20
  422.5 2.2 collective-permute-start.26
  424.7 21.2 %collective-permute-done.20 = bf16[192,768]{0,1:T(8,128)(2,1)S(1)} collective-permute-done((bf16[192,768]{0,1:T(8,128)(2,1)S(1)}, bf16[192,768]{0,1:T(8,128)(2,1)S(1)}, u32[]{:S(2)}, u32[]{:S(2)}) %collective-permute-start.20) | collective-permute-done | bytes 294944 | tf_op jit(solution)/shard_map/ppermute | solution.py:153
  449.7 1.9 collective-permute-start.27
  451.6 11.2 %collective-permute-done.21 = bf16[96,768]{0,1:T(8,128)(2,1)S(1)} collective-permute-done((bf16[96,768]{0,1:T(8,128)(2,1)S(1)}, bf16[96,768]{0,1:T(8,128)(2,1)S(1)}, u32[]{:S(2)}, u32[]{:S(2)}) %collective-permute-start.21) | collective-permute-done | bytes 147488 | tf_op jit(solution)/shard_map/ppermute | solution.py:153
  464.4 3.0 collective-permute-start.37
  467.3 10.2 %collective-permute-done.27 = bf16[96,768]{0,1:T(8,128)(2,1)S(1)} collective-permute-done((bf16[96,768]{0,1:T(8,128)(2,1)S(1)}, bf16[96,768]{0,1:T(8,128)(2,1)S(1)}, u32[]{:S(2)}, u32[]{:S(2)}) %collective-permute-start.27) | collective-permute-done | bytes 147488 | tf_op jit(solution)/shard_map/ppermute | solution.py:159
  477.8 4.0 collective-permute-done.22
  482.2 5.5 collective-permute-done.37
  487.9 14.3 %collective-permute-done.28 = bf16[192,768]{0,1:T(8,128)(2,1)S(1)} collective-permute-done((bf16[192,768]{0,1:T(8,128)(2,1)S(1)}, bf16[192,768]{0,1:T(8,128)(2,1)S(1)}, u32[]{:S(2)}, u32[]{:S(2)}) %collective-permute-start.28) | collective-permute-done | bytes 294944 | tf_op jit(solution)/shard_map/ppermute | solution.py:159
  502.6 8.2 %collective-permute-done.23 = bf16[192,768]{0,1:T(8,128)(2,1)S(1)} collective-permute-done((bf16[192,768]{0,1:T(8,128)(2,1)S(1)}, bf16[192,768]{0,1:T(8,128)(2,1)S(1)}, u32[]{:S(2)}, u32[]{:S(2)}) %collective-permute-start.23) | collective-permute-done | bytes 294944 | tf_op jit(solution)/shard_map/ppermute | solution.py:159
  513.4 2.1 collective-permute-start.31
  516.8 23.9 %collective-permute-done.31 = bf16[192,1536]{1,0:T(8,128)(2,1)S(1)} collective-permute-done((bf16[192,1536]{1,0:T(8,128)(2,1)S(1)}, bf16[192,1536]{1,0:T(8,128)(2,1)S(1)}, u32[]{:S(2)}, u32[]{:S(2)}) %collective-permute-start.31) | collective-permute-done | bytes 589856 | tf_op jit(solution)/shard_map/ppermute | solution.py:153
  542.8 13.9 %collective-permute-done.32 = bf16[96,1536]{1,0:T(8,128)(2,1)S(1)} collective-permute-done((bf16[96,1536]{1,0:T(8,128)(2,1)S(1)}, bf16[96,1536]{1,0:T(8,128)(2,1)S(1)}, u32[]{:S(2)}, u32[]{:S(2)}) %collective-permute-start.32) | collective-permute-done | bytes 294944 | tf_op jit(solution)/shard_map/ppermute | solution.py:153
  557.2 15.1 %collective-permute-done.33 = bf16[96,1536]{1,0:T(8,128)(2,1)S(1)} collective-permute-done((bf16[96,1536]{1,0:T(8,128)(2,1)S(1)}, bf16[96,1536]{1,0:T(8,128)(2,1)S(1)}, u32[]{:S(2)}, u32[]{:S(2)}) %collective-permute-start.33) | collective-permute-done | bytes 294944 | tf_op jit(solution)/shard_map/ppermute | solution.py:159
  573.9 2.7 broadcast_select_fusion.12
  579.6 9.9 %collective-permute-done.34 = bf16[192,1536]{1,0:T(8,128)(2,1)} collective-permute-done((bf16[192,1536]{1,0:T(8,128)(2,1)}, bf16[192,1536]{1,0:T(8,128)(2,1)}, u32[]{:S(2)}, u32[]{:S(2)}) %collective-permute-start.34) | collective-permute-done | bytes 589856 | tf_op jit(solution)/shard_map/ppermute | solution.py:159
  (730 shorter events, 184.1 us)
Async XLA Ops:
  7.2 107.1 %all-gather.7.cloned.1.call-start = ((), (), s32[]{:S(2)}) async-start(), calls=%async_computation.4 | async-start | bytes 8847360 | tf_op jit(solution)/shard_map/all_gather | solution.py:124
  19.1 6.5 %collective-permute-start.2 = (bf16[192,2304]{1,0:T(8,128)(2,1)}, bf16[192,2304]{1,0:T(8,128)(2,1)}, u32[]{:S(2)}, u32[]{:S(2)}) collective-permute-start(bf16[192,2304]{1,0:T(8,128)(2,1)} %copy.225), channel_id=1, source_target_pairs={{0,1},{1,0},{2,3},{3,2},{4,5},{5,4},{6,7},{7,6},{8,9},{9,8},{10,11... | collective-permute-start | bytes 2654216 | tf_op jit(solution)/shard_map/ppermute | solution.py:103
  23.7 3.5 collective-permute-start.5
  33.8 20.2 %copy-start.16 = (bf16[192,2304]{0,1:T(8,128)(2,1)S(1)}, bf16[192,2304]{0,1:T(8,128)(2,1)}, u32[]{:S(2)}) copy-start(bf16[192,2304]{0,1:T(8,128)(2,1)} %get-tuple-element.179) | copy-start | bytes 2654212
  33.9 158.8 %all-gather.9.cloned.1.call-start = ((), (), s32[]{:S(2)}) async-start(), calls=%async_computation.5 | async-start | bytes 8847360 | tf_op jit(solution)/shard_map/all_gather | solution.py:124
  34.8 21.9 %collective-permute-start.9 = (bf16[192,512]{1,0:T(8,128)(2,1)S(1)}, bf16[192,512]{1,0:T(8,128)(2,1)}, u32[]{:S(2)}, u32[]{:S(2)}) collective-permute-start(bf16[192,512]{1,0:T(8,128)(2,1)S(1)} %constant_dynamic-slice_fusion.8), channel_id=1, source_target_pairs={{0,2},{2,0},{1,3},{3,1},{4,6},{6,4},{5,7},{7,5},{8,10},{10,8},{9,1... | collective-permute-start | bytes 589832 | tf_op jit(solution)/shard_map/ppermute | solution.py:103
  37.9 18.9 %collective-permute-start = (bf16[192,512]{1,0:T(8,128)(2,1)S(1)}, bf16[192,512]{1,0:T(8,128)(2,1)}, u32[]{:S(2)}, u32[]{:S(2)}) collective-permute-start(bf16[192,512]{1,0:T(8,128)(2,1)S(1)} %constant_dynamic-slice_fusion.12), channel_id=1, source_target_pairs={{0,2},{2,0},{1,3},{3,1},{4,6},{6,4},{5,7},{7,5},{8,10},{10,8},{9,1... | collective-permute-start | bytes 589832 | tf_op jit(solution)/shard_map/ppermute | solution.py:103
  56.0 325.9 %reduce-scatter.13.cloned.1.call-start = ((), (), s32[]{:S(2)}) async-start(), calls=%async_computation.6 | async-start | bytes 2949120
  59.1 2.3 collective-permute-start.1
  62.6 77.0 %copy-start.2 = (f32[768,512]{0,1:T(8,128)}, f32[768,512]{0,1:T(8,128)S(1)}, u32[]{:S(2)}) copy-start(f32[768,512]{0,1:T(8,128)S(1)} %copy.218) | copy-start | bytes 4718596
  64.3 60.1 %copy-start.109 = (f32[512]{0:T(512)}, f32[512]{0:T(512)S(1)}, u32[]{:S(2)}) copy-start(f32[512]{0:T(512)S(1)} %get-tuple-element.283) | copy-start | bytes 6148
  64.3 60.1 %copy-start.111 = (f32[512]{0:T(512)}, f32[512]{0:T(512)S(1)}, u32[]{:S(2)}) copy-start(f32[512]{0:T(512)S(1)} %get-tuple-element.284) | copy-start | bytes 6148
  64.6 62.5 %copy-start.72 = (bf16[512,768]{1,0:T(8,128)(2,1)}, bf16[512,768]{1,0:T(8,128)(2,1)S(1)}, u32[]{:S(2)}) copy-start(bf16[512,768]{1,0:T(8,128)(2,1)S(1)} %add_convert_fusion.4) | copy-start | bytes 2359300
  135.0 4.6 collective-permute-start.3
  149.0 54.4 %copy-start.51 = (f32[512,768]{1,0:T(8,128)}, f32[512,768]{1,0:T(8,128)S(1)}, u32[]{:S(2)}) copy-start(f32[512,768]{1,0:T(8,128)S(1)} %convolution_add_fusion.7) | copy-start | bytes 4718596
  149.0 56.3 %collective-permute-start.4 = (f32[512,768]{1,0:T(8,128)S(1)}, f32[512,768]{1,0:T(8,128)}, u32[]{:S(2)}, u32[]{:S(2)}) collective-permute-start(f32[512,768]{1,0:T(8,128)S(1)} %convolution_add_fusion.7), channel_id=1, source_target_pairs={{0,1},{1,0},{2,3},{3,2},{4,5},{5,4},{6,7},{7,6},{8,9},{9,8},{10,11... | collective-permute-start | bytes 4718600 | tf_op jit(solution)/shard_map/ppermute | solution.py:31
  205.3 11.5 %copy-start.27 = (bf16[768,768]{1,0:T(8,128)(2,1)}, bf16[768,768]{1,0:T(8,128)(2,1)S(1)}, u32[]{:S(2)}) copy-start(bf16[768,768]{1,0:T(8,128)(2,1)S(1)} %get-tuple-element.173) | copy-start | bytes 3538948
  205.3 12.0 %copy-start.8 = (bf16[768,768]{1,0:T(8,128)(2,1)}, bf16[768,768]{1,0:T(8,128)(2,1)S(1)}, u32[]{:S(2)}) copy-start(bf16[768,768]{1,0:T(8,128)(2,1)S(1)} %get-tuple-element.172) | copy-start | bytes 3538948
  218.0 4.7 collective-permute-start.6
  218.4 3.6 collective-permute-start.10
  233.4 7.0 %collective-permute-start.11 = (f32[512,768]{1,0:T(8,128)}, f32[512,768]{1,0:T(8,128)}, u32[]{:S(2)}, u32[]{:S(2)}) collective-permute-start(f32[512,768]{1,0:T(8,128)} %convolution_add_fusion.3), channel_id=1, source_target_pairs={{0,1},{1,0},{2,3},{3,2},{4,5},{5,4},{6,7},{7,6},{8,9},{9,8},{10,11... | collective-permute-start | bytes 4718600 | tf_op jit(solution)/shard_map/ppermute | solution.py:31
  236.9 7.5 %collective-permute-start.7 = (f32[512,768]{1,0:T(8,128)}, f32[512,768]{1,0:T(8,128)}, u32[]{:S(2)}, u32[]{:S(2)}) collective-permute-start(f32[512,768]{1,0:T(8,128)} %convolution_add_fusion.4), channel_id=1, source_target_pairs={{0,1},{1,0},{2,3},{3,2},{4,5},{5,4},{6,7},{7,6},{8,9},{9,8},{10,11... | collective-permute-start | bytes 4718600 | tf_op jit(solution)/shard_map/ppermute | solution.py:31
  240.4 14.2 %slice-start.2 = ((s8[6291456]{0:T(1024)(128)(4,1)}), s8[4194304]{0:T(1024)(128)(4,1)S(1)}, s32[]{:S(2)}) async-start(s8[6291456]{0:T(1024)(128)(4,1)} %bitcast.333), calls=%async_computation.12 | async-start | bytes 8388608
  273.6 131.4 %reduce-scatter.15.cloned.1.call-start = ((), (), s32[]{:S(2)}) async-start(), calls=%async_computation.7 | async-start | bytes 5898240
  280.7 13.4 %collective-permute-start.12 = (f32[512,768]{1,0:T(8,128)}, f32[512,768]{1,0:T(8,128)}, u32[]{:S(2)}, u32[]{:S(2)}) collective-permute-start(f32[512,768]{1,0:T(8,128)} %convolution_add_fusion.2), channel_id=1, source_target_pairs={{0,1},{1,0},{2,3},{3,2},{4,5},{5,4},{6,7},{7,6},{8,9},{9,8},{10,11... | collective-permute-start | bytes 4718600 | tf_op jit(solution)/shard_map/ppermute | solution.py:31
  293.6 123.1 %reduce-scatter.17.cloned.1.call-start = ((), (), s32[]{:S(2)}) async-start(), calls=%async_computation.8 | async-start | bytes 2949120
  307.9 3.5 collective-permute-start.13
  331.8 180.3 %reduce-scatter.19.cloned.1.call-start = ((), (), s32[]{:S(2)}) async-start(), calls=%async_computation.9 | async-start | bytes 5898240
  333.3 14.0 %copy-start.126 = (f32[768]{0:T(1024)S(1)}, f32[768]{0:T(1024)}, u32[]{:S(2)}) copy-start(f32[768]{0:T(1024)} %get-tuple-element.154) | copy-start | bytes 9220
  333.3 14.6 %copy-start.143 = (f32[768]{0:T(1024)S(1)}, f32[768]{0:T(1024)}, u32[]{:S(2)}) copy-start(f32[768]{0:T(1024)} %get-tuple-element.119) | copy-start | bytes 9220
  333.3 16.6 %copy-start.68 = (bf16[512,768]{1,0:T(8,128)(2,1)S(1)}, bf16[512,768]{1,0:T(8,128)(2,1)}, u32[]{:S(2)}) copy-start(bf16[512,768]{1,0:T(8,128)(2,1)} %copy-done.67) | copy-start | bytes 2359300
  333.4 11.9 %collective-permute-start.8 = (bf16[192,512]{1,0:T(8,128)(2,1)S(1)}, bf16[192,512]{1,0:T(8,128)(2,1)S(1)}, u32[]{:S(2)}, u32[]{:S(2)}) collective-permute-start(bf16[192,512]{1,0:T(8,128)(2,1)S(1)} %select_bitcast_fusion.7), channel_id=1, source_target_pairs={{0,2},{2,0},{1,3},{3,1},{4,6},{6,4},{5,7},{7,5},{8,10},{10,8},{9,1... | collective-permute-start | bytes 589832 | tf_op jit(solution)/shard_map/ppermute | solution.py:103
  356.6 16.8 %collective-permute-start.14 = (f32[512,768]{1,0:T(8,128)}, f32[512,768]{1,0:T(8,128)S(1)}, u32[]{:S(2)}, u32[]{:S(2)}) collective-permute-start(f32[512,768]{1,0:T(8,128)} %convolution_add_fusion), channel_id=1, source_target_pairs={{0,1},{1,0},{2,3},{3,2},{4,5},{5,4},{6,7},{7,6},{8,9},{9,8},{10,11... | collective-permute-start | bytes 4718600 | tf_op jit(solution)/shard_map/ppermute | solution.py:31
  377.3 13.6 %copy-start.150 = (f32[512]{0:T(512)S(1)}, f32[512]{0:T(512)}, u32[]{:S(2)}) copy-start(f32[512]{0:T(512)} %get-tuple-element.114) | copy-start | bytes 6148
  377.3 18.7 %copy-start.110 = (f32[512]{0:T(512)S(1)}, f32[512]{0:T(512)}, u32[]{:S(2)}) copy-start(f32[512]{0:T(512)} %copy-done.109) | copy-start | bytes 6148
  377.3 18.8 %copy-start.112 = (f32[512]{0:T(512)S(1)}, f32[512]{0:T(512)}, u32[]{:S(2)}) copy-start(f32[512]{0:T(512)} %copy-done.111) | copy-start | bytes 6148
  379.6 4.6 collective-permute-start.16
  384.2 5.1 collective-permute-start.17
  389.3 4.2 collective-permute-start.18
  393.6 6.1 %collective-permute-start.19 = (f32[13824]{0:T(1024)S(1)}, f32[13824]{0:T(1024)S(1)}, u32[]{:S(2)}, u32[]{:S(2)}) collective-permute-start(f32[13824]{0:T(1024)S(1)} %add.495), channel_id=1, source_target_pairs={{0,16},{8,24},{16,0},{24,8},{1,17},{9,25},{17,1},{25,9},{2,18},{10... | collective-permute-start | bytes 165896 | tf_op jit(solution)/shard_map/ppermute | solution.py:172
  399.7 3.7 collective-permute-start.30
  408.9 12.2 %collective-permute-start.25 = (bf16[192,768]{0,1:T(8,128)(2,1)}, bf16[192,768]{0,1:T(8,128)(2,1)}, u32[]{:S(2)}, u32[]{:S(2)}) collective-permute-start(bf16[192,768]{0,1:T(8,128)(2,1)} %broadcast_select_fusion.20), channel_id=1, source_target_pairs={{0,8},{8,0},{16,24},{24,16},{1,9},{9,1},{17,25},{25,17},{2,10},{10... | collective-permute-start | bytes 884744 | tf_op jit(solution)/shard_map/ppermute | solution.py:153
  412.8 34.7 %collective-permute-start.15 = (f32[192,512]{1,0:T(8,128)}, f32[192,512]{1,0:T(8,128)}, u32[]{:S(2)}, u32[]{:S(2)}) collective-permute-start(f32[192,512]{1,0:T(8,128)} %select_bitcast_fusion), channel_id=1, source_target_pairs={{0,2},{2,0},{1,3},{3,1},{4,6},{6,4},{5,7},{7,5},{8,10},{10,8},{9,1... | collective-permute-start | bytes 1179656 | tf_op jit(solution)/shard_map/ppermute | solution.py:103
  415.3 47.7 %collective-permute-start.36 = (bf16[192,1536]{1,0:T(8,128)(2,1)}, bf16[192,1536]{1,0:T(8,128)(2,1)}, u32[]{:S(2)}, u32[]{:S(2)}) collective-permute-start(bf16[192,1536]{1,0:T(8,128)(2,1)} %broadcast_select_fusion.6), channel_id=1, source_target_pairs={{0,8},{8,0},{16,24},{24,16},{1,9},{9,1},{17,25},{25,17},{2,10},{10... | collective-permute-start | bytes 1769480 | tf_op jit(solution)/shard_map/ppermute | solution.py:153
  418.2 27.7 %collective-permute-start.20 = (bf16[192,768]{0,1:T(8,128)(2,1)S(1)}, bf16[192,768]{0,1:T(8,128)(2,1)S(1)}, u32[]{:S(2)}, u32[]{:S(2)}) collective-permute-start(bf16[192,768]{0,1:T(8,128)(2,1)S(1)} %broadcast_select_fusion.23), channel_id=1, source_target_pairs={{0,8},{8,0},{16,24},{24,16},{1,9},{9,1},{17,25},{25,17},{2,10},{10... | collective-permute-start | bytes 884744 | tf_op jit(solution)/shard_map/ppermute | solution.py:153
  422.5 27.0 %collective-permute-start.26 = (bf16[96,768]{0,1:T(8,128)(2,1)S(1)}, bf16[96,768]{0,1:T(8,128)(2,1)S(1)}, u32[]{:S(2)}, u32[]{:S(2)}) collective-permute-start(bf16[96,768]{0,1:T(8,128)(2,1)S(1)} %broadcast_select_fusion.52), channel_id=1, source_target_pairs={{0,16},{8,24},{16,0},{24,8},{1,17},{9,25},{17,1},{25,9},{2,18},{10... | collective-permute-start | bytes 442376 | tf_op jit(solution)/shard_map/ppermute | solution.py:153
  446.3 16.5 %collective-permute-start.21 = (bf16[96,768]{0,1:T(8,128)(2,1)S(1)}, bf16[96,768]{0,1:T(8,128)(2,1)S(1)}, u32[]{:S(2)}, u32[]{:S(2)}) collective-permute-start(bf16[96,768]{0,1:T(8,128)(2,1)S(1)} %broadcast_select_fusion.55), channel_id=1, source_target_pairs={{0,16},{8,24},{16,0},{24,8},{1,17},{9,25},{17,1},{25,9},{2,18},{10... | collective-permute-start | bytes 442376 | tf_op jit(solution)/shard_map/ppermute | solution.py:153
  449.7 27.9 %collective-permute-start.27 = (bf16[96,768]{0,1:T(8,128)(2,1)S(1)}, bf16[96,768]{0,1:T(8,128)(2,1)S(1)}, u32[]{:S(2)}, u32[]{:S(2)}) collective-permute-start(bf16[96,768]{0,1:T(8,128)(2,1)S(1)} %add_convert_fusion.11), channel_id=1, source_target_pairs={{0,16},{8,24},{16,0},{24,8},{1,17},{9,25},{17,1},{25,9},{2,18},{10... | collective-permute-start | bytes 442376 | tf_op jit(solution)/shard_map/ppermute | solution.py:159
  463.0 18.9 %collective-permute-start.22 = (bf16[96,768]{0,1:T(8,128)(2,1)S(1)}, bf16[96,768]{0,1:T(8,128)(2,1)S(1)}, u32[]{:S(2)}, u32[]{:S(2)}) collective-permute-start(bf16[96,768]{0,1:T(8,128)(2,1)S(1)} %add_convert_fusion.12), channel_id=1, source_target_pairs={{0,16},{8,24},{16,0},{24,8},{1,17},{9,25},{17,1},{25,9},{2,18},{10... | collective-permute-start | bytes 442376 | tf_op jit(solution)/shard_map/ppermute | solution.py:159
  464.4 23.3 %collective-permute-start.37 = (bf16[96,1536]{1,0:T(8,128)(2,1)S(1)}, bf16[96,1536]{1,0:T(8,128)(2,1)S(1)}, u32[]{:S(2)}, u32[]{:S(2)}) collective-permute-start(bf16[96,1536]{1,0:T(8,128)(2,1)S(1)} %broadcast_select_fusion.42), channel_id=1, source_target_pairs={{0,16},{8,24},{16,0},{24,8},{1,17},{9,25},{17,1},{25,9},{2,18},{10... | collective-permute-start | bytes 884744 | tf_op jit(solution)/shard_map/ppermute | solution.py:153
  477.8 24.4 %collective-permute-start.28 = (bf16[192,768]{0,1:T(8,128)(2,1)S(1)}, bf16[192,768]{0,1:T(8,128)(2,1)S(1)}, u32[]{:S(2)}, u32[]{:S(2)}) collective-permute-start(bf16[192,768]{0,1:T(8,128)(2,1)S(1)} %pad_maximum_fusion.24), channel_id=1, source_target_pairs={{0,8},{8,0},{16,24},{24,16},{1,9},{9,1},{17,25},{25,17},{2,10},{10... | collective-permute-start | bytes 884744 | tf_op jit(solution)/shard_map/ppermute | solution.py:159
  482.1 28.7 %collective-permute-start.23 = (bf16[192,768]{0,1:T(8,128)(2,1)S(1)}, bf16[192,768]{0,1:T(8,128)(2,1)S(1)}, u32[]{:S(2)}, u32[]{:S(2)}) collective-permute-start(bf16[192,768]{0,1:T(8,128)(2,1)S(1)} %pad_maximum_fusion.23), channel_id=1, source_target_pairs={{0,8},{8,0},{16,24},{24,16},{1,9},{9,1},{17,25},{25,17},{2,10},{10... | collective-permute-start | bytes 884744 | tf_op jit(solution)/shard_map/ppermute | solution.py:159
  487.8 23.4 %collective-permute-start.38 = (bf16[96,1536]{1,0:T(8,128)(2,1)S(1)}, bf16[96,1536]{1,0:T(8,128)(2,1)S(1)}, u32[]{:S(2)}, u32[]{:S(2)}) collective-permute-start(bf16[96,1536]{1,0:T(8,128)(2,1)S(1)} %add_convert_fusion.9), channel_id=1, source_target_pairs={{0,16},{8,24},{16,0},{24,8},{1,17},{9,25},{17,1},{25,9},{2,18},{10... | collective-permute-start | bytes 884744 | tf_op jit(solution)/shard_map/ppermute | solution.py:159
  502.5 13.0 %collective-permute-start.29 = (bf16[192,768]{0,1:T(8,128)(2,1)S(1)}, bf16[192,768]{0,1:T(8,128)(2,1)}, u32[]{:S(2)}, u32[]{:S(2)}) collective-permute-start(bf16[192,768]{0,1:T(8,128)(2,1)S(1)} %get-tuple-element.151), channel_id=1, source_target_pairs={{0,1},{1,0},{2,3},{3,2},{4,5},{5,4},{6,7},{7,6},{8,9},{9,8},{10,11... | collective-permute-start | bytes 884744 | tf_op jit(solution)/shard_map/ppermute | solution.py:103
  511.1 30.6 %collective-permute-start.24 = (bf16[192,768]{0,1:T(8,128)(2,1)S(1)}, bf16[192,768]{0,1:T(8,128)(2,1)}, u32[]{:S(2)}, u32[]{:S(2)}) collective-permute-start(bf16[192,768]{0,1:T(8,128)(2,1)S(1)} %get-tuple-element.148), channel_id=1, source_target_pairs={{0,1},{1,0},{2,3},{3,2},{4,5},{5,4},{6,7},{7,6},{8,9},{9,8},{10,11... | collective-permute-start | bytes 884744 | tf_op jit(solution)/shard_map/ppermute | solution.py:103
  512.1 61.9 %collective-permute-start.39 = (bf16[192,1536]{1,0:T(8,128)(2,1)}, bf16[192,1536]{1,0:T(8,128)(2,1)}, u32[]{:S(2)}, u32[]{:S(2)}) collective-permute-start(bf16[192,1536]{1,0:T(8,128)(2,1)} %pad_maximum_fusion.17), channel_id=1, source_target_pairs={{0,8},{8,0},{16,24},{24,16},{1,9},{9,1},{17,25},{25,17},{2,10},{10... | collective-permute-start | bytes 1769480 | tf_op jit(solution)/shard_map/ppermute | solution.py:159
  513.4 27.3 %collective-permute-start.31 = (bf16[192,1536]{1,0:T(8,128)(2,1)S(1)}, bf16[192,1536]{1,0:T(8,128)(2,1)S(1)}, u32[]{:S(2)}, u32[]{:S(2)}) collective-permute-start(bf16[192,1536]{1,0:T(8,128)(2,1)S(1)} %broadcast_select_fusion.9), channel_id=1, source_target_pairs={{0,8},{8,0},{16,24},{24,16},{1,9},{9,1},{17,25},{25,17},{2,10},{10... | collective-permute-start | bytes 1769480 | tf_op jit(solution)/shard_map/ppermute | solution.py:153
  515.5 25.2 %copy-start.18 = (bf16[1,384,1536]{2,1,0:T(8,128)(2,1)S(1)}, bf16[1,384,1536]{2,1,0:T(8,128)(2,1)}, u32[]{:S(2)}) copy-start(bf16[1,384,1536]{2,1,0:T(8,128)(2,1)} %reduce-scatter.19.cloned.1.call-done) | copy-start | bytes 3538948
  540.9 15.8 %collective-permute-start.32 = (bf16[96,1536]{1,0:T(8,128)(2,1)S(1)}, bf16[96,1536]{1,0:T(8,128)(2,1)S(1)}, u32[]{:S(2)}, u32[]{:S(2)}) collective-permute-start(bf16[96,1536]{1,0:T(8,128)(2,1)S(1)} %broadcast_select_fusion.45), channel_id=1, source_target_pairs={{0,16},{8,24},{16,0},{24,8},{1,17},{9,25},{17,1},{25,9},{2,18},{10... | collective-permute-start | bytes 884744 | tf_op jit(solution)/shard_map/ppermute | solution.py:153
  556.9 15.5 %collective-permute-start.33 = (bf16[96,1536]{1,0:T(8,128)(2,1)S(1)}, bf16[96,1536]{1,0:T(8,128)(2,1)S(1)}, u32[]{:S(2)}, u32[]{:S(2)}) collective-permute-start(bf16[96,1536]{1,0:T(8,128)(2,1)S(1)} %add_convert_fusion.10), channel_id=1, source_target_pairs={{0,16},{8,24},{16,0},{24,8},{1,17},{9,25},{17,1},{25,9},{2,18},{10... | collective-permute-start | bytes 884744 | tf_op jit(solution)/shard_map/ppermute | solution.py:159
  573.9 15.6 %collective-permute-start.34 = (bf16[192,1536]{1,0:T(8,128)(2,1)}, bf16[192,1536]{1,0:T(8,128)(2,1)}, u32[]{:S(2)}, u32[]{:S(2)}) collective-permute-start(bf16[192,1536]{1,0:T(8,128)(2,1)} %pad_maximum_fusion.16), channel_id=1, source_target_pairs={{0,8},{8,0},{16,24},{24,16},{1,9},{9,1},{17,25},{25,17},{2,10},{10... | collective-permute-start | bytes 1769480 | tf_op jit(solution)/shard_map/ppermute | solution.py:159
  576.6 14.3 %collective-permute-start.40 = (bf16[192,1536]{1,0:T(8,128)(2,1)}, bf16[192,1536]{1,0:T(8,128)(2,1)}, u32[]{:S(2)}, u32[]{:S(2)}) collective-permute-start(bf16[192,1536]{1,0:T(8,128)(2,1)} %get-tuple-element.145), channel_id=1, source_target_pairs={{0,1},{1,0},{2,3},{3,2},{4,5},{5,4},{6,7},{7,6},{8,9},{9,8},{10,11... | collective-permute-start | bytes 1769480 | tf_op jit(solution)/shard_map/ppermute | solution.py:103
  577.8 11.7 %copy-start.33 = (bf16[96,1536]{1,0:T(8,128)(2,1)S(1)}, bf16[96,1536]{1,0:T(8,128)(2,1)}, u32[]{:S(2)}) copy-start(bf16[96,1536]{1,0:T(8,128)(2,1)} %copy-done.32) | copy-start | bytes 884740
  590.9 2.1 collective-permute-start.35
  (166 other events, 465.1 us)
Sparse Core Ops, SparseCore 0:
  34.0 80.2 all-gather.6
  116.1 76.5 all-gather.8
  273.7 37.3 reduce-scatter.12
  314.0 61.2 reduce-scatter.14
  378.7 37.9 reduce-scatter.16
  419.5 58.1 reduce-scatter.18
